TPU v7x, 256 devices: a whole 4x4x8 slice. The times are simulated.
256 devices in a mesh: grp: 8 (over z), dev: 32 (over x, y, core).
Axes of the slice: x: 4, y: 4, z: 8, core: 2. Of those that a mesh axis runs over, the one named last changes fastest.
Arguments:
- rhs: float32 [2097152], P(('grp', 'dev')), may hold values from -6 to 6
- points: float32 [3, 2097152], P(None, ('grp', 'dev')), as said below
- leaf_basis: float32 [8192, 256, 64], P(('grp', 'dev')), may hold values from -0.375 to 0.375
- transfer: float32 [8192, 64, 64], P(('grp', 'dev')), may hold values from -0.75 to 0.75
- leaf_skel: float32 [3, 524288], P(None, ('grp', 'dev')), as said below
- node_skel: float32 [3, 16384], P(None, ('grp', 'dev')), as said below
- near_ids: int32 [8192, 8], P(('grp', 'dev')), may hold values from 0 to 8191, as said below
- near_count: int32 [8192], P(('grp', 'dev')), may hold values from 1 to 8, as said below
- far_leaf: int32 [8192, 16], P(('grp', 'dev')), may hold values from 0 to 8191, as said below
- far_node: int32 [256, 32], P(('grp', 'dev')), may hold values from 0 to 255
Outputs:
- solution: float32 [2097152], P(('grp', 'dev'))
- residual: float32 [2097152], P(('grp', 'dev'))
Inputs may be any that keep to these rules, and one draw needn't show every extreme that they name: Each leaf's points lie about a centre of their own; leaves in Morton order. `leaf_skel`: skeleton points lie about their leaf's centre. `node_skel`: skeleton points lie about the centre of their node's leaves. `near_ids`: slot 0 is the leaf itself; every entry is a leaf of the leaf's own device or of the devices just before and after it in Morton order. `near_count`: slots at or past the count are ignored. `far_leaf`: every entry is a leaf of the same grp index as the leaf.
All inputs are finite; a program needn't handle non-finite values.
Results may differ from a plain program's by a relative error of at most 0.0003.
Values sent between devices are 32-bit elements; how exact they have to be, the bound alone decides.
No kernel may reach another device: no remote copies, remote signals or barrier semaphores. Data moves between devices by JAX's collectives and lax.ppermute only.
A program may use at most 64 MiB of HBM per device.

v0:
```python
import math

import jax
import jax.numpy as jnp
from jax import lax
from jax.sharding import PartitionSpec as P

ITERS = 2


HIGH = lax.Precision.HIGHEST
amplitude = 0.00390625
length_scale = 0.25
nugget = 2.0


def padded(cells, sides, width):
    for axis, dim in sides:
        count = lax.axis_size(axis)
        ends = count - 1
        head = lax.slice_in_dim(cells, 0, width, axis=dim)
        tail = lax.slice_in_dim(cells, cells.shape[dim] - width, cells.shape[dim], axis=dim)
        cells = jnp.concatenate(
            [
                lax.ppermute(tail, axis, [(i, (i + 1) % count) for i in range(ends)]),
                cells,
                lax.ppermute(head, axis, [((i + 1) % count, i) for i in range(ends)]),
            ],
            axis=dim,
        )
    return cells


def matern(left, right):
    dist_sq = jnp.zeros(left.shape[1:-1] + (left.shape[-1], right.shape[-1]), jnp.float32)
    for comp in range(3):
        diff = left[comp][..., :, None] - right[comp][..., None, :]
        dist_sq = dist_sq + diff * diff
    scaled = jnp.sqrt(dist_sq) * (math.sqrt(5.0) / length_scale)
    return amplitude * (1.0 + scaled + scaled * scaled / 3.0) * jnp.exp(-scaled)


def on_device(
    rhs,
    points,
    leaf_basis,
    transfer,
    leaf_skel,
    node_skel,
    near_ids,
    near_count,
    far_leaf,
    far_node,
):
    leaf_dev, leaf_pts, rank = leaf_basis.shape
    slots = near_ids.shape[1]
    per_group = leaf_dev * lax.axis_size("dev")
    here = lax.axis_index("grp") * lax.axis_size("dev") + lax.axis_index("dev")
    first_leaf = here * leaf_dev
    group_first = lax.axis_index("grp") * per_group
    wide_pts = padded(points, ((("grp", "dev"), 1),), leaf_dev * leaf_pts)
    ext_pts = wide_pts.reshape(3, 3 * leaf_dev, leaf_pts)
    own_pts = points.reshape(3, leaf_dev, leaf_pts)
    near_local = near_ids - (first_leaf - leaf_dev)
    group_sk = lax.all_gather(leaf_skel, "dev", axis=1, tiled=True).reshape(3, per_group, rank)
    own_sk = leaf_skel.reshape(3, leaf_dev, rank)
    far_local = far_leaf - group_first
    leaf_kern = matern(own_sk[:, :, None, :], group_sk[:, far_local, :])
    all_nodes = lax.all_gather(node_skel, ("grp", "dev"), axis=1, tiled=True).reshape(3, -1, rank)
    partners = far_node[0]
    node_kern = matern(node_skel[:, None, :], all_nodes[:, partners, :])

    def squares(vector):
        return lax.psum(jnp.sum(vector * vector), ("grp", "dev"))

    solution = jnp.zeros_like(rhs)
    residual, direction = (rhs, rhs)
    norm_now = squares(residual)
    for step in range(ITERS):
        values = direction.reshape(leaf_dev, leaf_pts)
        weights = jnp.einsum("lpr,lp->lr", leaf_basis, values, precision=HIGH)
        upward = jnp.einsum("lrs,lr->s", transfer, weights, precision=HIGH)[None]
        every = lax.all_gather(upward, ("grp", "dev"), axis=0, tiled=True)
        downward = jnp.einsum("jrs,js->r", node_kern, every[partners], precision=HIGH)
        group_weights = lax.all_gather(weights, "dev", axis=0, tiled=True)
        local = jnp.einsum("ljrs,ljs->lr", leaf_kern, group_weights[far_local], precision=HIGH)
        local = local + jnp.einsum("lrs,s->lr", transfer, downward, precision=HIGH)
        wide_vals = padded(direction, ((("grp", "dev"), 0),), leaf_dev * leaf_pts)
        apply_ext_vals = wide_vals.reshape(3 * leaf_dev, leaf_pts)
        near_part = jnp.zeros((leaf_dev, leaf_pts), jnp.float32)
        for apply_slot in range(slots):
            column = near_local[:, apply_slot]
            block = matern(own_pts, ext_pts[:, column, :])
            part = jnp.einsum("lik,lk->li", block, apply_ext_vals[column], precision=HIGH)
            near_part = near_part + jnp.where((apply_slot < near_count)[:, None], part, 0.0)
        far_part = jnp.einsum("lpr,lr->lp", leaf_basis, local, precision=HIGH)
        image = (nugget * values + far_part + near_part).reshape(-1)
        alpha = norm_now / lax.psum(jnp.sum(direction * image), ("grp", "dev"))
        solution = solution + alpha * direction
        residual = residual - alpha * image
        norm_next = squares(residual)
        direction = residual + norm_next / norm_now * direction
        norm_now = norm_next
    return (solution, residual)


def solution(mesh):
    placed = (
        P(("grp", "dev")),
        P(None, ("grp", "dev")),
        P(("grp", "dev"), None, None),
        P(("grp", "dev"), None, None),
        P(None, ("grp", "dev")),
        P(None, ("grp", "dev")),
        P(("grp", "dev"), None),
        P(("grp", "dev")),
        P(("grp", "dev"), None),
        P(("grp", "dev"), None),
    )
    return jax.shard_map(
        on_device,
        mesh=mesh,
        in_specs=placed,
        out_specs=(P(("grp", "dev")), P(("grp", "dev"))),
        check_vma=False,
    )
```

profile of v0, /device:TPU:1, one launch (start us, length us, event | category | flops | bytes accessed | tf_op | source)
XLA Modules:
  0.0 1052.5 jit_solution(8575479291784962119)
XLA Ops:
  7.3 4.9 collective-permute-start
  24.8 31.5 %all_gather.18 = f32[3,65536]{1,0:T(4,128)} all-gather(f32[3,2048]{1,0:T(4,128)S(1)} %copy-done.15), channel_id=1, replica_groups=mesh['grp'=8,'dev'=32] {'dev'}, dimensions={1}, use_global_device_ids=true | all-gather | bytes 811008 | tf_op jit(solution)/shard_map/all_gather | solution.py:65
  57.2 3.2 reshape.128
  60.3 3.8 copy.20
  64.1 4.0 gather_fusion
  68.2 3.7 fusion.143
  71.8 24.7 %all_gather.19 = f32[1024,64]{1,0:T(8,128)} all-gather(f32[32,64]{1,0:T(8,128)S(1)} %bitcast.361), channel_id=1, replica_groups=mesh['grp'=8,'dev'=32] {'dev'}, dimensions={0}, use_global_device_ids=true | all-gather | bytes 270336 | tf_op jit(solution)/shard_map/all_gather | solution.py:85
  101.9 74.4 %all-gather.2 = f32[256,64,3]{1,2,0:T(4,128)S(1)} all-gather(f32[1,64,3]{1,2,0:T(4,128)S(1)} %bitcast.442), channel_id=1, replica_groups=mesh['grp'=8,'dev'=32] {'grp','dev'}, dimensions={0}, use_global_device_ids=true | all-gather | bytes 197376 | tf_op jit(solution)/shard_map/all_gather | solution.py:69
  184.0 30.1 %fusion.1 = f32[32,1,64,1]{2,1,3,0:T(1,128)S(1)} fusion(f32[32,16,64,1]{2,3,1,0:T(1,128)} %bitcast.353, f32[32,16,64]{2,1,0:T(8,128)} %bitcast.359, f32[32,64]{1,0:T(8,128)} %sub.242, f32[32,16,64]{2,1,0:T(8,128)} %bitcast.357, f32[32,64]{1,0:T(8,128)} %sub.237, f32[32,16,64]{2,1,0:T(8,128)} %bitcast.355, f32[32,64]{1,0:T(8,128)} %sub.230), kind=kOutput, calls=%fused_computation.40 | convolution fusion | flops 58720256 | bytes 557056 | tf_op jit(solution)/shard_map/ljrs,ljs->lr/dot_general | solution.py:86
  216.0 55.2 %all-reduce.6.cloned.1.call-done = f32[16384]{0:T(1024)} async-done(((f32[16384]{0:T(1024)}), f32[16384]{0:T(1024)}) %all-reduce.6.cloned.1.call-update) | async-done | bytes 65552
  309.9 15.3 %fusion.3 = f32[32,1,256]{2,1,0:T(1,128)S(1)} fusion(f32[32,256]{1,0:T(8,128)S(1)} %bitcast.384, f32[32,256]{1,0:T(8,128)S(1)} %copy-done.28, f32[32,256]{1,0:T(8,128)S(1)} %bitcast.386, f32[32,256]{1,0:T(8,128)S(1)} %copy-done.26, f32[32,256]{1,0:T(8,128)S(1)} %bitcast.388, f32[32,256]{1,0:T(8,128)S(1)} %copy-done.24, f32[32,256,1]{1,0,2:T(8,128)S(1)} %bitcast.374), kind=kOutput, calls=%fused_computation.42 | convolution fusion | flops 58720256 | bytes 262144 | tf_op jit(solution)/shard_map/lik,lk->li/dot_general | solution.py:94
  325.3 15.3 %fusion.5 = f32[32,1,256]{2,1,0:T(1,128)S(1)} fusion(f32[32,256]{1,0:T(8,128)S(1)} %bitcast.390, f32[32,256]{1,0:T(8,128)S(1)} %bitcast.392, f32[32,256]{1,0:T(8,128)S(1)} %bitcast.394, f32[32,256]{1,0:T(8,128)S(1)} %copy-done.28, f32[32,256]{1,0:T(8,128)S(1)} %copy-done.26, f32[32,256]{1,0:T(8,128)S(1)} %copy-done.24, f32[32,256,1]{1,0,2:T(8,128)S(1)} %bitcast.375), kind=kOutput, calls=%fused_computation.44 | convolution fusion | flops 58720256 | bytes 262144 | tf_op jit(solution)/shard_map/lik,lk->li/dot_general | solution.py:94
  340.6 15.3 %fusion.7 = f32[32,1,256]{2,1,0:T(1,128)S(1)} fusion(f32[32,256]{1,0:T(8,128)S(1)} %bitcast.396, f32[32,256]{1,0:T(8,128)S(1)} %bitcast.398, f32[32,256]{1,0:T(8,128)S(1)} %bitcast.400, f32[32,256]{1,0:T(8,128)S(1)} %copy-done.28, f32[32,256]{1,0:T(8,128)S(1)} %copy-done.26, f32[32,256]{1,0:T(8,128)S(1)} %copy-done.24, f32[32,256,1]{1,0,2:T(8,128)S(1)} %bitcast.372), kind=kOutput, calls=%fused_computation.46 | convolution fusion | flops 58720256 | bytes 262144 | tf_op jit(solution)/shard_map/lik,lk->li/dot_general | solution.py:94
  356.0 15.5 %fusion.9 = f32[32,1,256]{2,1,0:T(1,128)S(1)} fusion(f32[32,256]{1,0:T(8,128)S(1)} %bitcast.402, f32[32,256]{1,0:T(8,128)S(1)} %bitcast.404, f32[32,256]{1,0:T(8,128)S(1)} %bitcast.406, f32[32,256]{1,0:T(8,128)S(1)} %copy-done.28, f32[32,256]{1,0:T(8,128)S(1)} %copy-done.26, f32[32,256]{1,0:T(8,128)S(1)} %copy-done.24, f32[32,256,1]{1,0,2:T(8,128)S(1)} %bitcast.373), kind=kOutput, calls=%fused_computation.48 | convolution fusion | flops 58720256 | bytes 262144 | tf_op jit(solution)/shard_map/lik,lk->li/dot_general | solution.py:94
  371.6 15.3 %fusion.11 = f32[32,1,256]{2,1,0:T(1,128)S(1)} fusion(f32[32,256]{1,0:T(8,128)S(1)} %bitcast.408, f32[32,256]{1,0:T(8,128)S(1)} %bitcast.410, f32[32,256]{1,0:T(8,128)S(1)} %bitcast.412, f32[32,256]{1,0:T(8,128)S(1)} %copy-done.28, f32[32,256]{1,0:T(8,128)S(1)} %copy-done.26, f32[32,256]{1,0:T(8,128)S(1)} %copy-done.24, f32[32,256,1]{1,0,2:T(8,128)S(1)} %bitcast.370), kind=kOutput, calls=%fused_computation.50 | convolution fusion | flops 58720256 | bytes 262144 | tf_op jit(solution)/shard_map/lik,lk->li/dot_general | solution.py:94
  386.9 15.3 %fusion.13 = f32[32,1,256]{2,1,0:T(1,128)S(1)} fusion(f32[32,256]{1,0:T(8,128)S(1)} %bitcast.414, f32[32,256]{1,0:T(8,128)S(1)} %bitcast.416, f32[32,256]{1,0:T(8,128)S(1)} %bitcast.418, f32[32,256]{1,0:T(8,128)S(1)} %copy-done.28, f32[32,256]{1,0:T(8,128)S(1)} %copy-done.26, f32[32,256]{1,0:T(8,128)S(1)} %copy-done.24, f32[32,256,1]{1,0,2:T(8,128)S(1)} %bitcast.371), kind=kOutput, calls=%fused_computation.52 | convolution fusion | flops 58720256 | bytes 262144 | tf_op jit(solution)/shard_map/lik,lk->li/dot_general | solution.py:94
  402.3 15.3 %fusion.15 = f32[32,1,256]{2,1,0:T(1,128)S(1)} fusion(f32[32,256]{1,0:T(8,128)S(1)} %bitcast.420, f32[32,256]{1,0:T(8,128)S(1)} %bitcast.422, f32[32,256]{1,0:T(8,128)S(1)} %bitcast.424, f32[32,256]{1,0:T(8,128)S(1)} %copy-done.28, f32[32,256]{1,0:T(8,128)S(1)} %copy-done.26, f32[32,256]{1,0:T(8,128)S(1)} %copy-done.24, f32[32,256,1]{1,0,2:T(8,128)S(1)} %bitcast.368), kind=kOutput, calls=%fused_computation.54 | convolution fusion | flops 58720256 | bytes 262144 | tf_op jit(solution)/shard_map/lik,lk->li/dot_general | solution.py:94
  417.8 15.3 %fusion.17 = f32[32,1,256]{2,1,0:T(1,128)S(1)} fusion(f32[32,256]{1,0:T(8,128)S(1)} %bitcast.426, f32[32,256]{1,0:T(8,128)S(1)} %bitcast.428, f32[32,256]{1,0:T(8,128)S(1)} %bitcast.430, f32[32,256]{1,0:T(8,128)S(1)} %copy-done.28, f32[32,256]{1,0:T(8,128)S(1)} %copy-done.26, f32[32,256]{1,0:T(8,128)S(1)} %copy-done.24, f32[32,256,1]{1,0,2:T(8,128)S(1)} %bitcast.369), kind=kOutput, calls=%fused_computation.56 | convolution fusion | flops 58720256 | bytes 262144 | tf_op jit(solution)/shard_map/lik,lk->li/dot_general | solution.py:94
  434.0 74.4 %all-reduce.2 = (f32[]{:T(128)}, f32[]{:T(128)}) all-reduce(f32[]{:T(128)} %get-tuple-element.6, f32[]{:T(128)} %get-tuple-element.5), channel_id=1, replica_groups=mesh['grp'=8,'dev'=32] {'grp','dev'}, use_global_device_ids=true, to_apply=%region_1.0 | all-reduce | flops 2 | bytes 16 | tf_op jit(solution)/shard_map/psum | solution.py:74
  510.4 73.4 %psum.30 = f32[]{:T(128)} all-reduce(f32[]{:T(128)} %multiply_reduce_fusion.1), channel_id=1, replica_groups=mesh['grp'=8,'dev'=32] {'grp','dev'}, use_global_device_ids=true, to_apply=%region_5.6 | all-reduce | flops 1 | bytes 8 | tf_op jit(solution)/shard_map/psum | solution.py:74
  593.3 29.3 %all_gather.22 = f32[1024,64]{1,0:T(8,128)} all-gather(f32[32,64]{1,0:T(8,128)S(1)} %bitcast.362), channel_id=1, replica_groups=mesh['grp'=8,'dev'=32] {'dev'}, dimensions={0}, use_global_device_ids=true | all-gather | bytes 270336 | tf_op jit(solution)/shard_map/all_gather | solution.py:85
  625.6 29.7 %fusion = f32[32,1,64,1]{2,1,3,0:T(1,128)S(1)} fusion(f32[32,16,64,1]{2,3,1,0:T(1,128)} %bitcast.354, f32[32,16,64]{2,1,0:T(8,128)} %bitcast.360, f32[32,64]{1,0:T(8,128)S(1)} %copy-done.80, f32[32,16,64]{2,1,0:T(8,128)} %bitcast.358, f32[32,64]{1,0:T(8,128)S(1)} %copy-done.79, f32[32,16,64]{2,1,0:T(8,128)} %bitcast.356, f32[32,64]{1,0:T(8,128)S(1)} %copy-done.78), kind=kOutput, calls=%fused_computation.39 | convolution fusion | flops 58720256 | bytes 557056 | tf_op jit(solution)/shard_map/ljrs,ljs->lr/dot_general | solution.py:86
  655.3 175.6 %all-reduce.8.cloned.1.call-done = f32[16384]{0:T(1024)} async-done(((f32[16384]{0:T(1024)}), f32[16384]{0:T(1024)}) %all-reduce.8.cloned.1.call-update) | async-done | bytes 65552
  844.8 15.5 %fusion.2 = f32[32,1,256]{2,1,0:T(1,128)S(1)} fusion(f32[32,256]{1,0:T(8,128)S(1)} %bitcast.385, f32[32,256]{1,0:T(8,128)S(1)} %copy-done.29, f32[32,256]{1,0:T(8,128)S(1)} %bitcast.387, f32[32,256]{1,0:T(8,128)S(1)} %copy-done.27, f32[32,256]{1,0:T(8,128)S(1)} %bitcast.389, f32[32,256]{1,0:T(8,128)S(1)} %copy-done.25, f32[32,256,1]{1,0,2:T(8,128)S(1)} %bitcast.383), kind=kOutput, calls=%fused_computation.41 | convolution fusion | flops 58720256 | bytes 262144 | tf_op jit(solution)/shard_map/lik,lk->li/dot_general | solution.py:94
  860.4 15.3 %fusion.4 = f32[32,1,256]{2,1,0:T(1,128)S(1)} fusion(f32[32,256]{1,0:T(8,128)S(1)} %bitcast.391, f32[32,256]{1,0:T(8,128)S(1)} %bitcast.393, f32[32,256]{1,0:T(8,128)S(1)} %bitcast.395, f32[32,256]{1,0:T(8,128)S(1)} %copy-done.29, f32[32,256]{1,0:T(8,128)S(1)} %copy-done.27, f32[32,256]{1,0:T(8,128)S(1)} %copy-done.25, f32[32,256,1]{1,0,2:T(8,128)S(1)} %bitcast.382), kind=kOutput, calls=%fused_computation.43 | convolution fusion | flops 58720256 | bytes 262144 | tf_op jit(solution)/shard_map/lik,lk->li/dot_general | solution.py:94
  875.8 15.3 %fusion.6 = f32[32,1,256]{2,1,0:T(1,128)S(1)} fusion(f32[32,256]{1,0:T(8,128)S(1)} %bitcast.397, f32[32,256]{1,0:T(8,128)S(1)} %bitcast.399, f32[32,256]{1,0:T(8,128)S(1)} %bitcast.401, f32[32,256]{1,0:T(8,128)S(1)} %copy-done.29, f32[32,256]{1,0:T(8,128)S(1)} %copy-done.27, f32[32,256]{1,0:T(8,128)S(1)} %copy-done.25, f32[32,256,1]{1,0,2:T(8,128)S(1)} %bitcast.381), kind=kOutput, calls=%fused_computation.45 | convolution fusion | flops 58720256 | bytes 262144 | tf_op jit(solution)/shard_map/lik,lk->li/dot_general | solution.py:94
  891.2 15.3 %fusion.8 = f32[32,1,256]{2,1,0:T(1,128)S(1)} fusion(f32[32,256]{1,0:T(8,128)S(1)} %bitcast.403, f32[32,256]{1,0:T(8,128)S(1)} %bitcast.405, f32[32,256]{1,0:T(8,128)S(1)} %bitcast.407, f32[32,256]{1,0:T(8,128)S(1)} %copy-done.29, f32[32,256]{1,0:T(8,128)S(1)} %copy-done.27, f32[32,256]{1,0:T(8,128)S(1)} %copy-done.25, f32[32,256,1]{1,0,2:T(8,128)S(1)} %bitcast.380), kind=kOutput, calls=%fused_computation.47 | convolution fusion | flops 58720256 | bytes 262144 | tf_op jit(solution)/shard_map/lik,lk->li/dot_general | solution.py:94
  906.5 15.3 %fusion.10 = f32[32,1,256]{2,1,0:T(1,128)S(1)} fusion(f32[32,256]{1,0:T(8,128)S(1)} %bitcast.409, f32[32,256]{1,0:T(8,128)S(1)} %bitcast.411, f32[32,256]{1,0:T(8,128)S(1)} %bitcast.413, f32[32,256]{1,0:T(8,128)S(1)} %copy-done.29, f32[32,256]{1,0:T(8,128)S(1)} %copy-done.27, f32[32,256]{1,0:T(8,128)S(1)} %copy-done.25, f32[32,256,1]{1,0,2:T(8,128)S(1)} %bitcast.379), kind=kOutput, calls=%fused_computation.49 | convolution fusion | flops 58720256 | bytes 262144 | tf_op jit(solution)/shard_map/lik,lk->li/dot_general | solution.py:94
  921.9 15.3 %fusion.12 = f32[32,1,256]{2,1,0:T(1,128)S(1)} fusion(f32[32,256]{1,0:T(8,128)S(1)} %bitcast.415, f32[32,256]{1,0:T(8,128)S(1)} %bitcast.417, f32[32,256]{1,0:T(8,128)S(1)} %bitcast.419, f32[32,256]{1,0:T(8,128)S(1)} %copy-done.29, f32[32,256]{1,0:T(8,128)S(1)} %copy-done.27, f32[32,256]{1,0:T(8,128)S(1)} %copy-done.25, f32[32,256,1]{1,0,2:T(8,128)S(1)} %bitcast.378), kind=kOutput, calls=%fused_computation.51 | convolution fusion | flops 58720256 | bytes 262144 | tf_op jit(solution)/shard_map/lik,lk->li/dot_general | solution.py:94
  937.3 15.3 %fusion.14 = f32[32,1,256]{2,1,0:T(1,128)S(1)} fusion(f32[32,256]{1,0:T(8,128)S(1)} %bitcast.421, f32[32,256]{1,0:T(8,128)S(1)} %bitcast.423, f32[32,256]{1,0:T(8,128)S(1)} %bitcast.425, f32[32,256]{1,0:T(8,128)S(1)} %copy-done.29, f32[32,256]{1,0:T(8,128)S(1)} %copy-done.27, f32[32,256]{1,0:T(8,128)S(1)} %copy-done.25, f32[32,256,1]{1,0,2:T(8,128)S(1)} %bitcast.377), kind=kOutput, calls=%fused_computation.53 | convolution fusion | flops 58720256 | bytes 262144 | tf_op jit(solution)/shard_map/lik,lk->li/dot_general | solution.py:94
  952.7 15.5 %fusion.16 = f32[32,1,256]{2,1,0:T(1,128)S(1)} fusion(f32[32,256]{1,0:T(8,128)S(1)} %bitcast.427, f32[32,256]{1,0:T(8,128)S(1)} %bitcast.429, f32[32,256]{1,0:T(8,128)S(1)} %bitcast.431, f32[32,256]{1,0:T(8,128)S(1)} %copy-done.29, f32[32,256]{1,0:T(8,128)S(1)} %copy-done.27, f32[32,256]{1,0:T(8,128)S(1)} %copy-done.25, f32[32,256,1]{1,0,2:T(8,128)S(1)} %bitcast.376), kind=kOutput, calls=%fused_computation.55 | convolution fusion | flops 58720256 | bytes 262144 | tf_op jit(solution)/shard_map/lik,lk->li/dot_general | solution.py:94
  969.1 74.4 %psum.31 = f32[]{:T(128)} all-reduce(f32[]{:T(128)} %multiply_reduce_fusion), channel_id=1, replica_groups=mesh['grp'=8,'dev'=32] {'grp','dev'}, use_global_device_ids=true, to_apply=%region_7.8 | all-reduce | flops 1 | bytes 8 | tf_op jit(solution)/shard_map/psum | solution.py:98
  (387 shorter events, 94.2 us)
Async XLA Ops:
  7.2 264.0 %all-reduce.6.cloned.1.call-start = ((), (), s32[]{:S(2)}) async-start(), calls=%async_computation | async-start | bytes 131072
  7.3 283.0 %collective-permute-start = (f32[3,8192]{1,0:T(4,128)}, f32[3,8192]{1,0:T(4,128)}, u32[]{:S(2)}, u32[]{:S(2)}) collective-permute-start(f32[3,8192]{1,0:T(4,128)} %param.11), channel_id=1, source_target_pairs={{0,1},{1,2},{2,3},{3,4},{4,5},{5,6},{6,7},{7,8},{8,9},{9,10},{10,1... | collective-permute-start | bytes 294920 | tf_op jit(solution)/shard_map/ppermute | solution.py:25
  12.1 278.1 %collective-permute-start.1 = (f32[3,8192]{1,0:T(4,128)}, f32[3,8192]{1,0:T(4,128)}, u32[]{:S(2)}, u32[]{:S(2)}) collective-permute-start(f32[3,8192]{1,0:T(4,128)} %param.11), channel_id=1, source_target_pairs={{1,0},{2,1},{3,2},{4,3},{5,4},{6,5},{7,6},{8,7},{9,8},{10,9},{11,1... | collective-permute-start | bytes 294920 | tf_op jit(solution)/shard_map/ppermute | solution.py:27
  14.6 264.4 %collective-permute-start.2 = (f32[8192]{0:T(1024)}, f32[8192]{0:T(1024)}, u32[]{:S(2)}, u32[]{:S(2)}) collective-permute-start(f32[8192]{0:T(1024)} %param.10), channel_id=1, source_target_pairs={{0,1},{1,2},{2,3},{3,4},{4,5},{5,6},{6,7},{7,8},{8,9},{9,10},{10,1... | collective-permute-start | bytes 98312 | tf_op jit(solution)/shard_map/ppermute | solution.py:25
  17.7 262.1 %collective-permute-start.3 = (f32[8192]{0:T(1024)}, f32[8192]{0:T(1024)}, u32[]{:S(2)}, u32[]{:S(2)}) collective-permute-start(f32[8192]{0:T(1024)} %param.10), channel_id=1, source_target_pairs={{1,0},{2,1},{3,2},{4,3},{5,4},{6,5},{7,6},{8,7},{9,8},{10,9},{11,1... | collective-permute-start | bytes 98312 | tf_op jit(solution)/shard_map/ppermute | solution.py:27
  23.9 807.1 %all-reduce.8.cloned.1.call-start = ((), (), s32[]{:S(2)}) async-start(), calls=%async_computation.1 | async-start | bytes 131072
  99.3 82.0 %copy-start.117 = (s32[32]{0:T(128)S(1)}, s32[32]{0:T(128)}, u32[]{:S(2)}) copy-start(s32[32]{0:T(128)} %param.17) | copy-start | bytes 388
  101.3 80.6 %copy-start.94 = (s32[1024]{0:T(1024)}, s32[1024]{0:T(1024)S(1)}, u32[]{:S(2)}) copy-start(s32[1024]{0:T(1024)S(1)} %pad_clamp_fusion.8) | copy-start | bytes 12292
  181.2 91.6 %copy-start.81 = (f32[1,32,64]{2,0,1:T(1,128)}, f32[1,32,64]{2,0,1:T(1,128)S(1)}, u32[]{:S(2)}) copy-start(f32[1,32,64]{2,0,1:T(1,128)S(1)} %get-tuple-element.39) | copy-start | bytes 24580
  181.2 91.6 %copy-start.83 = (f32[1,32,64]{2,0,1:T(1,128)}, f32[1,32,64]{2,0,1:T(1,128)S(1)}, u32[]{:S(2)}) copy-start(f32[1,32,64]{2,0,1:T(1,128)S(1)} %get-tuple-element.40) | copy-start | bytes 24580
  181.2 91.6 %copy-start.85 = (f32[1,32,64]{2,0,1:T(1,128)}, f32[1,32,64]{2,0,1:T(1,128)S(1)}, u32[]{:S(2)}) copy-start(f32[1,32,64]{2,0,1:T(1,128)S(1)} %get-tuple-element.41) | copy-start | bytes 24580
  182.5 108.8 %copy-start.89 = (s32[1024]{0:T(1024)}, s32[1024]{0:T(1024)S(1)}, u32[]{:S(2)}) copy-start(s32[1024]{0:T(1024)S(1)} %get-tuple-element.70) | copy-start | bytes 12292
  182.5 110.1 %copy-start.88 = (s32[1024]{0:T(1024)}, s32[1024]{0:T(1024)S(1)}, u32[]{:S(2)}) copy-start(s32[1024]{0:T(1024)S(1)} %get-tuple-element.69) | copy-start | bytes 12292
  183.2 99.8 %copy-start.91 = (s32[1024]{0:T(1024)}, s32[1024]{0:T(1024)S(1)}, u32[]{:S(2)}) copy-start(s32[1024]{0:T(1024)S(1)} %get-tuple-element.68) | copy-start | bytes 12292
  183.2 112.1 %copy-start.90 = (s32[1024]{0:T(1024)}, s32[1024]{0:T(1024)S(1)}, u32[]{:S(2)}) copy-start(s32[1024]{0:T(1024)S(1)} %get-tuple-element.67) | copy-start | bytes 12292
  183.9 101.6 %copy-start.93 = (s32[1024]{0:T(1024)}, s32[1024]{0:T(1024)S(1)}, u32[]{:S(2)}) copy-start(s32[1024]{0:T(1024)S(1)} %get-tuple-element.66) | copy-start | bytes 12292
  183.9 102.8 %copy-start.92 = (s32[1024]{0:T(1024)}, s32[1024]{0:T(1024)S(1)}, u32[]{:S(2)}) copy-start(s32[1024]{0:T(1024)S(1)} %get-tuple-element.65) | copy-start | bytes 12292
  183.9 89.0 %copy-start.118 = (f32[64]{0:T(128)S(1)}, f32[64]{0:T(128)}, u32[]{:S(2)}) copy-start(f32[64]{0:T(128)} %get-tuple-element.52) | copy-start | bytes 772
  183.9 89.0 %copy-start.119 = (f32[64]{0:T(128)S(1)}, f32[64]{0:T(128)}, u32[]{:S(2)}) copy-start(f32[64]{0:T(128)} %get-tuple-element.53) | copy-start | bytes 772
  183.9 89.0 %copy-start.120 = (f32[64]{0:T(128)S(1)}, f32[64]{0:T(128)}, u32[]{:S(2)}) copy-start(f32[64]{0:T(128)} %get-tuple-element.54) | copy-start | bytes 772
  309.4 77.4 %copy-start.60 = (f32[1,32,256]{2,1,0:T(8,128)}, f32[1,32,256]{2,1,0:T(8,128)S(1)}, u32[]{:S(2)}) copy-start(f32[1,32,256]{2,1,0:T(8,128)S(1)} %copy.179) | copy-start | bytes 98308
  309.6 92.7 %copy-start.66 = (f32[1,32,256]{2,1,0:T(8,128)}, f32[1,32,256]{2,1,0:T(8,128)S(1)}, u32[]{:S(2)}) copy-start(f32[1,32,256]{2,1,0:T(8,128)S(1)} %copy.176) | copy-start | bytes 98308
  309.6 92.6 %copy-start.68 = (f32[1,32,256]{2,1,0:T(8,128)}, f32[1,32,256]{2,1,0:T(8,128)S(1)}, u32[]{:S(2)}) copy-start(f32[1,32,256]{2,1,0:T(8,128)S(1)} %copy.177) | copy-start | bytes 98308
  309.6 92.6 %copy-start.70 = (f32[1,32,256]{2,1,0:T(8,128)}, f32[1,32,256]{2,1,0:T(8,128)S(1)}, u32[]{:S(2)}) copy-start(f32[1,32,256]{2,1,0:T(8,128)S(1)} %copy.178) | copy-start | bytes 98308
  309.8 107.9 %copy-start.72 = (f32[1,32,256]{2,1,0:T(8,128)}, f32[1,32,256]{2,1,0:T(8,128)S(1)}, u32[]{:S(2)}) copy-start(f32[1,32,256]{2,1,0:T(8,128)S(1)} %copy.173) | copy-start | bytes 98308
  309.8 107.9 %copy-start.74 = (f32[1,32,256]{2,1,0:T(8,128)}, f32[1,32,256]{2,1,0:T(8,128)S(1)}, u32[]{:S(2)}) copy-start(f32[1,32,256]{2,1,0:T(8,128)S(1)} %copy.174) | copy-start | bytes 98308
  309.8 107.8 %copy-start.76 = (f32[1,32,256]{2,1,0:T(8,128)}, f32[1,32,256]{2,1,0:T(8,128)S(1)}, u32[]{:S(2)}) copy-start(f32[1,32,256]{2,1,0:T(8,128)S(1)} %copy.175) | copy-start | bytes 98308
  585.2 253.7 %collective-permute-start.4 = (f32[8192]{0:T(1024)S(1)}, f32[8192]{0:T(1024)S(1)}, u32[]{:S(2)}, u32[]{:S(2)}) collective-permute-start(f32[8192]{0:T(1024)S(1)} %multiply_add_fusion.1), channel_id=1, source_target_pairs={{0,1},{1,2},{2,3},{3,4},{4,5},{5,6},{6,7},{7,8},{8,9},{9,10},{10,1... | collective-permute-start | bytes 98312 | tf_op jit(solution)/shard_map/ppermute | solution.py:25
  587.9 251.0 %collective-permute-start.5 = (f32[8192]{0:T(1024)S(1)}, f32[8192]{0:T(1024)S(1)}, u32[]{:S(2)}, u32[]{:S(2)}) collective-permute-start(f32[8192]{0:T(1024)S(1)} %multiply_add_fusion.1), channel_id=1, source_target_pairs={{1,0},{2,1},{3,2},{4,3},{5,4},{6,5},{7,6},{8,7},{9,8},{10,9},{11,1... | collective-permute-start | bytes 98312 | tf_op jit(solution)/shard_map/ppermute | solution.py:27
  625.6 207.0 %copy-start.82 = (f32[1,32,64]{2,0,1:T(1,128)S(1)}, f32[1,32,64]{2,0,1:T(1,128)}, u32[]{:S(2)}) copy-start(f32[1,32,64]{2,0,1:T(1,128)} %copy-done.81) | copy-start | bytes 24580
  625.6 207.0 %copy-start.84 = (f32[1,32,64]{2,0,1:T(1,128)S(1)}, f32[1,32,64]{2,0,1:T(1,128)}, u32[]{:S(2)}) copy-start(f32[1,32,64]{2,0,1:T(1,128)} %copy-done.83) | copy-start | bytes 24580
  625.6 207.0 %copy-start.86 = (f32[1,32,64]{2,0,1:T(1,128)S(1)}, f32[1,32,64]{2,0,1:T(1,128)}, u32[]{:S(2)}) copy-start(f32[1,32,64]{2,0,1:T(1,128)} %copy-done.85) | copy-start | bytes 24580
  (98 other events, 2240.0 us)
Sparse Core Ops, SparseCore 0:
  24.0 247.1 all-reduce.5
  593.4 237.5 all-reduce.7
where the time goes:
time: 1060 us; the launch traced here: 1050 us
  blocking collectives  382 us (36%)
  matrix products  323 us (30%)
  waiting for transfers between devices  231 us (22%)
  local copies, waits for them, and re-layouts  71.5 us (7%)
  between operations  20.3 us (2%)
  starting transfers between devices  17.1 us (2%)
    dot_general x16, matrix products, on_device(): jnp.einsum('lik,lk->li', block, apply_ext_vals[column], precision=HIGH)  246 us
    unnamed x4, waiting for transfers between devices  231 us
    psum x2, blocking collectives, squares(): return lax.psum(jnp.sum(vector * vector), ('grp', 'dev'))  148 us
    all_gather x1, blocking collectives, on_device(): lax.all_gather(node_skel, ('grp', 'dev'), axis=1, tiled=True)  74.4 us
    psum x1, blocking collectives, on_device(): alpha = norm_now / lax.psum(jnp.sum(direction * image), ('grp', 'dev'))  74.4 us
    dot_general x2, matrix products, on_device(): jnp.einsum('ljrs,ljs->lr', leaf_kern, group_weights[far_local], precision...  59.8 us
    all_gather x2, blocking collectives, on_device(): group_weights = lax.all_gather(weights, 'dev', axis=0, tiled=True)  54 us
    all_gather x1, blocking collectives, on_device(): lax.all_gather(leaf_skel, 'dev', axis=1, tiled=True)  31.5 us
  transfers between devices with their start and end apart: 8, of which 2 were waited for; matrix products, arithmetic and copies ran while one was open for 12% of the time, Pallas kernels for 0%

commit v1 on v0

v1 whole, which is shorter than its diff:
```python
import functools
import math

import jax
import jax.numpy as jnp
from jax import lax
from jax.experimental import pallas as pl
from jax.experimental.pallas import tpu as pltpu
from jax.sharding import PartitionSpec as P

AXES = ("grp", "dev")
F32 = jnp.float32
BF16 = jnp.bfloat16
LN2 = math.log(2.0)
AMPLITUDE = 0.00390625
LENGTH = 0.25
NUGGET = 2.0
SCALE = math.sqrt(5.0) / LENGTH / LN2
SHIFT = 1.5 / LN2
OFFSET = 0.75 / (LN2 * LN2)
FACTOR = AMPLITUDE * LN2 * LN2 / 3.0
SMEM = pl.BlockSpec(memory_space=pltpu.SMEM)
LEAVES, PTS, RANK = 32, 256, 64
DEPTH = 48
DUMMY = 96
STEP = 4
LIST = 272


def params():
    return pltpu.CompilerParams(vmem_limit_bytes=58 * 1024 * 1024)


def split(x):
    hi = x.astype(BF16).astype(F32)
    rest = x - hi
    mid = rest.astype(BF16).astype(F32)
    return hi, mid, rest - mid


def rows_of(shape):
    return lax.broadcasted_iota(jnp.int32, shape, 0)


def lanes_of(shape):
    return lax.broadcasted_iota(jnp.int32, shape, 1)


def source_stack(coords):
    row = rows_of(coords.shape)
    norm = jnp.sum(coords * coords, axis=0, keepdims=True)
    full = jnp.where(row < 3, coords, jnp.where(row == 3, norm, jnp.where(row == 4, 1.0, 0.0)))
    hi, mid, low = split(full)
    return jnp.concatenate([hi, hi, mid, mid, hi, low], axis=0).astype(BF16)


def target_stack(coords):
    row = rows_of(coords.shape)
    norm = jnp.sum(coords * coords, axis=0, keepdims=True)
    full = jnp.where(row < 3, -2.0 * coords, jnp.where(row == 3, 1.0, jnp.where(row == 4, norm, 0.0)))
    hi, mid, low = split(full)
    stack = jnp.concatenate([hi, mid, hi, mid, low, hi, jnp.zeros((128 - DEPTH,) + hi.shape[1:], F32)], axis=0)
    return stack.T.astype(BF16)


def weighted(dist_sq, weights):
    dist_sq = jnp.maximum(dist_sq, 1e-30)
    dist = dist_sq * lax.rsqrt(dist_sq)
    moved = dist + SHIFT
    value = (moved * moved + OFFSET) * jnp.exp2(-dist) * weights
    total = value[:, :128]
    for at in range(128, value.shape[1], 128):
        total = total + value[:, at : at + 128]
    return total


def centred(tile, centre):
    shape = tile.shape
    return jnp.where(rows_of(shape) < 3, (tile - centre) * SCALE, 0.0)


def eight(tile):
    return jnp.concatenate([tile, jnp.zeros((8 - tile.shape[0], tile.shape[1]), F32)], axis=0)


def row_of(ref, l):
    pair = ref[pl.ds(2 * l, 2), :]
    return jnp.concatenate([pair[:1], pair[1:]], axis=1)


def pair_of(row):
    return jnp.concatenate([row[:, :128], row[:, 128:]], axis=0)


def project(carry, l, row, basis_ref, transfer_ref):
    weights, node = carry
    column = jnp.sum(basis_ref[l] * row, axis=1, keepdims=True)
    return jnp.where(lanes_of(weights.shape) == l, column, weights), node + transfer_ref[l] * column


def project_start():
    return jnp.zeros((RANK, 128), F32), jnp.zeros((RANK, RANK), F32)


def project_end(carry):
    rows = carry[0].T
    return jnp.concatenate([rows[:16], rows[16:32]], axis=1), jnp.sum(carry[1], axis=0, keepdims=True)


def prepare_kernel(rhs_ref, points_ref, basis_ref, transfer_ref, leaf_skel_ref, node_skel_ref, near_ref, pay_ref):
    near_ref[:3, :] = points_ref[...]
    for half in range(2 * LEAVES):
        near_ref[3:4, half * 128 : (half + 1) * 128] = rhs_ref[half : half + 1, :]
    weights, node = project_end(
        lax.fori_loop(
            0, LEAVES, lambda l, c: project(c, l, row_of(rhs_ref, l), basis_ref, transfer_ref), project_start(), unroll=8
        )
    )
    skel = leaf_skel_ref[...]
    tiles = []
    for m in range(16):
        low = skel[:, m * RANK : (m + 1) * RANK]
        high = skel[:, (m + 16) * RANK : (m + 17) * RANK]
        tiles.append(jnp.concatenate([low, high], axis=1))
        tiles.append(weights[m : m + 1])
    own = node_skel_ref[...]
    tiles.append(jnp.concatenate([own[:1], own[1:2]], axis=1))
    tiles.append(jnp.concatenate([own[2:3], node], axis=1))
    tiles.append(jnp.zeros((6, 128), F32))
    payload = jnp.concatenate(tiles, axis=0)
    for d in range(32):
        pay_ref[d] = payload


def near_pairs(list_ref, target_ref, centre_ref, source_ref, acc_ref, dist_ref):
    def distances(code, slot):
        l = lax.shift_right_logical(code, 8)
        centre = centre_ref[l]
        coords = centred(source_ref[code & 255], jnp.concatenate([centre, centre], axis=1))
        dist_ref[slot] = jnp.dot(target_ref[l, :, :DEPTH], source_stack(coords), preferred_element_type=F32)

    def products(code, slot):
        l = lax.shift_right_logical(code, 8)
        weights = source_ref[code & 255, 3:4, :] * FACTOR
        for at in range(0, PTS, 64):
            acc_ref[l, at : at + 64, :] += weighted(dist_ref[slot, at : at + 64, :], weights)

    def step(i, carry):
        codes = [list_ref[STEP * i + k + 1] for k in range(STEP + 1)]
        for k in range(STEP):
            distances(codes[k + 1], (k + 1) % 2)
            products(codes[k], k % 2)
        return carry

    distances(list_ref[1], 0)
    lax.fori_loop(0, (list_ref[0] + STEP - 1) // STEP, step, 0)


def clear(acc_ref):
    def leaf(l, carry):
        acc_ref[l] = jnp.zeros((PTS, 128), F32)
        return carry

    lax.fori_loop(0, LEAVES, leaf, 0, unroll=2)


def near_rows(acc_ref, out_ref, add_ref):
    def leaf(l, carry):
        parts = [jnp.sum(acc_ref[l, h * 128 : (h + 1) * 128, :].T, axis=0, keepdims=True) for h in range(2)]
        value = jnp.concatenate(parts, axis=0)
        if add_ref is not None:
            value = value + add_ref[pl.ds(2 * l, 2), :]
        out_ref[pl.ds(2 * l, 2), :] = value
        return carry

    lax.fori_loop(0, LEAVES, leaf, 0, unroll=4)


def fill(source_ref, at, block_ref):
    for l in range(LEAVES):
        source_ref[at + l] = eight(block_ref[:, l * PTS : (l + 1) * PTS])
    source_ref[DUMMY] = jnp.zeros((8, PTS), F32)


def set_values(source_ref, at, block_ref):
    for l in range(LEAVES):
        pair = block_ref[2 * l : 2 * l + 2, :]
        source_ref[at + l, 3:4, :] = jnp.concatenate([pair[:1], pair[1:]], axis=1)


def skel_target(tile):
    wide = jnp.concatenate([eight(tile), jnp.zeros((8, 64), F32)], axis=1)
    centre = jnp.broadcast_to(jnp.sum(wide, axis=1, keepdims=True) * (1.0 / RANK), wide.shape)
    return centre, target_stack(centred(wide, centre))[:RANK]


def own_first_kernel(
    ids_ref, count_ref, pay_ref, skel_ref, target_ref, centre_ref, far_target_ref, far_centre_ref, own_list_ref, other_list_ref, out_ref,
    source_ref, acc_ref, dist_ref,
):
    here = lax.shift_right_logical(ids_ref[0, 0], 5)
    base = (here - 1) * LEAVES

    def leaf_slots(l, counts):
        def slot(j, counts):
            own, other = counts
            n = ids_ref[j, l]
            code = l * 256 + (n - base)
            is_own = (lax.shift_right_logical(n, 5) == here).astype(jnp.int32)
            own_list_ref[own] = code
            other_list_ref[other] = code
            return own + is_own, other + 1 - is_own

        return lax.fori_loop(0, jnp.minimum(count_ref[l], 8), slot, counts)

    own, other = lax.fori_loop(0, LEAVES, leaf_slots, (jnp.int32(1), jnp.int32(1)))
    for k in range(STEP + 1):
        own_list_ref[own + k] = DUMMY
        other_list_ref[other + k] = DUMMY
    own_list_ref[0] = own - 1
    other_list_ref[0] = other - 1
    fill(source_ref, LEAVES, pay_ref)
    clear(acc_ref)

    def targets(l, carry):
        tile = source_ref[LEAVES + l]
        centre = jnp.broadcast_to(jnp.sum(tile, axis=1, keepdims=True) * (1.0 / PTS), (8, 128))
        centre_ref[l] = centre
        target_ref[l] = target_stack(centred(tile, jnp.concatenate([centre, centre], axis=1)))
        return carry

    lax.fori_loop(0, LEAVES, targets, 0, unroll=4)
    near_pairs(own_list_ref, target_ref, centre_ref, source_ref, acc_ref, dist_ref)
    near_rows(acc_ref, out_ref, None)
    for l in range(LEAVES):
        far_centre_ref[l], far_target_ref[l] = skel_target(skel_ref[:, l * RANK : (l + 1) * RANK])


def own_next_kernel(own_list_ref, pay_ref, field_ref, target_ref, centre_ref, out_ref, source_ref, acc_ref, dist_ref):
    fill(source_ref, LEAVES, pay_ref)
    set_values(source_ref, LEAVES, field_ref)
    clear(acc_ref)
    near_pairs(own_list_ref, target_ref, centre_ref, source_ref, acc_ref, dist_ref)
    near_rows(acc_ref, out_ref, None)


def node_first_kernel(in_ref, out_ref):
    block = jnp.concatenate([in_ref[:, 0, :], in_ref[:, 1, :]], axis=0)
    for g in range(8):
        out_ref[g] = block


def node_next_kernel(in_ref, out_ref):
    for g in range(8):
        out_ref[g] = in_ref[:, 0, :]


def swap(tile):
    return pltpu.roll(tile, 64, 1)


def far_partners(far_leaf_ref, l, rows_at):
    low_lanes = lanes_of((1, 128)) < 64
    for j in range(8):
        tiles = []
        for k in range(2):
            p = far_leaf_ref[2 * j + k, l] & 1023
            tile = rows_at(lax.shift_right_logical(p, 5), p & 15)
            here = (lax.shift_right_logical(p, 4) & 1) == k
            tiles.append(jnp.where(here, tile, swap(tile)))
        yield jnp.where(low_lanes, tiles[0], tiles[1])


def far_sums(stack_ref, weight_ref, target_ref, out_ref, dist_ref):
    def distances(l, slot):
        for c in range(4):
            dist_ref[slot, c * RANK : (c + 1) * RANK, :] = jnp.dot(
                target_ref[l, :, :DEPTH], stack_ref[l, :, c * 256 : (c + 1) * 256], preferred_element_type=F32
            )

    def products(l, slot):
        total = jnp.zeros((RANK, 128), F32)
        for c in range(4):
            weights = weight_ref[l, :1, c * 256 : (c + 1) * 256]
            total = total + weighted(dist_ref[slot, c * RANK : (c + 1) * RANK, :], weights)
        out_ref[l] = total

    def step(i, carry):
        for k in range(STEP):
            distances(jnp.minimum(STEP * i + k + 1, LEAVES - 1), (k + 1) % 2)
            products(STEP * i + k, k % 2)
        return carry

    distances(0, 0)
    lax.fori_loop(0, LEAVES // STEP, step, 0)


def middle_first_kernel(
    other_list_ref, far_leaf_ref, prev_ref, next_ref, target_ref, centre_ref, own_ref, far_target_ref, far_centre_ref, group_ref,
    near_ref, far_ref, stack_ref, source_ref, acc_ref, dist_ref, weight_ref,
):
    def gather(l, carry):
        centre = far_centre_ref[l]
        rows = far_partners(far_leaf_ref, l, lambda d, m: group_ref[d, pl.ds(4 * m, 4), :])
        for j, tile in enumerate(rows):
            at = j * 128
            weight_ref[l, :1, at : at + 128] = tile[3:4] * FACTOR
            stack_ref[l, :, at : at + 128] = source_stack(centred(eight(tile), centre))
        return carry

    lax.fori_loop(0, LEAVES, gather, 0, unroll=2)
    far_sums(stack_ref, weight_ref, far_target_ref, far_ref, dist_ref)
    fill(source_ref, 0, prev_ref)
    fill(source_ref, 2 * LEAVES, next_ref)
    clear(acc_ref)
    near_pairs(other_list_ref, target_ref, centre_ref, source_ref, acc_ref, dist_ref)
    near_rows(acc_ref, near_ref, own_ref)


def middle_next_kernel(
    other_list_ref, far_leaf_ref, prev_ref, next_ref, prev_val_ref, next_val_ref, target_ref, centre_ref, own_ref, far_target_ref,
    stack_ref, group_ref, near_ref, far_ref, source_ref, acc_ref, dist_ref, weight_ref,
):
    def gather(l, carry):
        rows = far_partners(far_leaf_ref, l, lambda d, m: group_ref[d, pl.ds(m, 1), :])
        for j, tile in enumerate(rows):
            weight_ref[l, :1, j * 128 : (j + 1) * 128] = tile * FACTOR
        return carry

    lax.fori_loop(0, LEAVES, gather, 0, unroll=2)
    far_sums(stack_ref, weight_ref, far_target_ref, far_ref, dist_ref)
    fill(source_ref, 0, prev_ref)
    fill(source_ref, 2 * LEAVES, next_ref)
    set_values(source_ref, 0, prev_val_ref)
    set_values(source_ref, 2 * LEAVES, next_val_ref)
    clear(acc_ref)
    near_pairs(other_list_ref, target_ref, centre_ref, source_ref, acc_ref, dist_ref)
    near_rows(acc_ref, near_ref, own_ref)


def node_down(far_node_ref, node_skel_ref, nodes_ref, weight_ref):
    low_lanes = lanes_of((1, 128)) < 64
    own = node_skel_ref[...]
    centre, target = skel_target(jnp.concatenate([own[:1], own[2:3], own[1:2]], axis=0))
    total = jnp.zeros((RANK, 128), F32)
    for at in range(0, 32, 4):
        coords, weights = [], []
        for j in (at, at + 2):
            tiles = []
            for p in (far_node_ref[0, j], far_node_ref[0, j + 1]):
                g, d = lax.shift_right_logical(p, 5), p & 31
                rows = [nodes_ref[g, pl.ds(d, 1), :], nodes_ref[g, pl.ds(d + 32, 1), :]]
                if weight_ref is not None:
                    rows.append(weight_ref[g, pl.ds(d, 1), :])
                tiles.append(jnp.concatenate(rows, axis=0))
            even = jnp.where(low_lanes, tiles[0], swap(tiles[1]))
            odd = jnp.where(low_lanes, swap(tiles[0]), tiles[1])
            coords.append(eight(jnp.concatenate([even[:2], odd[:2]], axis=0)))
            weights.append(odd[1:2] if weight_ref is None else even[2:3])
        wide = jnp.concatenate([centre, centre], axis=1)
        sources = source_stack(centred(jnp.concatenate(coords, axis=1), wide))
        dist_sq = jnp.dot(target[:, :DEPTH], sources, preferred_element_type=F32)
        total = total + weighted(dist_sq, jnp.concatenate(weights, axis=1) * FACTOR)
    return jnp.sum(total.T, axis=0, keepdims=True)


def leaf_row(l, down, far_ref, near_ref, basis_ref, transfer_ref):
    moved = transfer_ref[l] * down
    total = far_ref[l] + jnp.concatenate([moved, jnp.zeros((RANK, 64), F32)], axis=1)
    column = jnp.sum(total, axis=1, keepdims=True)
    return row_of(near_ref, l) + jnp.sum(basis_ref[l] * column, axis=0, keepdims=True)


def scalars(values):
    lane = lanes_of((1, 128))
    out = jnp.zeros((1, 128), F32)
    for at, value in enumerate(values):
        out = jnp.where(lane == 64 + at, value, out)
    return out


def dot(a, b):
    return jnp.sum(jnp.sum(a * b, axis=0, keepdims=True), axis=1, keepdims=True)


def finish_first_kernel(
    far_node_ref, node_skel_ref, nodes_ref, near_ref, far_ref, rhs_ref, basis_ref, transfer_ref, out_ref, pay_ref
):
    down = node_down(far_node_ref, node_skel_ref, nodes_ref, None)

    def leaf(l, carry):
        row = leaf_row(l, down, far_ref, near_ref, basis_ref, transfer_ref)
        out_ref[pl.ds(2 * l, 2), :] = pair_of(row)
        return project(carry, l, row, basis_ref, transfer_ref)

    weights, node = project_end(lax.fori_loop(0, LEAVES, leaf, project_start(), unroll=8))
    rhs, image = rhs_ref[...], out_ref[...]
    extra = scalars([dot(rhs, rhs), dot(rhs, image)])
    last = jnp.where(lanes_of((1, 128)) < 64, jnp.concatenate([node, node], axis=1), extra)
    payload = jnp.concatenate([weights, last, jnp.zeros((7, 128), F32)], axis=0)
    for d in range(32):
        pay_ref[d] = payload


def lane(row, at):
    return jnp.sum(jnp.where(lanes_of(row.shape) == at, row, 0.0), axis=1, keepdims=True)


def first_scalars(node_ref):
    total = jnp.sum(jnp.sum(node_ref[...], axis=0), axis=0, keepdims=True)
    norm, inner = lane(total, 64), lane(total, 65)
    energy = NUGGET * norm + inner
    return norm, inner, energy, norm / energy


def finish_next_kernel(
    far_node_ref, node_skel_ref, nodes_ref, node_in_ref, near_ref, far_ref, rhs_ref, field_ref, basis_ref, transfer_ref, out_ref, pay_ref
):
    down = node_down(far_node_ref, node_skel_ref, nodes_ref, node_in_ref)

    def leaf(l, carry):
        out_ref[pl.ds(2 * l, 2), :] = pair_of(leaf_row(l, down, far_ref, near_ref, basis_ref, transfer_ref))
        return carry

    lax.fori_loop(0, LEAVES, leaf, 0, unroll=8)
    _, inner, energy, alpha = first_scalars(node_in_ref)
    rhs, field, field2 = rhs_ref[...], field_ref[...], out_ref[...]
    keep = inner / energy
    residual = keep * rhs - alpha * field
    image = NUGGET * residual + keep * field - alpha * field2
    base = NUGGET * rhs + field
    block = scalars([dot(residual, residual), dot(residual, image), dot(residual, base) + dot(rhs, image)])
    pay_ref[...] = jnp.broadcast_to(block[None], pay_ref.shape)


def last_kernel(rhs_ref, field_ref, field2_ref, node_ref, last_ref, solution_ref, residual_ref):
    norm, inner, energy, alpha = first_scalars(node_ref)
    total = jnp.sum(last_ref[...], axis=0)
    norm2 = lane(total, 64)
    beta = norm2 / norm
    alpha2 = norm2 / (lane(total, 65) + beta * lane(total, 66) + beta * beta * energy)
    rhs, field, field2 = rhs_ref[...], field_ref[...], field2_ref[...]
    keep = inner / energy
    residual = keep * rhs - alpha * field
    image = NUGGET * residual + keep * field - alpha * field2
    direction = residual + beta * rhs
    solution_ref[...] = alpha * rhs + alpha2 * direction
    residual_ref[...] = residual - alpha2 * (image + beta * (NUGGET * rhs + field))


def whole(shape):
    return pl.BlockSpec(shape, lambda i: (0,) * len(shape))


def call(kernel, name, outs, ins, scratch=(), work=0):
    def spec(shape, dtype):
        return SMEM if dtype == jnp.int32 else whole(shape)

    return pl.pallas_call(
        kernel,
        grid=(1,),
        out_shape=[jax.ShapeDtypeStruct(shape, dtype) for shape, dtype in outs],
        in_specs=[spec(array.shape, array.dtype) for array in ins],
        out_specs=[spec(shape, dtype) for shape, dtype in outs],
        scratch_shapes=list(scratch),
        compiler_params=params(),
        cost_estimate=pl.CostEstimate(flops=work * 1_000_000_000, bytes_accessed=1_000_000, transcendentals=0),
        name=name,
    )(*ins)


def neighbours(block):
    count = lax.axis_size("grp") * lax.axis_size("dev")
    up = [(i, i + 1) for i in range(count - 1)]
    down = [(i + 1, i) for i in range(count - 1)]
    return lax.ppermute(block, AXES, up), lax.ppermute(block, AXES, down)


def exchange(copies, axes):
    return lax.all_to_all(copies, axes, 0, 0, tiled=True)


def on_device(rhs, points, leaf_basis, transfer, leaf_skel, node_skel, near_ids, near_count, far_leaf, far_node):
    rhs = rhs.reshape(2 * LEAVES, 128)
    basis = jnp.swapaxes(leaf_basis, 1, 2)
    far_leaf = far_leaf.T
    I32 = jnp.int32
    vector = ((2 * LEAVES, 128), F32)
    distances = pltpu.VMEM((2, PTS, 256), F32)
    near_scratch = [pltpu.VMEM((DUMMY + 1, 8, PTS), F32), pltpu.VMEM((LEAVES, PTS, 128), F32), distances]
    far_scratch = [pltpu.VMEM((LEAVES, 8, 1024), F32)]
    near_pay, pay = call(
        prepare_kernel,
        "prepare",
        [((4, LEAVES * PTS), F32), ((32, 72, 128), F32)],
        [rhs, points, basis, transfer, leaf_skel, node_skel],
        work=4,
    )
    prev_pay, next_pay = neighbours(near_pay)
    group = exchange(pay, "dev")
    targets, centres, far_targets, far_centres, own_list, other_list, own_part = call(
        own_first_kernel,
        "own_first",
        [
            ((LEAVES, PTS, 128), BF16),
            ((LEAVES, 8, 128), F32),
            ((LEAVES, RANK, 128), BF16),
            ((LEAVES, 8, 128), F32),
            ((LIST,), I32),
            ((LIST,), I32),
            vector,
        ],
        [near_ids.T, near_count, near_pay, leaf_skel],
        near_scratch,
        work=15,
    )
    (node_pay,) = call(node_first_kernel, "node_first", [((8, 64, 128), F32)], [group[:, 64:72]], work=1)
    nodes = exchange(node_pay, "grp")
    near_part, far_part, stacks = call(
        middle_first_kernel,
        "middle_first",
        [vector, ((LEAVES, RANK, 128), F32), ((LEAVES, DEPTH, 1024), BF16)],
        [other_list, far_leaf, prev_pay, next_pay, targets, centres, own_part, far_targets, far_centres, group],
        near_scratch + far_scratch,
        work=20,
    )
    field, pay = call(
        finish_first_kernel,
        "finish_first",
        [vector, ((32, 24, 128), F32)],
        [far_node, node_skel, nodes, near_part, far_part, rhs, basis, transfer],
        work=4,
    )
    prev_val, next_val = neighbours(field)
    leaf_in = exchange(pay, "dev")
    (own_part,) = call(
        own_next_kernel, "own_next", [vector], [own_list, near_pay, field, targets, centres], near_scratch, work=10
    )
    (node_pay,) = call(node_next_kernel, "node_next", [((8, 32, 128), F32)], [leaf_in[:, 16:24]], work=1)
    node_in = exchange(node_pay, "grp")
    near_part, far_part = call(
        middle_next_kernel,
        "middle_next",
        [vector, ((LEAVES, RANK, 128), F32)],
        [
            other_list, far_leaf, prev_pay, next_pay, prev_val, next_val, targets, centres, own_part, far_targets, stacks, leaf_in,
        ],
        near_scratch + far_scratch,
        work=20,
    )
    field2, pay = call(
        finish_next_kernel,
        "finish_next",
        [vector, ((256, 1, 128), F32)],
        [far_node, node_skel, nodes, node_in, near_part, far_part, rhs, field, basis, transfer],
        work=4,
    )
    last = exchange(pay, AXES)
    answer, residual = call(last_kernel, "last", [vector, vector], [rhs, field, field2, node_in, last], work=1)
    return answer.reshape(-1), residual.reshape(-1)


def solution(mesh):
    placed = (
        P(AXES),
        P(None, AXES),
        P(AXES, None, None),
        P(AXES, None, None),
        P(None, AXES),
        P(None, AXES),
        P(AXES, None),
        P(AXES),
        P(AXES, None),
        P(AXES, None),
    )
    return jax.shard_map(on_device, mesh=mesh, in_specs=placed, out_specs=(P(AXES), P(AXES)), check_vma=False)
```

time: 1060 us -> 173 us (0.16)
  blocking collectives: 382 us -> 32.1 us
  matrix products: 323 us -> 0 us
  waiting for transfers between devices: 231 us -> 4.03 us
  Pallas kernels: 0 us -> 79 us
  local copies, waits for them, and re-layouts: 71.5 us -> 4.1 us
  starting transfers between devices: 17.1 us -> 50.2 us
  between operations: 20.3 us -> 0.77 us
    dot_general x28 -> x0, matrix products: 323 us -> none  [the longest x16 246 us: on_device(): jnp.einsum('lik,lk->li', block, apply_ext_vals[column], precision=HIGH)]
    unnamed x4 -> x0, waiting for transfers between devices: 231 us -> none
    psum x3 -> x0, blocking collectives: 222 us -> none  [the longest x2 148 us: squares(): return lax.psum(jnp.sum(vector * vector), ('grp', 'dev'))]
    all_gather x4 -> x0, blocking collectives: 160 us -> none  [the longest x1 74.4 us: on_device(): lax.all_gather(node_skel, ('grp', 'dev'), axis=1, tiled=True)]
    pallas_call x0 -> x10, Pallas kernels: none -> 79 us  [call(): pl.pallas_call(kernel, grid=(1,), out_shape=[jax.ShapeDtypeStruct(shape,...]
    all_to_all x0 -> x4, starting transfers between devices: none -> 39.4 us  [exchange(): return lax.all_to_all(copies, axes, 0, 0, tiled=True)]
    gather x30 -> x0, local copies, waits for them, and re-layouts: 38.9 us -> none  [the longest x16 15.4 us: on_device(): apply_ext_vals[column]]
    all_to_all x0 -> x1, blocking collectives: none -> 32.1 us  [exchange(): return lax.all_to_all(copies, axes, 0, 0, tiled=True)]
  transfers between devices with their start and end apart: 8 -> 8, of which waited for: 2 -> 1; matrix products, arithmetic and copies ran while one was open for 12% -> 1% of each run, Pallas kernels for 0% -> 37%
where the time goes in v1:
time: 173 us; the launch traced here: 170 us
  Pallas kernels  79 us (46%)
  starting transfers between devices  50.2 us (29%)
  blocking collectives  32.1 us (19%)
  local copies, waits for them, and re-layouts  4.1 us (2%)
  waiting for transfers between devices  4.03 us (2%)
    pallas_call x10, Pallas kernels, call(): pl.pallas_call(kernel, grid=(1,), out_shape=[jax.ShapeDtypeStruct(shape,...  79 us
    all_to_all x4, starting transfers between devices, exchange(): return lax.all_to_all(copies, axes, 0, 0, tiled=True)  39.4 us
    all_to_all x1, blocking collectives, exchange(): return lax.all_to_all(copies, axes, 0, 0, tiled=True)  32.1 us
    ppermute x4, starting transfers between devices, neighbours(): return (lax.ppermute(block, AXES, up), lax.ppermute(block, AXES, down))  10.8 us
    all_to_all x4, waiting for transfers between devices, exchange(): return lax.all_to_all(copies, axes, 0, 0, tiled=True)  4.02 us
  transfers between devices with their start and end apart: 8, of which 1 were waited for; matrix products, arithmetic and copies ran while one was open for 1% of the time, Pallas kernels for 37%

profile of v1, /device:TPU:1, one launch (start us, length us, event | category | flops | bytes accessed | tf_op | source)
XLA Modules:
  0.0 170.3 jit_solution(12305837477463262366)
XLA Ops:
  0.6 3.9 %prepare.1 = (f32[4,8192]{1,0:T(4,128)}, f32[32,72,128]{2,1,0:T(8,128)}) custom-call(f32[64,128]{1,0:T(8,128)} %bitcast.9, f32[3,8192]{1,0:T(4,128)} %points_ref.1, f32[32,64,256]{2,1,0:T(8,128)} %bitcast.6, f32[32,64,64]{2,1,0:T(8,128)} %transfer_ref.5, f32[3,2048]{1,0:T(4,128)} %skel_ref.1, f32[3,64]{1,0:T(4,128)} %node_skel_ref.5), custom_call_target="tpu_custom_call" | custom-call | flops 4000000000 | bytes 1000000 | tf_op jit(solution)/shard_map/prepare/pallas_call | solution.py:459
  4.5 4.6 %collective-permute-start = (f32[4,8192]{1,0:T(4,128)}, f32[4,8192]{1,0:T(4,128)S(1)}, u32[]{:S(2)}, u32[]{:S(2)}) collective-permute-start(f32[4,8192]{1,0:T(4,128)} %get-tuple-element.23.pay_ref), channel_id=1, source_target_pairs={{0,1},{1,2},{2,3},{3,4},{4,5},{5,6},{6,7},{7,8},{8,9},{9,10},{10,1... | collective-permute-start | bytes 393224 | tf_op jit(solution)/shard_map/ppermute | solution.py:476
  9.1 1.9 %collective-permute-start.1 = (f32[4,8192]{1,0:T(4,128)}, f32[4,8192]{1,0:T(4,128)S(1)}, u32[]{:S(2)}, u32[]{:S(2)}) collective-permute-start(f32[4,8192]{1,0:T(4,128)} %get-tuple-element.23.pay_ref), channel_id=1, source_target_pairs={{1,0},{2,1},{3,2},{4,3},{5,4},{6,5},{7,6},{8,7},{9,8},{10,9},{11,1... | collective-permute-start | bytes 393224 | tf_op jit(solution)/shard_map/ppermute | solution.py:476
  11.1 7.6 %all-to-all-start = ((f32[32,72,128]{2,1,0:T(8,128)}), f32[32,72,128]{2,1,0:T(8,128)S(1)}, u32[]{:S(2)}, u32[]{:S(2)}) async-start(f32[32,72,128]{2,1,0:T(8,128)} %get-tuple-element.22), calls=%async_computation | async-start | bytes 2359296 | tf_op jit(solution)/shard_map/all_to_all | solution.py:480
  18.7 14.3 %own_first.1 = (bf16[32,256,128]{2,1,0:T(8,128)(2,1)}, f32[32,8,128]{2,1,0:T(8,128)}, bf16[32,64,128]{2,1,0:T(8,128)(2,1)}, f32[32,8,128]{2,1,0:T(8,128)}, s32[2...) custom-call(s32[8,32]{1,0:T(8,128)} %bitcast.15, s32[32]{0:T(128)} %count_ref.1, f32[4,8192]{1,0:T(4,128)} %get-tuple-element.23.pay_ref, ...), custom_call_target="tpu_custom_call" | custom-call | flops 15000000512 | bytes 1000000 | tf_op jit(solution)/shard_map/own_first/pallas_call | solution.py:459
  33.1 4.0 %all-to-all-done.group_ref = f32[32,72,128]{2,1,0:T(8,128)S(1)} async-done(((f32[32,72,128]{2,1,0:T(8,128)}), f32[32,72,128]{2,1,0:T(8,128)S(1)}, u32[]{:S(2)}, u32[]{:S(2)}) %all-to-all-start) | async-done | bytes 1179680 | tf_op jit(solution)/shard_map/all_to_all | solution.py:480
  37.1 0.7 slice.8.in_ref
  37.8 1.7 node_first.1
  39.5 10.2 %all-to-all-start.1 = ((f32[8,64,128]{2,1,0:T(8,128)}), f32[8,64,128]{2,1,0:T(8,128)S(1)}, u32[]{:S(2)}, u32[]{:S(2)}) async-start(f32[8,64,128]{2,1,0:T(8,128)} %node_first.1), calls=%async_computation.1 | async-start | bytes 524288 | tf_op jit(solution)/shard_map/all_to_all | solution.py:480
  49.7 0.0 collective-permute-done.1.next_ref
  49.7 0.6 copy-done.4
  50.3 0.1 copy-done.5
  50.4 18.0 %middle_first.1 = (f32[64,128]{1,0:T(8,128)}, f32[32,64,128]{2,1,0:T(8,128)}, bf16[32,48,1024]{2,1,0:T(8,128)(2,1)}) custom-call(s32[272]{0:T(512)} %get-tuple-element.24.other_list_ref, s32[16,32]{1,0:T(8,128)} %bitcast.13, f32[4,8192]{1,0:T(4,128)} %copy-done.4, f32[4,8192]{1,0:T(4,128)} %copy-done.5, bf16[32,256,128]{2,1,0:T(8,128)(2,1)} %get-tuple-element.25.target_ref, ...), custom_call_target="tpu_custom_call" | custom-call | flops 20000000000 | bytes 1000000 | tf_op jit(solution)/shard_map/middle_first/pallas_call | solution.py:459
  68.4 0.7 copy-done.2
  69.1 4.9 %finish_first.1 = (f32[64,128]{1,0:T(8,128)}, f32[32,24,128]{2,1,0:T(8,128)}) custom-call(s32[1,32]{1,0:T(1,128)} %far_node_ref.3, f32[3,64]{1,0:T(4,128)} %node_skel_ref.5, f32[8,64,128]{2,1,0:T(8,128)} %copy-done.2, f32[64,128]{1,0:T(8,128)} %get-tuple-element.30.near_ref, f32[32,64,128]{2,1,0:T(8,128)} %get-tuple-element.31.far_ref, f32[64,128]{1,0:T(8,128)} %bitcast.10, ...), custom_call_target="tpu_custom_call" | custom-call | flops 4000000000 | bytes 1000000 | tf_op jit(solution)/shard_map/finish_first/pallas_call | solution.py:459
  74.0 1.9 %collective-permute-start.2 = (f32[64,128]{1,0:T(8,128)}, f32[64,128]{1,0:T(8,128)S(1)}, u32[]{:S(2)}, u32[]{:S(2)}) collective-permute-start(f32[64,128]{1,0:T(8,128)} %get-tuple-element.32.field_ref), channel_id=1, source_target_pairs={{0,1},{1,2},{2,3},{3,4},{4,5},{5,6},{6,7},{7,8},{8,9},{9,10},{10,1... | collective-permute-start | bytes 98312 | tf_op jit(solution)/shard_map/ppermute | solution.py:476
  76.0 2.4 %collective-permute-start.3 = (f32[64,128]{1,0:T(8,128)}, f32[64,128]{1,0:T(8,128)S(1)}, u32[]{:S(2)}, u32[]{:S(2)}) collective-permute-start(f32[64,128]{1,0:T(8,128)} %get-tuple-element.32.field_ref), channel_id=1, source_target_pairs={{1,0},{2,1},{3,2},{4,3},{5,4},{6,5},{7,6},{8,7},{9,8},{10,9},{11,1... | collective-permute-start | bytes 98312 | tf_op jit(solution)/shard_map/ppermute | solution.py:476
  78.4 13.8 %all-to-all-start.2 = ((f32[32,24,128]{2,1,0:T(8,128)}), f32[32,24,128]{2,1,0:T(8,128)S(1)}, u32[]{:S(2)}, u32[]{:S(2)}) async-start(f32[32,24,128]{2,1,0:T(8,128)} %get-tuple-element.33), calls=%async_computation.2 | async-start | bytes 786432 | tf_op jit(solution)/shard_map/all_to_all | solution.py:480
  92.2 10.9 %own_next.1.own_ref = f32[64,128]{1,0:T(8,128)} custom-call(s32[272]{0:T(512)} %get-tuple-element.34.own_list_ref, f32[4,8192]{1,0:T(4,128)} %get-tuple-element.23.pay_ref, f32[64,128]{1,0:T(8,128)} %get-tuple-element.32.field_ref, bf16[32,256,128]{2,1,0:T(8,128)(2,1)} %get-tuple-element.25.target_ref, f32[32,8,128]{2,1,0:T(8,128)} %get-tuple-element.26.centre_ref), custom_call_target="tpu_custom_call" | custom-call | flops 10000000000 | bytes 1000000 | tf_op jit(solution)/shard_map/own_next/pallas_call | solution.py:459
  103.1 0.0 all-to-all-done.2.group_ref
  103.1 0.7 slice.9.in_ref
  103.8 1.6 node_next.1
  105.4 7.8 %all-to-all-start.3 = ((f32[8,32,128]{2,1,0:T(8,128)}), f32[8,32,128]{2,1,0:T(8,128)S(1)}, u32[]{:S(2)}, u32[]{:S(2)}) async-start(f32[8,32,128]{2,1,0:T(8,128)} %node_next.1), calls=%async_computation.3 | async-start | bytes 262144 | tf_op jit(solution)/shard_map/all_to_all | solution.py:480
  113.2 0.0 copy-start.6
  113.2 0.0 copy-start.7
  113.2 0.6 copy-done.6
  113.8 0.0 copy-done.7
  113.8 17.1 %middle_next.1 = (f32[64,128]{1,0:T(8,128)}, f32[32,64,128]{2,1,0:T(8,128)}) custom-call(s32[272]{0:T(512)} %get-tuple-element.24.other_list_ref, s32[16,32]{1,0:T(8,128)} %bitcast.14, f32[4,8192]{1,0:T(4,128)} %copy-done.4, f32[4,8192]{1,0:T(4,128)} %copy-done.5, f32[64,128]{1,0:T(8,128)} %copy-done.6, f32[64,128]{1,0:T(8,128)} %copy-done.7, ...), custom_call_target="tpu_custom_call" | custom-call | flops 20000000000 | bytes 1000000 | tf_op jit(solution)/shard_map/middle_next/pallas_call | solution.py:459
  130.9 0.6 copy-done.3
  131.6 4.6 %finish_next.1 = (f32[64,128]{1,0:T(8,128)}, f32[256,1,128]{2,1,0:T(1,128)}) custom-call(s32[1,32]{1,0:T(1,128)} %far_node_ref.3, f32[3,64]{1,0:T(4,128)} %node_skel_ref.5, f32[8,64,128]{2,1,0:T(8,128)} %copy-done.2, f32[8,32,128]{2,1,0:T(8,128)} %copy-done.3, f32[64,128]{1,0:T(8,128)} %get-tuple-element.36.near_ref, ...), custom_call_target="tpu_custom_call" | custom-call | flops 4000000000 | bytes 1000000 | tf_op jit(solution)/shard_map/finish_next/pallas_call | solution.py:459
  136.2 32.1 %all_to_all.25.last_ref = f32[256,1,128]{2,1,0:T(1,128)} all-to-all(f32[256,1,128]{2,1,0:T(1,128)} %get-tuple-element.39), channel_id=1, replica_groups=mesh['grp'=8,'dev'=32] {'grp','dev'}, dimensions={0} | all-to-all | bytes 262144 | tf_op jit(solution)/shard_map/all_to_all | solution.py:480
  168.3 2.0 %last.1 = (f32[64,128]{1,0:T(8,128)}, f32[64,128]{1,0:T(8,128)}) custom-call(f32[64,128]{1,0:T(8,128)} %bitcast.12, f32[64,128]{1,0:T(8,128)} %get-tuple-element.32.field_ref, f32[64,128]{1,0:T(8,128)} %get-tuple-element.38.field2_ref, f32[8,32,128]{2,1,0:T(8,128)} %copy-done.3, f32[256,1,128]{2,1,0:T(1,128)} %all_to_all.25.last_ref), custom_call_target="tpu_custom_call" | custom-call | flops 1000000000 | bytes 1000000 | tf_op jit(solution)/shard_map/last/pallas_call | solution.py:459
  (13 shorter events, 0.0 us)
Async XLA Ops:
  4.5 45.1 %collective-permute-start = (f32[4,8192]{1,0:T(4,128)}, f32[4,8192]{1,0:T(4,128)S(1)}, u32[]{:S(2)}, u32[]{:S(2)}) collective-permute-start(f32[4,8192]{1,0:T(4,128)} %get-tuple-element.23.pay_ref), channel_id=1, source_target_pairs={{0,1},{1,2},{2,3},{3,4},{4,5},{5,6},{6,7},{7,8},{8,9},{9,10},{10,1... | collective-permute-start | bytes 393224 | tf_op jit(solution)/shard_map/ppermute | solution.py:476
  9.1 40.6 %collective-permute-start.1 = (f32[4,8192]{1,0:T(4,128)}, f32[4,8192]{1,0:T(4,128)S(1)}, u32[]{:S(2)}, u32[]{:S(2)}) collective-permute-start(f32[4,8192]{1,0:T(4,128)} %get-tuple-element.23.pay_ref), channel_id=1, source_target_pairs={{1,0},{2,1},{3,2},{4,3},{5,4},{6,5},{7,6},{8,7},{9,8},{10,9},{11,1... | collective-permute-start | bytes 393224 | tf_op jit(solution)/shard_map/ppermute | solution.py:476
  11.1 26.0 %all-to-all-start = ((f32[32,72,128]{2,1,0:T(8,128)}), f32[32,72,128]{2,1,0:T(8,128)S(1)}, u32[]{:S(2)}, u32[]{:S(2)}) async-start(f32[32,72,128]{2,1,0:T(8,128)} %get-tuple-element.22), calls=%async_computation | async-start | bytes 2359296 | tf_op jit(solution)/shard_map/all_to_all | solution.py:480
  37.1 2.4 %copy-start = (f32[32,72,128]{2,1,0:T(8,128)}, f32[32,72,128]{2,1,0:T(8,128)S(1)}, u32[]{:S(2)}) copy-start(f32[32,72,128]{2,1,0:T(8,128)S(1)} %all-to-all-done.group_ref) | copy-start | bytes 3538948
  39.5 28.9 %all-to-all-start.1 = ((f32[8,64,128]{2,1,0:T(8,128)}), f32[8,64,128]{2,1,0:T(8,128)S(1)}, u32[]{:S(2)}, u32[]{:S(2)}) async-start(f32[8,64,128]{2,1,0:T(8,128)} %node_first.1), calls=%async_computation.1 | async-start | bytes 524288 | tf_op jit(solution)/shard_map/all_to_all | solution.py:480
  49.7 0.7 copy-start.4
  49.7 0.7 copy-start.5
  68.4 0.7 copy-start.2
  74.0 39.1 %collective-permute-start.2 = (f32[64,128]{1,0:T(8,128)}, f32[64,128]{1,0:T(8,128)S(1)}, u32[]{:S(2)}, u32[]{:S(2)}) collective-permute-start(f32[64,128]{1,0:T(8,128)} %get-tuple-element.32.field_ref), channel_id=1, source_target_pairs={{0,1},{1,2},{2,3},{3,4},{4,5},{5,6},{6,7},{7,8},{8,9},{9,10},{10,1... | collective-permute-start | bytes 98312 | tf_op jit(solution)/shard_map/ppermute | solution.py:476
  76.0 37.2 %collective-permute-start.3 = (f32[64,128]{1,0:T(8,128)}, f32[64,128]{1,0:T(8,128)S(1)}, u32[]{:S(2)}, u32[]{:S(2)}) collective-permute-start(f32[64,128]{1,0:T(8,128)} %get-tuple-element.32.field_ref), channel_id=1, source_target_pairs={{1,0},{2,1},{3,2},{4,3},{5,4},{6,5},{7,6},{8,7},{9,8},{10,9},{11,1... | collective-permute-start | bytes 98312 | tf_op jit(solution)/shard_map/ppermute | solution.py:476
  78.4 24.7 %all-to-all-start.2 = ((f32[32,24,128]{2,1,0:T(8,128)}), f32[32,24,128]{2,1,0:T(8,128)S(1)}, u32[]{:S(2)}, u32[]{:S(2)}) async-start(f32[32,24,128]{2,1,0:T(8,128)} %get-tuple-element.33), calls=%async_computation.2 | async-start | bytes 786432 | tf_op jit(solution)/shard_map/all_to_all | solution.py:480
  103.1 2.3 %copy-start.1 = (f32[32,24,128]{2,1,0:T(8,128)}, f32[32,24,128]{2,1,0:T(8,128)S(1)}, u32[]{:S(2)}) copy-start(f32[32,24,128]{2,1,0:T(8,128)S(1)} %all-to-all-done.2.group_ref) | copy-start | bytes 1179652
  105.4 25.5 %all-to-all-start.3 = ((f32[8,32,128]{2,1,0:T(8,128)}), f32[8,32,128]{2,1,0:T(8,128)S(1)}, u32[]{:S(2)}, u32[]{:S(2)}) async-start(f32[8,32,128]{2,1,0:T(8,128)} %node_next.1), calls=%async_computation.3 | async-start | bytes 262144 | tf_op jit(solution)/shard_map/all_to_all | solution.py:480
  113.2 0.6 copy-start.6
  113.2 0.6 copy-start.7
  130.9 0.7 copy-start.3

commit v2 on v1

--- a/solution.py
+++ b/solution.py
@@ -1,4 +1,3 @@
-import functools
 import math
 
 import jax
@@ -15,10 +14,9 @@
 AMPLITUDE = 0.00390625
 LENGTH = 0.25
 NUGGET = 2.0
-SCALE = math.sqrt(5.0) / LENGTH / LN2
-SHIFT = 1.5 / LN2
-OFFSET = 0.75 / (LN2 * LN2)
-FACTOR = AMPLITUDE * LN2 * LN2 / 3.0
+SCALE = math.sqrt(5.0) / LENGTH / 3.0
+POWER = -3.0 / LN2
+FACTOR = AMPLITUDE * 3.0
 SMEM = pl.BlockSpec(memory_space=pltpu.SMEM)
 LEAVES, PTS, RANK = 32, 256, 64
 DEPTH = 48
@@ -59,15 +57,18 @@
     norm = jnp.sum(coords * coords, axis=0, keepdims=True)
     full = jnp.where(row < 3, -2.0 * coords, jnp.where(row == 3, 1.0, jnp.where(row == 4, norm, 0.0)))
     hi, mid, low = split(full)
-    stack = jnp.concatenate([hi, mid, hi, mid, low, hi, jnp.zeros((128 - DEPTH,) + hi.shape[1:], F32)], axis=0)
-    return stack.T.astype(BF16)
+    rest = jnp.zeros((128 - DEPTH,) + hi.shape[1:], F32)
+    return jnp.concatenate([hi, mid, hi, mid, low, hi, rest], axis=0).T.astype(BF16)
+
+
+def squares(targets, sources):
+    return jnp.dot(targets[:, :DEPTH], sources, preferred_element_type=F32)
 
 
 def weighted(dist_sq, weights):
     dist_sq = jnp.maximum(dist_sq, 1e-30)
     dist = dist_sq * lax.rsqrt(dist_sq)
-    moved = dist + SHIFT
-    value = (moved * moved + OFFSET) * jnp.exp2(-dist) * weights
+    value = (dist_sq + (dist + 1.0 / 3.0)) * jnp.exp2(dist * POWER) * weights
     total = value[:, :128]
     for at in range(128, value.shape[1], 128):
         total = total + value[:, at : at + 128]
@@ -111,6 +112,8 @@
     near_ref[:3, :] = points_ref[...]
     for half in range(2 * LEAVES):
         near_ref[3:4, half * 128 : (half + 1) * 128] = rhs_ref[half : half + 1, :]
+    basis_ref.wait()
+    transfer_ref.wait()
     weights, node = project_end(
         lax.fori_loop(
             0, LEAVES, lambda l, c: project(c, l, row_of(rhs_ref, l), basis_ref, transfer_ref), project_start(), unroll=8
@@ -132,27 +135,51 @@
         pay_ref[d] = payload
 
 
+def near_parts(target_ref, centre_ref, source_ref, acc_ref, dist_ref):
+    def distances(l, at, slot):
+        centre = centre_ref[l]
+        coords = centred(source_ref[at], jnp.concatenate([centre, centre], axis=1))
+        dist_ref[slot] = squares(target_ref[l], source_stack(coords))
+
+    def products(l, at, slot, first):
+        weights = source_ref[at, 3:4, :] * FACTOR
+        for row in range(0, PTS, 64):
+            value = weighted(dist_ref[slot, row : row + 64, :], weights)
+            if first:
+                acc_ref[l, row : row + 64, :] = value
+            else:
+                acc_ref[l, row : row + 64, :] += value
+
+    return distances, products
+
+
+def near_self(target_ref, centre_ref, source_ref, acc_ref, dist_ref, beside, carry):
+    distances, products = near_parts(target_ref, centre_ref, source_ref, acc_ref, dist_ref)
+
+    def step(i, carry):
+        for k in range(STEP):
+            l = STEP * i + k
+            later = jnp.minimum(l + 1, LEAVES - 1)
+            distances(later, LEAVES + later, (k + 1) % 2)
+            products(l, LEAVES + l, k % 2, True)
+            carry = beside(l, carry)
+        return carry
+
+    distances(0, LEAVES, 0)
+    return lax.fori_loop(0, LEAVES // STEP, step, carry)
+
+
 def near_pairs(list_ref, target_ref, centre_ref, source_ref, acc_ref, dist_ref):
-    def distances(code, slot):
-        l = lax.shift_right_logical(code, 8)
-        centre = centre_ref[l]
-        coords = centred(source_ref[code & 255], jnp.concatenate([centre, centre], axis=1))
-        dist_ref[slot] = jnp.dot(target_ref[l, :, :DEPTH], source_stack(coords), preferred_element_type=F32)
-
-    def products(code, slot):
-        l = lax.shift_right_logical(code, 8)
-        weights = source_ref[code & 255, 3:4, :] * FACTOR
-        for at in range(0, PTS, 64):
-            acc_ref[l, at : at + 64, :] += weighted(dist_ref[slot, at : at + 64, :], weights)
+    distances, products = near_parts(target_ref, centre_ref, source_ref, acc_ref, dist_ref)
 
     def step(i, carry):
         codes = [list_ref[STEP * i + k + 1] for k in range(STEP + 1)]
         for k in range(STEP):
-            distances(codes[k + 1], (k + 1) % 2)
-            products(codes[k], k % 2)
-        return carry
-
-    distances(list_ref[1], 0)
+            distances(lax.shift_right_logical(codes[k + 1], 8), codes[k + 1] & 255, (k + 1) % 2)
+            products(lax.shift_right_logical(codes[k], 8), codes[k] & 255, k % 2, False)
+        return carry
+
+    distances(lax.shift_right_logical(list_ref[1], 8), list_ref[1] & 255, 0)
     lax.fori_loop(0, (list_ref[0] + STEP - 1) // STEP, step, 0)
 
 
@@ -201,35 +228,37 @@
     here = lax.shift_right_logical(ids_ref[0, 0], 5)
     base = (here - 1) * LEAVES
 
-    def leaf_slots(l, counts):
-        def slot(j, counts):
-            own, other = counts
+    fill(source_ref, LEAVES, pay_ref)
+
+    def targets(l, carry):
+        tile = source_ref[LEAVES + l]
+        centre = jnp.broadcast_to(jnp.sum(tile, axis=1, keepdims=True) * (1.0 / PTS), (8, 128))
+        centre_ref[l] = centre
+        target_ref[l] = target_stack(centred(tile, jnp.concatenate([centre, centre], axis=1)))
+        return carry
+
+    lax.fori_loop(0, LEAVES, targets, 0, unroll=4)
+
+    def slots(l, counts):
+        own, other = counts
+        used = count_ref[l]
+        for j in range(1, 8):
             n = ids_ref[j, l]
             code = l * 256 + (n - base)
-            is_own = (lax.shift_right_logical(n, 5) == here).astype(jnp.int32)
             own_list_ref[own] = code
             other_list_ref[other] = code
-            return own + is_own, other + 1 - is_own
-
-        return lax.fori_loop(0, jnp.minimum(count_ref[l], 8), slot, counts)
-
-    own, other = lax.fori_loop(0, LEAVES, leaf_slots, (jnp.int32(1), jnp.int32(1)))
+            is_used = (j < used).astype(jnp.int32)
+            is_own = (lax.shift_right_logical(n, 5) == here).astype(jnp.int32) * is_used
+            own, other = own + is_own, other + is_used - is_own
+        return own, other
+
+    one = jnp.int32(1)
+    own, other = near_self(target_ref, centre_ref, source_ref, acc_ref, dist_ref, slots, (one, one))
     for k in range(STEP + 1):
         own_list_ref[own + k] = DUMMY
         other_list_ref[other + k] = DUMMY
     own_list_ref[0] = own - 1
     other_list_ref[0] = other - 1
-    fill(source_ref, LEAVES, pay_ref)
-    clear(acc_ref)
-
-    def targets(l, carry):
-        tile = source_ref[LEAVES + l]
-        centre = jnp.broadcast_to(jnp.sum(tile, axis=1, keepdims=True) * (1.0 / PTS), (8, 128))
-        centre_ref[l] = centre
-        target_ref[l] = target_stack(centred(tile, jnp.concatenate([centre, centre], axis=1)))
-        return carry
-
-    lax.fori_loop(0, LEAVES, targets, 0, unroll=4)
     near_pairs(own_list_ref, target_ref, centre_ref, source_ref, acc_ref, dist_ref)
     near_rows(acc_ref, out_ref, None)
     for l in range(LEAVES):
@@ -239,51 +268,41 @@
 def own_next_kernel(own_list_ref, pay_ref, field_ref, target_ref, centre_ref, out_ref, source_ref, acc_ref, dist_ref):
     fill(source_ref, LEAVES, pay_ref)
     set_values(source_ref, LEAVES, field_ref)
-    clear(acc_ref)
+    near_self(target_ref, centre_ref, source_ref, acc_ref, dist_ref, lambda l, carry: carry, 0)
     near_pairs(own_list_ref, target_ref, centre_ref, source_ref, acc_ref, dist_ref)
     near_rows(acc_ref, out_ref, None)
 
 
-def node_first_kernel(in_ref, out_ref):
-    block = jnp.concatenate([in_ref[:, 0, :], in_ref[:, 1, :]], axis=0)
-    for g in range(8):
-        out_ref[g] = block
-
-
-def node_next_kernel(in_ref, out_ref):
-    for g in range(8):
-        out_ref[g] = in_ref[:, 0, :]
-
-
 def swap(tile):
     return pltpu.roll(tile, 64, 1)
 
 
+def low_lanes():
+    return lanes_of((1, 128)) < 64
+
+
+def spread(tile):
+    other = swap(tile)
+    return jnp.where(low_lanes(), tile, other), jnp.where(low_lanes(), other, tile)
+
+
 def far_partners(far_leaf_ref, l, rows_at):
-    low_lanes = lanes_of((1, 128)) < 64
-    for j in range(8):
-        tiles = []
-        for k in range(2):
-            p = far_leaf_ref[2 * j + k, l] & 1023
-            tile = rows_at(lax.shift_right_logical(p, 5), p & 15)
-            here = (lax.shift_right_logical(p, 4) & 1) == k
-            tiles.append(jnp.where(here, tile, swap(tile)))
-        yield jnp.where(low_lanes, tiles[0], tiles[1])
+    for j in range(0, 16, 2):
+        yield jnp.where(low_lanes(), rows_at(far_leaf_ref[j, l] & 1023), rows_at(far_leaf_ref[j + 1, l] & 1023))
 
 
 def far_sums(stack_ref, weight_ref, target_ref, out_ref, dist_ref):
     def distances(l, slot):
         for c in range(4):
-            dist_ref[slot, c * RANK : (c + 1) * RANK, :] = jnp.dot(
-                target_ref[l, :, :DEPTH], stack_ref[l, :, c * 256 : (c + 1) * 256], preferred_element_type=F32
-            )
+            dist_ref[slot, c * RANK : (c + 1) * RANK, :] = squares(target_ref[l], stack_ref[l, :, c * 256 : (c + 1) * 256])
 
     def products(l, slot):
         total = jnp.zeros((RANK, 128), F32)
         for c in range(4):
             weights = weight_ref[l, :1, c * 256 : (c + 1) * 256]
             total = total + weighted(dist_ref[slot, c * RANK : (c + 1) * RANK, :], weights)
-        out_ref[l] = total
+        column = jnp.sum(total, axis=1, keepdims=True)
+        out_ref[...] = jnp.where(lanes_of((RANK, 128)) == l, column, out_ref[...])
 
     def step(i, carry):
         for k in range(STEP):
@@ -291,44 +310,67 @@
             products(STEP * i + k, k % 2)
         return carry
 
+    out_ref[...] = jnp.zeros((RANK, 128), F32)
     distances(0, 0)
     lax.fori_loop(0, LEAVES // STEP, step, 0)
 
 
 def middle_first_kernel(
     other_list_ref, far_leaf_ref, prev_ref, next_ref, target_ref, centre_ref, own_ref, far_target_ref, far_centre_ref, group_ref,
-    near_ref, far_ref, stack_ref, source_ref, acc_ref, dist_ref, weight_ref,
+    near_ref, far_ref, stack_out_ref, source_ref, acc_ref, dist_ref, weight_ref, table_ref, stack_ref, stack_sem,
 ):
+    def table(d, carry):
+        for m in range(0, 16, 2):
+            low, high = spread(group_ref[d, 4 * m : 4 * m + 8, :])
+            for k in range(2):
+                table_ref[d * LEAVES + m + k] = low[4 * k : 4 * k + 4]
+                table_ref[d * LEAVES + m + k + 16] = high[4 * k : 4 * k + 4]
+        return carry
+
+    lax.fori_loop(0, 32, table, 0, unroll=4)
+
     def gather(l, carry):
         centre = far_centre_ref[l]
-        rows = far_partners(far_leaf_ref, l, lambda d, m: group_ref[d, pl.ds(4 * m, 4), :])
+        rows = far_partners(far_leaf_ref, l, lambda p: table_ref[p])
         for j, tile in enumerate(rows):
             at = j * 128
             weight_ref[l, :1, at : at + 128] = tile[3:4] * FACTOR
             stack_ref[l, :, at : at + 128] = source_stack(centred(eight(tile), centre))
         return carry
 
-    lax.fori_loop(0, LEAVES, gather, 0, unroll=2)
+    lax.fori_loop(0, LEAVES, gather, 0, unroll=4)
+    stack_copy = pltpu.make_async_copy(stack_ref, stack_out_ref, stack_sem)
+    stack_copy.start()
+    far_target_ref.wait()
     far_sums(stack_ref, weight_ref, far_target_ref, far_ref, dist_ref)
+    for operand in (prev_ref, next_ref, target_ref, centre_ref, own_ref):
+        operand.wait()
     fill(source_ref, 0, prev_ref)
     fill(source_ref, 2 * LEAVES, next_ref)
     clear(acc_ref)
     near_pairs(other_list_ref, target_ref, centre_ref, source_ref, acc_ref, dist_ref)
     near_rows(acc_ref, near_ref, own_ref)
+    stack_copy.wait()
 
 
 def middle_next_kernel(
     other_list_ref, far_leaf_ref, prev_ref, next_ref, prev_val_ref, next_val_ref, target_ref, centre_ref, own_ref, far_target_ref,
-    stack_ref, group_ref, near_ref, far_ref, source_ref, acc_ref, dist_ref, weight_ref,
+    stack_ref, group_ref, near_ref, far_ref, source_ref, acc_ref, dist_ref, weight_ref, table_ref,
 ):
+    for d in range(32):
+        low, high = spread(group_ref[d, :16, :])
+        table_ref[d * LEAVES : d * LEAVES + 16, :] = low
+        table_ref[d * LEAVES + 16 : d * LEAVES + 32, :] = high
+
     def gather(l, carry):
-        rows = far_partners(far_leaf_ref, l, lambda d, m: group_ref[d, pl.ds(m, 1), :])
+        rows = far_partners(far_leaf_ref, l, lambda p: table_ref[pl.ds(p, 1), :])
         for j, tile in enumerate(rows):
             weight_ref[l, :1, j * 128 : (j + 1) * 128] = tile * FACTOR
         return carry
 
-    lax.fori_loop(0, LEAVES, gather, 0, unroll=2)
-    far_sums(stack_ref, weight_ref, far_target_ref, far_ref, dist_ref)
+    lax.fori_loop(0, LEAVES, gather, 0, unroll=4)
+    for operand in (prev_ref, next_ref, prev_val_ref, next_val_ref, target_ref, centre_ref, own_ref):
+        operand.wait()
     fill(source_ref, 0, prev_ref)
     fill(source_ref, 2 * LEAVES, next_ref)
     set_values(source_ref, 0, prev_val_ref)
@@ -336,10 +378,12 @@
     clear(acc_ref)
     near_pairs(other_list_ref, target_ref, centre_ref, source_ref, acc_ref, dist_ref)
     near_rows(acc_ref, near_ref, own_ref)
+    far_target_ref.wait()
+    stack_ref.wait()
+    far_sums(stack_ref, weight_ref, far_target_ref, far_ref, dist_ref)
 
 
 def node_down(far_node_ref, node_skel_ref, nodes_ref, weight_ref):
-    low_lanes = lanes_of((1, 128)) < 64
     own = node_skel_ref[...]
     centre, target = skel_target(jnp.concatenate([own[:1], own[2:3], own[1:2]], axis=0))
     total = jnp.zeros((RANK, 128), F32)
@@ -353,20 +397,20 @@
                 if weight_ref is not None:
                     rows.append(weight_ref[g, pl.ds(d, 1), :])
                 tiles.append(jnp.concatenate(rows, axis=0))
-            even = jnp.where(low_lanes, tiles[0], swap(tiles[1]))
-            odd = jnp.where(low_lanes, swap(tiles[0]), tiles[1])
+            even = jnp.where(low_lanes(), tiles[0], swap(tiles[1]))
+            odd = jnp.where(low_lanes(), swap(tiles[0]), tiles[1])
             coords.append(eight(jnp.concatenate([even[:2], odd[:2]], axis=0)))
             weights.append(odd[1:2] if weight_ref is None else even[2:3])
         wide = jnp.concatenate([centre, centre], axis=1)
         sources = source_stack(centred(jnp.concatenate(coords, axis=1), wide))
-        dist_sq = jnp.dot(target[:, :DEPTH], sources, preferred_element_type=F32)
+        dist_sq = squares(target, sources)
         total = total + weighted(dist_sq, jnp.concatenate(weights, axis=1) * FACTOR)
     return jnp.sum(total.T, axis=0, keepdims=True)
 
 
 def leaf_row(l, down, far_ref, near_ref, basis_ref, transfer_ref):
     moved = transfer_ref[l] * down
-    total = far_ref[l] + jnp.concatenate([moved, jnp.zeros((RANK, 64), F32)], axis=1)
+    total = jnp.where(lanes_of((RANK, 128)) == l, far_ref[...], 0.0) + jnp.concatenate([moved, jnp.zeros((RANK, 64), F32)], axis=1)
     column = jnp.sum(total, axis=1, keepdims=True)
     return row_of(near_ref, l) + jnp.sum(basis_ref[l] * column, axis=0, keepdims=True)
 
@@ -387,6 +431,8 @@
     far_node_ref, node_skel_ref, nodes_ref, near_ref, far_ref, rhs_ref, basis_ref, transfer_ref, out_ref, pay_ref
 ):
     down = node_down(far_node_ref, node_skel_ref, nodes_ref, None)
+    for operand in (near_ref, far_ref, rhs_ref, basis_ref, transfer_ref):
+        operand.wait()
 
     def leaf(l, carry):
         row = leaf_row(l, down, far_ref, near_ref, basis_ref, transfer_ref)
@@ -417,6 +463,8 @@
     far_node_ref, node_skel_ref, nodes_ref, node_in_ref, near_ref, far_ref, rhs_ref, field_ref, basis_ref, transfer_ref, out_ref, pay_ref
 ):
     down = node_down(far_node_ref, node_skel_ref, nodes_ref, node_in_ref)
+    for operand in (near_ref, far_ref, rhs_ref, field_ref, basis_ref, transfer_ref):
+        operand.wait()
 
     def leaf(l, carry):
         out_ref[pl.ds(2 * l, 2), :] = pair_of(leaf_row(l, down, far_ref, near_ref, basis_ref, transfer_ref))
@@ -448,21 +496,48 @@
     residual_ref[...] = residual - alpha2 * (image + beta * (NUGGET * rhs + field))
 
 
-def whole(shape):
-    return pl.BlockSpec(shape, lambda i: (0,) * len(shape))
-
-
-def call(kernel, name, outs, ins, scratch=(), work=0):
-    def spec(shape, dtype):
-        return SMEM if dtype == jnp.int32 else whole(shape)
+class Operand:
+    def __init__(self, ref, copy):
+        self.ref, self.copy = ref, copy
+        self.shape = ref.shape
+
+    def wait(self):
+        self.copy.wait()
+
+    def __getitem__(self, at):
+        return self.ref[at]
+
+
+def call(kernel, name, outs, ins, scratch=(), work=0, late=(), apart=()):
+    floats = [at for at, array in enumerate(ins) if array.dtype != jnp.int32]
+
+    def whole(shape):
+        return pl.BlockSpec(shape, lambda i: (0,) * len(shape))
+
+    def body(*refs):
+        operands = list(refs[: len(ins)])
+        buffers, sems = refs[-1 - len(floats) : -1], refs[-1]
+        for k, at in enumerate(floats):
+            operands[at] = Operand(buffers[k], pltpu.make_async_copy(operands[at], buffers[k], sems.at[k]))
+        for at in [at for at in floats if at not in late] + list(late):
+            operands[at].copy.start()
+        for at in floats:
+            if at not in late:
+                operands[at].wait()
+        kernel(*operands, *refs[len(ins) : -1 - len(floats)])
 
     return pl.pallas_call(
-        kernel,
+        body,
         grid=(1,),
         out_shape=[jax.ShapeDtypeStruct(shape, dtype) for shape, dtype in outs],
-        in_specs=[spec(array.shape, array.dtype) for array in ins],
-        out_specs=[spec(shape, dtype) for shape, dtype in outs],
-        scratch_shapes=list(scratch),
+        in_specs=[SMEM if array.dtype == jnp.int32 else pl.BlockSpec(memory_space=pl.ANY) for array in ins],
+        out_specs=[
+            SMEM if dtype == jnp.int32 else pl.BlockSpec(memory_space=pl.ANY) if at in apart else whole(shape)
+            for at, (shape, dtype) in enumerate(outs)
+        ],
+        scratch_shapes=list(scratch)
+        + [pltpu.VMEM(ins[at].shape, ins[at].dtype) for at in floats]
+        + [pltpu.SemaphoreType.DMA((len(floats),))],
         compiler_params=params(),
         cost_estimate=pl.CostEstimate(flops=work * 1_000_000_000, bytes_accessed=1_000_000, transcendentals=0),
         name=name,
@@ -495,6 +570,7 @@
         [((4, LEAVES * PTS), F32), ((32, 72, 128), F32)],
         [rhs, points, basis, transfer, leaf_skel, node_skel],
         work=4,
+        late=(2, 3),
     )
     prev_pay, next_pay = neighbours(near_pay)
     group = exchange(pay, "dev")
@@ -514,15 +590,18 @@
         near_scratch,
         work=15,
     )
-    (node_pay,) = call(node_first_kernel, "node_first", [((8, 64, 128), F32)], [group[:, 64:72]], work=1)
+    rows = jnp.swapaxes(group[:, 64:66], 0, 1).reshape(1, 64, 128)
+    node_pay = jnp.broadcast_to(rows, (8, 64, 128))
     nodes = exchange(node_pay, "grp")
     near_part, far_part, stacks = call(
         middle_first_kernel,
         "middle_first",
-        [vector, ((LEAVES, RANK, 128), F32), ((LEAVES, DEPTH, 1024), BF16)],
+        [vector, ((RANK, 128), F32), ((LEAVES, DEPTH, 1024), BF16)],
         [other_list, far_leaf, prev_pay, next_pay, targets, centres, own_part, far_targets, far_centres, group],
-        near_scratch + far_scratch,
+        near_scratch + far_scratch + [pltpu.VMEM((1024, 4, 128), F32), pltpu.VMEM((LEAVES, DEPTH, 1024), BF16), pltpu.SemaphoreType.DMA],
         work=20,
+        apart=(2,),
+        late=(7, 2, 3, 4, 5, 6),
     )
     field, pay = call(
         finish_first_kernel,
@@ -530,23 +609,25 @@
         [vector, ((32, 24, 128), F32)],
         [far_node, node_skel, nodes, near_part, far_part, rhs, basis, transfer],
         work=4,
+        late=(3, 4, 5, 6, 7),
     )
     prev_val, next_val = neighbours(field)
     leaf_in = exchange(pay, "dev")
     (own_part,) = call(
         own_next_kernel, "own_next", [vector], [own_list, near_pay, field, targets, centres], near_scratch, work=10
     )
-    (node_pay,) = call(node_next_kernel, "node_next", [((8, 32, 128), F32)], [leaf_in[:, 16:24]], work=1)
+    node_pay = jnp.broadcast_to(leaf_in[None, :, 16], (8, 32, 128))
     node_in = exchange(node_pay, "grp")
     near_part, far_part = call(
         middle_next_kernel,
         "middle_next",
-        [vector, ((LEAVES, RANK, 128), F32)],
+        [vector, ((RANK, 128), F32)],
         [
             other_list, far_leaf, prev_pay, next_pay, prev_val, next_val, targets, centres, own_part, far_targets, stacks, leaf_in,
         ],
-        near_scratch + far_scratch,
+        near_scratch + far_scratch + [pltpu.VMEM((1024, 128), F32)],
         work=20,
+        late=(6, 2, 3, 4, 5, 7, 8, 9, 10),
     )
     field2, pay = call(
         finish_next_kernel,
@@ -554,6 +635,7 @@
         [vector, ((256, 1, 128), F32)],
         [far_node, node_skel, nodes, node_in, near_part, far_part, rhs, field, basis, transfer],
         work=4,
+        late=(4, 5, 6, 7, 8, 9),
     )
     last = exchange(pay, AXES)
     answer, residual = call(last_kernel, "last", [vector, vector], [rhs, field, field2, node_in, last], work=1)

time: 173 us -> 162 us (0.936); the launches traced: 170 us -> 162 us
  Pallas kernels: 79 us -> 87.1 us
  starting transfers between devices: 50.2 us -> 42.9 us
  blocking collectives: 32.1 us -> 25.6 us
  waiting for transfers between devices: 4.03 us -> 0.94 us
    pallas_call x10 -> x8, Pallas kernels: 79 us -> 87.1 us  [call(): pl.pallas_call(body, grid=(1,), out_shape=[jax.ShapeDtypeStruct(shape, dt...]
    all_to_all x4, starting transfers between devices: 39.4 us -> 31.7 us  [exchange(): return lax.all_to_all(copies, axes, 0, 0, tiled=True)]
    all_to_all x1, blocking collectives: 32.1 us -> 25.6 us  [exchange(): return lax.all_to_all(copies, axes, 0, 0, tiled=True)]
    all_to_all x4, waiting for transfers between devices: 4.02 us -> 0.93 us  [exchange(): return lax.all_to_all(copies, axes, 0, 0, tiled=True)]
  transfers between devices with their start and end apart: 8 -> 8, of which waited for: 1 -> 1; matrix products, arithmetic and copies ran while one was open for 1% -> 1% of each run, Pallas kernels for 37% -> 45%
where the time goes in v2:
time: 162 us
  Pallas kernels  87.1 us (54%)
  starting transfers between devices  42.9 us (26%)
  blocking collectives  25.6 us (16%)
  local copies, waits for them, and re-layouts  4.2 us (3%)
    pallas_call x8, Pallas kernels, call(): pl.pallas_call(body, grid=(1,), out_shape=[jax.ShapeDtypeStruct(shape, dt...  87.1 us
    all_to_all x4, starting transfers between devices, exchange(): return lax.all_to_all(copies, axes, 0, 0, tiled=True)  31.7 us
    all_to_all x1, blocking collectives, exchange(): return lax.all_to_all(copies, axes, 0, 0, tiled=True)  25.6 us
    ppermute x4, starting transfers between devices, neighbours(): return (lax.ppermute(block, AXES, up), lax.ppermute(block, AXES, down))  11.2 us
  transfers between devices with their start and end apart: 8, of which 1 were waited for; matrix products, arithmetic and copies ran while one was open for 1% of the time, Pallas kernels for 45%

profile of v2, /device:TPU:1, one launch (start us, length us, event | category | flops | bytes accessed | tf_op | source)
XLA Modules:
  0.0 161.7 jit_solution(10297214680830672268)
XLA Ops:
  0.6 3.9 %prepare.1 = (f32[4,8192]{1,0:T(4,128)}, f32[32,72,128]{2,1,0:T(8,128)}) custom-call(f32[64,128]{1,0:T(8,128)} %bitcast.15, f32[3,8192]{1,0:T(4,128)} %refs_1_.4, f32[32,64,256]{2,1,0:T(8,128)} %bitcast.12, f32[32,64,64]{2,1,0:T(8,128)} %refs_9_.1, f32[3,2048]{1,0:T(4,128)} %refs_3_.3, f32[3,64]{1,0:T(4,128)} %refs_1_.7), custom_call_target="tpu_custom_call" | custom-call | flops 4000000000 | bytes 1000000 | tf_op jit(solution)/shard_map/prepare/pallas_call | solution.py:529
  4.6 4.6 %collective-permute-start = (f32[4,8192]{1,0:T(4,128)}, f32[4,8192]{1,0:T(4,128)S(1)}, u32[]{:S(2)}, u32[]{:S(2)}) collective-permute-start(f32[4,8192]{1,0:T(4,128)} %get-tuple-element.23.refs_2_.refs_1_), channel_id=1, source_target_pairs={{0,1},{1,2},{2,3},{3,4},{4,5},{5,6},{6,7},{7,8},{8,9},{9,10},{10,1... | collective-permute-start | bytes 393224 | tf_op jit(solution)/shard_map/ppermute | solution.py:551
  9.2 1.9 %collective-permute-start.1 = (f32[4,8192]{1,0:T(4,128)}, f32[4,8192]{1,0:T(4,128)S(1)}, u32[]{:S(2)}, u32[]{:S(2)}) collective-permute-start(f32[4,8192]{1,0:T(4,128)} %get-tuple-element.23.refs_2_.refs_1_), channel_id=1, source_target_pairs={{1,0},{2,1},{3,2},{4,3},{5,4},{6,5},{7,6},{8,7},{9,8},{10,9},{11,1... | collective-permute-start | bytes 393224 | tf_op jit(solution)/shard_map/ppermute | solution.py:551
  11.1 7.6 %all-to-all-start = ((f32[32,72,128]{2,1,0:T(8,128)}), f32[32,72,128]{2,1,0:T(8,128)S(1)}, u32[]{:S(2)}, u32[]{:S(2)}) async-start(f32[32,72,128]{2,1,0:T(8,128)} %get-tuple-element.22), calls=%async_computation | async-start | bytes 2359296 | tf_op jit(solution)/shard_map/all_to_all | solution.py:555
  18.7 17.4 %own_first.1 = (bf16[32,256,128]{2,1,0:T(8,128)(2,1)}, f32[32,8,128]{2,1,0:T(8,128)}, bf16[32,64,128]{2,1,0:T(8,128)(2,1)}, f32[32,8,128]{2,1,0:T(8,128)}, s32[2...) custom-call(s32[8,32]{1,0:T(8,128)} %bitcast.21, s32[32]{0:T(128)} %refs_1_.5, f32[4,8192]{1,0:T(4,128)} %get-tuple-element.23.refs_2_.refs_1_, ...), custom_call_target="tpu_custom_call" | custom-call | flops 15000000512 | bytes 1000000 | tf_op jit(solution)/shard_map/own_first/pallas_call | solution.py:529
  36.2 0.9 all-to-all-done.refs_9_
  37.1 0.8 broadcast_in_dim.15
  37.9 10.2 %all-to-all-start.1 = ((f32[8,64,128]{2,1,0:T(8,128)}), f32[8,64,128]{2,1,0:T(8,128)S(1)}, u32[]{:S(2)}, u32[]{:S(2)}) async-start(f32[8,64,128]{2,1,0:T(8,128)} %broadcast_in_dim.15), calls=%async_computation.1 | async-start | bytes 524288 | tf_op jit(solution)/shard_map/all_to_all | solution.py:555
  48.1 0.0 collective-permute-done.refs_2_
  48.2 0.0 collective-permute-done.1.refs_3_
  48.2 0.6 copy-done.4
  48.8 0.1 copy-done.5
  48.9 20.7 %middle_first.1 = (f32[64,128]{1,0:T(8,128)}, f32[64,128]{1,0:T(8,128)}, bf16[32,48,1024]{2,1,0:T(8,128)(2,1)}) custom-call(s32[272]{0:T(512)} %get-tuple-element.24.refs_0_, s32[16,32]{1,0:T(8,128)} %bitcast.19, f32[4,8192]{1,0:T(4,128)} %copy-done.4, f32[4,8192]{1,0:T(4,128)} %copy-done.5, bf16[32,256,128]{2,1,0:T(8,128)(2,1)} %get-tuple-element.25.refs_4_.refs_3_.refs_6_, ...), custom_call_target="tpu_custom_call" | custom-call | flops 20000000000 | bytes 1000000 | tf_op jit(solution)/shard_map/middle_first/pallas_call | solution.py:529
  69.6 0.0 all-to-all-done.1.refs_2_
  69.6 0.7 copy-done.2
  70.3 4.7 %finish_first.1 = (f32[64,128]{1,0:T(8,128)}, f32[32,24,128]{2,1,0:T(8,128)}) custom-call(s32[1,32]{1,0:T(1,128)} %refs_0_.3, f32[3,64]{1,0:T(4,128)} %refs_1_.7, f32[8,64,128]{2,1,0:T(8,128)} %copy-done.2, f32[64,128]{1,0:T(8,128)} %get-tuple-element.30.refs_3_, f32[64,128]{1,0:T(8,128)} %get-tuple-element.31.refs_4_, f32[64,128]{1,0:T(8,128)} %bitcast.16, ...), custom_call_target="tpu_custom_call" | custom-call | flops 4000000000 | bytes 1000000 | tf_op jit(solution)/shard_map/finish_first/pallas_call | solution.py:529
  75.0 2.8 %collective-permute-start.2 = (f32[64,128]{1,0:T(8,128)}, f32[64,128]{1,0:T(8,128)S(1)}, u32[]{:S(2)}, u32[]{:S(2)}) collective-permute-start(f32[64,128]{1,0:T(8,128)} %get-tuple-element.32.refs_2_.refs_7_.refs_1_), channel_id=1, source_target_pairs={{0,1},{1,2},{2,3},{3,4},{4,5},{5,6},{6,7},{7,8},{8,9},{9,10},{10,1... | collective-permute-start | bytes 98312 | tf_op jit(solution)/shard_map/ppermute | solution.py:551
  77.9 1.9 %collective-permute-start.3 = (f32[64,128]{1,0:T(8,128)}, f32[64,128]{1,0:T(8,128)S(1)}, u32[]{:S(2)}, u32[]{:S(2)}) collective-permute-start(f32[64,128]{1,0:T(8,128)} %get-tuple-element.32.refs_2_.refs_7_.refs_1_), channel_id=1, source_target_pairs={{1,0},{2,1},{3,2},{4,3},{5,4},{6,5},{7,6},{8,7},{9,8},{10,9},{11,1... | collective-permute-start | bytes 98312 | tf_op jit(solution)/shard_map/ppermute | solution.py:551
  79.8 7.1 %all-to-all-start.2 = ((f32[32,24,128]{2,1,0:T(8,128)}), f32[32,24,128]{2,1,0:T(8,128)S(1)}, u32[]{:S(2)}, u32[]{:S(2)}) async-start(f32[32,24,128]{2,1,0:T(8,128)} %get-tuple-element.33), calls=%async_computation.2 | async-start | bytes 786432 | tf_op jit(solution)/shard_map/all_to_all | solution.py:555
  86.9 14.6 %own_next.1.refs_8_ = f32[64,128]{1,0:T(8,128)} custom-call(s32[272]{0:T(512)} %get-tuple-element.34.refs_0_, f32[4,8192]{1,0:T(4,128)} %get-tuple-element.23.refs_2_.refs_1_, f32[64,128]{1,0:T(8,128)} %get-tuple-element.32.refs_2_.refs_7_.refs_1_, bf16[32,256,128]{2,1,0:T(8,128)(2,1)} %get-tuple-element.25.refs_4_.refs_3_.refs_6_, ...), custom_call_target="tpu_custom_call" | custom-call | flops 10000000000 | bytes 1000000 | tf_op jit(solution)/shard_map/own_next/pallas_call | solution.py:529
  101.6 0.7 broadcast_in_dim.17
  102.3 6.7 %all-to-all-start.3 = ((f32[8,32,128]{2,1,0:T(8,128)}), f32[8,32,128]{2,1,0:T(8,128)S(1)}, u32[]{:S(2)}, u32[]{:S(2)}) async-start(f32[8,32,128]{2,1,0:T(8,128)} %broadcast_in_dim.17), calls=%async_computation.3 | async-start | bytes 262144 | tf_op jit(solution)/shard_map/all_to_all | solution.py:555
  109.0 0.0 copy-start.6
  109.0 0.0 copy-start.7
  109.0 0.6 copy-done.6
  109.6 0.0 copy-done.7
  109.6 19.3 %middle_next.1 = (f32[64,128]{1,0:T(8,128)}, f32[64,128]{1,0:T(8,128)}) custom-call(s32[272]{0:T(512)} %get-tuple-element.24.refs_0_, s32[16,32]{1,0:T(8,128)} %bitcast.20, f32[4,8192]{1,0:T(4,128)} %copy-done.4, f32[4,8192]{1,0:T(4,128)} %copy-done.5, f32[64,128]{1,0:T(8,128)} %copy-done.6, f32[64,128]{1,0:T(8,128)} %copy-done.7, ...), custom_call_target="tpu_custom_call" | custom-call | flops 20000000000 | bytes 1000000 | tf_op jit(solution)/shard_map/middle_next/pallas_call | solution.py:529
  128.9 0.0 all-to-all-done.3.refs_3_
  128.9 0.6 copy-done.3
  129.6 4.4 %finish_next.1 = (f32[64,128]{1,0:T(8,128)}, f32[256,1,128]{2,1,0:T(1,128)}) custom-call(s32[1,32]{1,0:T(1,128)} %refs_0_.3, f32[3,64]{1,0:T(4,128)} %refs_1_.7, f32[8,64,128]{2,1,0:T(8,128)} %copy-done.2, f32[8,32,128]{2,1,0:T(8,128)} %copy-done.3, f32[64,128]{1,0:T(8,128)} %get-tuple-element.36.refs_4_, f32[64,128]{1,0:T(8,128)} %get-tuple-element.37.refs_5_, ...), custom_call_target="tpu_custom_call" | custom-call | flops 4000000000 | bytes 1000000 | tf_op jit(solution)/shard_map/finish_next/pallas_call | solution.py:529
  134.0 25.6 %all_to_all.25.refs_4_ = f32[256,1,128]{2,1,0:T(1,128)} all-to-all(f32[256,1,128]{2,1,0:T(1,128)} %get-tuple-element.39), channel_id=1, replica_groups=mesh['grp'=8,'dev'=32] {'grp','dev'}, dimensions={0} | all-to-all | bytes 262144 | tf_op jit(solution)/shard_map/all_to_all | solution.py:555
  159.6 2.1 %last.1 = (f32[64,128]{1,0:T(8,128)}, f32[64,128]{1,0:T(8,128)}) custom-call(f32[64,128]{1,0:T(8,128)} %bitcast.18, f32[64,128]{1,0:T(8,128)} %get-tuple-element.32.refs_2_.refs_7_.refs_1_, f32[64,128]{1,0:T(8,128)} %get-tuple-element.38.refs_2_, f32[8,32,128]{2,1,0:T(8,128)} %copy-done.3, f32[256,1,128]{2,1,0:T(1,128)} %all_to_all.25.refs_4_), custom_call_target="tpu_custom_call" | custom-call | flops 1000000000 | bytes 1000000 | tf_op jit(solution)/shard_map/last/pallas_call | solution.py:529
  (14 shorter events, 0.0 us)
Async XLA Ops:
  4.6 43.6 %collective-permute-start = (f32[4,8192]{1,0:T(4,128)}, f32[4,8192]{1,0:T(4,128)S(1)}, u32[]{:S(2)}, u32[]{:S(2)}) collective-permute-start(f32[4,8192]{1,0:T(4,128)} %get-tuple-element.23.refs_2_.refs_1_), channel_id=1, source_target_pairs={{0,1},{1,2},{2,3},{3,4},{4,5},{5,6},{6,7},{7,8},{8,9},{9,10},{10,1... | collective-permute-start | bytes 393224 | tf_op jit(solution)/shard_map/ppermute | solution.py:551
  9.2 39.0 %collective-permute-start.1 = (f32[4,8192]{1,0:T(4,128)}, f32[4,8192]{1,0:T(4,128)S(1)}, u32[]{:S(2)}, u32[]{:S(2)}) collective-permute-start(f32[4,8192]{1,0:T(4,128)} %get-tuple-element.23.refs_2_.refs_1_), channel_id=1, source_target_pairs={{1,0},{2,1},{3,2},{4,3},{5,4},{6,5},{7,6},{8,7},{9,8},{10,9},{11,1... | collective-permute-start | bytes 393224 | tf_op jit(solution)/shard_map/ppermute | solution.py:551
  11.1 26.0 %all-to-all-start = ((f32[32,72,128]{2,1,0:T(8,128)}), f32[32,72,128]{2,1,0:T(8,128)S(1)}, u32[]{:S(2)}, u32[]{:S(2)}) async-start(f32[32,72,128]{2,1,0:T(8,128)} %get-tuple-element.22), calls=%async_computation | async-start | bytes 2359296 | tf_op jit(solution)/shard_map/all_to_all | solution.py:555
  37.1 11.1 %copy-start = (f32[32,72,128]{2,1,0:T(8,128)}, f32[32,72,128]{2,1,0:T(8,128)S(1)}, u32[]{:S(2)}) copy-start(f32[32,72,128]{2,1,0:T(8,128)S(1)} %all-to-all-done.refs_9_) | copy-start | bytes 3538948
  37.9 31.7 %all-to-all-start.1 = ((f32[8,64,128]{2,1,0:T(8,128)}), f32[8,64,128]{2,1,0:T(8,128)S(1)}, u32[]{:S(2)}, u32[]{:S(2)}) async-start(f32[8,64,128]{2,1,0:T(8,128)} %broadcast_in_dim.15), calls=%async_computation.1 | async-start | bytes 524288 | tf_op jit(solution)/shard_map/all_to_all | solution.py:555
  48.1 0.6 copy-start.4
  48.2 0.7 copy-start.5
  69.6 0.7 copy-start.2
  75.0 33.9 %collective-permute-start.2 = (f32[64,128]{1,0:T(8,128)}, f32[64,128]{1,0:T(8,128)S(1)}, u32[]{:S(2)}, u32[]{:S(2)}) collective-permute-start(f32[64,128]{1,0:T(8,128)} %get-tuple-element.32.refs_2_.refs_7_.refs_1_), channel_id=1, source_target_pairs={{0,1},{1,2},{2,3},{3,4},{4,5},{5,6},{6,7},{7,8},{8,9},{9,10},{10,1... | collective-permute-start | bytes 98312 | tf_op jit(solution)/shard_map/ppermute | solution.py:551
  77.9 31.1 %collective-permute-start.3 = (f32[64,128]{1,0:T(8,128)}, f32[64,128]{1,0:T(8,128)S(1)}, u32[]{:S(2)}, u32[]{:S(2)}) collective-permute-start(f32[64,128]{1,0:T(8,128)} %get-tuple-element.32.refs_2_.refs_7_.refs_1_), channel_id=1, source_target_pairs={{1,0},{2,1},{3,2},{4,3},{5,4},{6,5},{7,6},{8,7},{9,8},{10,9},{11,1... | collective-permute-start | bytes 98312 | tf_op jit(solution)/shard_map/ppermute | solution.py:551
  79.8 21.7 %all-to-all-start.2 = ((f32[32,24,128]{2,1,0:T(8,128)}), f32[32,24,128]{2,1,0:T(8,128)S(1)}, u32[]{:S(2)}, u32[]{:S(2)}) async-start(f32[32,24,128]{2,1,0:T(8,128)} %get-tuple-element.33), calls=%async_computation.2 | async-start | bytes 786432 | tf_op jit(solution)/shard_map/all_to_all | solution.py:555
  101.5 7.5 %copy-start.1 = (f32[32,24,128]{2,1,0:T(8,128)}, f32[32,24,128]{2,1,0:T(8,128)S(1)}, u32[]{:S(2)}) copy-start(f32[32,24,128]{2,1,0:T(8,128)S(1)} %all-to-all-done.2.refs_11_) | copy-start | bytes 1179652
  102.3 26.6 %all-to-all-start.3 = ((f32[8,32,128]{2,1,0:T(8,128)}), f32[8,32,128]{2,1,0:T(8,128)S(1)}, u32[]{:S(2)}, u32[]{:S(2)}) async-start(f32[8,32,128]{2,1,0:T(8,128)} %broadcast_in_dim.17), calls=%async_computation.3 | async-start | bytes 262144 | tf_op jit(solution)/shard_map/all_to_all | solution.py:555
  109.0 0.6 copy-start.6
  109.0 0.6 copy-start.7
  128.9 0.7 copy-start.3

commit v3 on v2

--- a/solution.py
+++ b/solution.py
@@ -108,12 +108,7 @@
     return jnp.concatenate([rows[:16], rows[16:32]], axis=1), jnp.sum(carry[1], axis=0, keepdims=True)
 
 
-def prepare_kernel(rhs_ref, points_ref, basis_ref, transfer_ref, leaf_skel_ref, node_skel_ref, near_ref, pay_ref):
-    near_ref[:3, :] = points_ref[...]
-    for half in range(2 * LEAVES):
-        near_ref[3:4, half * 128 : (half + 1) * 128] = rhs_ref[half : half + 1, :]
-    basis_ref.wait()
-    transfer_ref.wait()
+def prepare_kernel(rhs_ref, basis_ref, transfer_ref, leaf_skel_ref, node_skel_ref, pay_ref):
     weights, node = project_end(
         lax.fori_loop(
             0, LEAVES, lambda l, c: project(c, l, row_of(rhs_ref, l), basis_ref, transfer_ref), project_start(), unroll=8
@@ -222,13 +217,17 @@
 
 
 def own_first_kernel(
-    ids_ref, count_ref, pay_ref, skel_ref, target_ref, centre_ref, far_target_ref, far_centre_ref, own_list_ref, other_list_ref, out_ref,
+    ids_ref, count_ref, points_ref, rhs_ref, skel_ref, target_ref, centre_ref, far_target_ref, far_centre_ref, own_list_ref, other_list_ref, out_ref, near_ref,
     source_ref, acc_ref, dist_ref,
 ):
     here = lax.shift_right_logical(ids_ref[0, 0], 5)
     base = (here - 1) * LEAVES
 
-    fill(source_ref, LEAVES, pay_ref)
+    near_ref[:3, :] = points_ref[...]
+    for half in range(2 * LEAVES):
+        near_ref[3:4, half * 128 : (half + 1) * 128] = rhs_ref[half : half + 1, :]
+    fill(source_ref, LEAVES, points_ref)
+    set_values(source_ref, LEAVES, rhs_ref)
 
     def targets(l, carry):
         tile = source_ref[LEAVES + l]
@@ -265,8 +264,11 @@
         far_centre_ref[l], far_target_ref[l] = skel_target(skel_ref[:, l * RANK : (l + 1) * RANK])
 
 
-def own_next_kernel(own_list_ref, pay_ref, field_ref, target_ref, centre_ref, out_ref, source_ref, acc_ref, dist_ref):
-    fill(source_ref, LEAVES, pay_ref)
+def own_next_kernel(
+    own_list_ref, points_ref, field_ref, target_ref, centre_ref, out_ref, field_out_ref, source_ref, acc_ref, dist_ref
+):
+    field_out_ref[...] = field_ref[...]
+    fill(source_ref, LEAVES, points_ref)
     set_values(source_ref, LEAVES, field_ref)
     near_self(target_ref, centre_ref, source_ref, acc_ref, dist_ref, lambda l, carry: carry, 0)
     near_pairs(own_list_ref, target_ref, centre_ref, source_ref, acc_ref, dist_ref)
@@ -564,17 +566,15 @@
     distances = pltpu.VMEM((2, PTS, 256), F32)
     near_scratch = [pltpu.VMEM((DUMMY + 1, 8, PTS), F32), pltpu.VMEM((LEAVES, PTS, 128), F32), distances]
     far_scratch = [pltpu.VMEM((LEAVES, 8, 1024), F32)]
-    near_pay, pay = call(
+    (pay,) = call(
         prepare_kernel,
         "prepare",
-        [((4, LEAVES * PTS), F32), ((32, 72, 128), F32)],
-        [rhs, points, basis, transfer, leaf_skel, node_skel],
+        [((32, 72, 128), F32)],
+        [rhs, basis, transfer, leaf_skel, node_skel],
         work=4,
-        late=(2, 3),
-    )
-    prev_pay, next_pay = neighbours(near_pay)
+    )
     group = exchange(pay, "dev")
-    targets, centres, far_targets, far_centres, own_list, other_list, own_part = call(
+    targets, centres, far_targets, far_centres, own_list, other_list, own_part, near_pay = call(
         own_first_kernel,
         "own_first",
         [
@@ -585,11 +585,13 @@
             ((LIST,), I32),
             ((LIST,), I32),
             vector,
+            ((4, LEAVES * PTS), F32),
         ],
-        [near_ids.T, near_count, near_pay, leaf_skel],
+        [near_ids.T, near_count, points, rhs, leaf_skel],
         near_scratch,
         work=15,
     )
+    prev_pay, next_pay = neighbours(near_pay)
     rows = jnp.swapaxes(group[:, 64:66], 0, 1).reshape(1, 64, 128)
     node_pay = jnp.broadcast_to(rows, (8, 64, 128))
     nodes = exchange(node_pay, "grp")
@@ -611,11 +613,11 @@
         work=4,
         late=(3, 4, 5, 6, 7),
     )
-    prev_val, next_val = neighbours(field)
     leaf_in = exchange(pay, "dev")
-    (own_part,) = call(
-        own_next_kernel, "own_next", [vector], [own_list, near_pay, field, targets, centres], near_scratch, work=10
-    )
+    own_part, near_field = call(
+        own_next_kernel, "own_next", [vector, vector], [own_list, points, field, targets, centres], near_scratch, work=10
+    )
+    prev_val, next_val = neighbours(near_field)
     node_pay = jnp.broadcast_to(leaf_in[None, :, 16], (8, 32, 128))
     node_in = exchange(node_pay, "grp")
     near_part, far_part = call(

time: 162 us -> 164 us (1.012)
  Pallas kernels: 87.1 us -> 64.1 us
  starting transfers between devices: 42.9 us -> 58.6 us
  blocking collectives: 25.6 us -> 35.6 us
    pallas_call x8, Pallas kernels: 87.1 us -> 64.1 us  [call(): pl.pallas_call(body, grid=(1,), out_shape=[jax.ShapeDtypeStruct(shape, dt...]
    all_to_all x4, starting transfers between devices: 31.7 us -> 45.8 us  [exchange(): return lax.all_to_all(copies, axes, 0, 0, tiled=True)]
    all_to_all x1, blocking collectives: 25.6 us -> 35.6 us  [exchange(): return lax.all_to_all(copies, axes, 0, 0, tiled=True)]
  transfers between devices with their start and end apart: 8 -> 8, of which waited for: 1 -> 0; matrix products, arithmetic and copies ran while one was open for 1% -> 1% of each run, Pallas kernels for 45% -> 30%
where the time goes in v3:
time: 164 us; the launch traced here: 163 us
  Pallas kernels  64.1 us (39%)
  starting transfers between devices  58.6 us (36%)
  blocking collectives  35.6 us (22%)
  local copies, waits for them, and re-layouts  4.24 us (3%)
    pallas_call x8, Pallas kernels, call(): pl.pallas_call(body, grid=(1,), out_shape=[jax.ShapeDtypeStruct(shape, dt...  64.1 us
    all_to_all x4, starting transfers between devices, exchange(): return lax.all_to_all(copies, axes, 0, 0, tiled=True)  45.8 us
    all_to_all x1, blocking collectives, exchange(): return lax.all_to_all(copies, axes, 0, 0, tiled=True)  35.6 us
    ppermute x4, starting transfers between devices, neighbours(): return (lax.ppermute(block, AXES, up), lax.ppermute(block, AXES, down))  12.8 us
  transfers between devices with their start and end apart: 8, of which 0 were waited for; matrix products, arithmetic and copies ran while one was open for 1% of the time, Pallas kernels for 30%

profile of v3, /device:TPU:1, one launch (start us, length us, event | category | flops | bytes accessed | tf_op | source)
XLA Modules:
  0.0 163.4 jit_solution(10095137913030986115)
XLA Ops:
  0.6 3.8 %prepare.1 = f32[32,72,128]{2,1,0:T(8,128)} custom-call(f32[64,128]{1,0:T(8,128)} %bitcast.15, f32[32,64,256]{2,1,0:T(8,128)} %bitcast.12, f32[32,64,64]{2,1,0:T(8,128)} %refs_9_.1, f32[3,2048]{1,0:T(4,128)} %refs_4_.3, f32[3,64]{1,0:T(4,128)} %refs_1_.7), custom_call_target="tpu_custom_call" | custom-call | flops 4000000000 | bytes 1000000 | tf_op jit(solution)/shard_map/prepare/pallas_call | solution.py:531
  4.4 8.6 %all-to-all-start = ((f32[32,72,128]{2,1,0:T(8,128)}), f32[32,72,128]{2,1,0:T(8,128)S(1)}, u32[]{:S(2)}, u32[]{:S(2)}) async-start(f32[32,72,128]{2,1,0:T(8,128)} %prepare.1), calls=%async_computation | async-start | bytes 2359296 | tf_op jit(solution)/shard_map/all_to_all | solution.py:557
  13.0 12.9 %own_first.1 = (bf16[32,256,128]{2,1,0:T(8,128)(2,1)}, f32[32,8,128]{2,1,0:T(8,128)}, bf16[32,64,128]{2,1,0:T(8,128)(2,1)}, f32[32,8,128]{2,1,0:T(8,128)}, s32[2...) custom-call(s32[8,32]{1,0:T(8,128)} %bitcast.22, s32[32]{0:T(128)} %refs_1_.4, f32[3,8192]{1,0:T(4,128)} %refs_1_.6, ...), custom_call_target="tpu_custom_call" | custom-call | flops 15000000512 | bytes 1000000 | tf_op jit(solution)/shard_map/own_first/pallas_call | solution.py:531
  25.9 4.5 %collective-permute-start = (f32[4,8192]{1,0:T(4,128)}, f32[4,8192]{1,0:T(4,128)S(1)}, u32[]{:S(2)}, u32[]{:S(2)}) collective-permute-start(f32[4,8192]{1,0:T(4,128)} %get-tuple-element.24), channel_id=1, source_target_pairs={{0,1},{1,2},{2,3},{3,4},{4,5},{5,6},{6,7},{7,8},{8,9},{9,10},{10,1... | collective-permute-start | bytes 393224 | tf_op jit(solution)/shard_map/ppermute | solution.py:553
  30.4 1.9 %collective-permute-start.1 = (f32[4,8192]{1,0:T(4,128)}, f32[4,8192]{1,0:T(4,128)S(1)}, u32[]{:S(2)}, u32[]{:S(2)}) collective-permute-start(f32[4,8192]{1,0:T(4,128)} %get-tuple-element.24), channel_id=1, source_target_pairs={{1,0},{2,1},{3,2},{4,3},{5,4},{6,5},{7,6},{8,7},{9,8},{10,9},{11,1... | collective-permute-start | bytes 393224 | tf_op jit(solution)/shard_map/ppermute | solution.py:553
  32.3 0.0 all-to-all-done.refs_9_
  32.4 0.8 broadcast_in_dim.15
  33.2 11.0 %all-to-all-start.1 = ((f32[8,64,128]{2,1,0:T(8,128)}), f32[8,64,128]{2,1,0:T(8,128)S(1)}, u32[]{:S(2)}, u32[]{:S(2)}) async-start(f32[8,64,128]{2,1,0:T(8,128)} %broadcast_in_dim.15), calls=%async_computation.1 | async-start | bytes 524288 | tf_op jit(solution)/shard_map/all_to_all | solution.py:557
  44.2 0.0 collective-permute-done.refs_2_
  44.2 0.0 collective-permute-done.1.refs_3_
  44.2 0.6 copy-done.4
  44.8 0.1 copy-done.5
  44.9 13.8 %middle_first.1 = (f32[64,128]{1,0:T(8,128)}, f32[64,128]{1,0:T(8,128)}, bf16[32,48,1024]{2,1,0:T(8,128)(2,1)}) custom-call(s32[272]{0:T(512)} %get-tuple-element.23.refs_0_, s32[16,32]{1,0:T(8,128)} %bitcast.20, f32[4,8192]{1,0:T(4,128)} %copy-done.4, f32[4,8192]{1,0:T(4,128)} %copy-done.5, bf16[32,256,128]{2,1,0:T(8,128)(2,1)} %get-tuple-element.25.refs_4_.refs_3_.refs_6_, ...), custom_call_target="tpu_custom_call" | custom-call | flops 20000000000 | bytes 1000000 | tf_op jit(solution)/shard_map/middle_first/pallas_call | solution.py:531
  58.7 0.7 copy-done.2
  59.4 4.7 %finish_first.1 = (f32[64,128]{1,0:T(8,128)}, f32[32,24,128]{2,1,0:T(8,128)}) custom-call(s32[1,32]{1,0:T(1,128)} %refs_0_.3, f32[3,64]{1,0:T(4,128)} %refs_1_.7, f32[8,64,128]{2,1,0:T(8,128)} %copy-done.2, f32[64,128]{1,0:T(8,128)} %get-tuple-element.30.refs_3_, f32[64,128]{1,0:T(8,128)} %get-tuple-element.31.refs_4_, f32[64,128]{1,0:T(8,128)} %bitcast.17, ...), custom_call_target="tpu_custom_call" | custom-call | flops 4000000000 | bytes 1000000 | tf_op jit(solution)/shard_map/finish_first/pallas_call | solution.py:531
  64.2 17.1 %all-to-all-start.2 = ((f32[32,24,128]{2,1,0:T(8,128)}), f32[32,24,128]{2,1,0:T(8,128)S(1)}, u32[]{:S(2)}, u32[]{:S(2)}) async-start(f32[32,24,128]{2,1,0:T(8,128)} %get-tuple-element.33), calls=%async_computation.2 | async-start | bytes 786432 | tf_op jit(solution)/shard_map/all_to_all | solution.py:557
  81.2 10.0 %own_next.1 = (f32[64,128]{1,0:T(8,128)}, f32[64,128]{1,0:T(8,128)}) custom-call(s32[272]{0:T(512)} %get-tuple-element.34.refs_0_, f32[3,8192]{1,0:T(4,128)} %refs_1_.6, f32[64,128]{1,0:T(8,128)} %get-tuple-element.32.refs_2_.refs_7_.refs_1_, bf16[32,256,128]{2,1,0:T(8,128)(2,1)} %get-tuple-element.25.refs_4_.refs_3_.refs_6_, ...), custom_call_target="tpu_custom_call" | custom-call | flops 10000000000 | bytes 1000000 | tf_op jit(solution)/shard_map/own_next/pallas_call | solution.py:531
  91.2 4.5 %collective-permute-start.2 = (f32[64,128]{1,0:T(8,128)}, f32[64,128]{1,0:T(8,128)S(1)}, u32[]{:S(2)}, u32[]{:S(2)}) collective-permute-start(f32[64,128]{1,0:T(8,128)} %get-tuple-element.35), channel_id=1, source_target_pairs={{0,1},{1,2},{2,3},{3,4},{4,5},{5,6},{6,7},{7,8},{8,9},{9,10},{10,1... | collective-permute-start | bytes 98312 | tf_op jit(solution)/shard_map/ppermute | solution.py:553
  95.7 1.9 %collective-permute-start.3 = (f32[64,128]{1,0:T(8,128)}, f32[64,128]{1,0:T(8,128)S(1)}, u32[]{:S(2)}, u32[]{:S(2)}) collective-permute-start(f32[64,128]{1,0:T(8,128)} %get-tuple-element.35), channel_id=1, source_target_pairs={{1,0},{2,1},{3,2},{4,3},{5,4},{6,5},{7,6},{8,7},{9,8},{10,9},{11,1... | collective-permute-start | bytes 98312 | tf_op jit(solution)/shard_map/ppermute | solution.py:553
  97.6 0.0 all-to-all-done.2.refs_11_
  97.7 0.7 broadcast_in_dim.17
  98.4 9.2 %all-to-all-start.3 = ((f32[8,32,128]{2,1,0:T(8,128)}), f32[8,32,128]{2,1,0:T(8,128)S(1)}, u32[]{:S(2)}, u32[]{:S(2)}) async-start(f32[8,32,128]{2,1,0:T(8,128)} %broadcast_in_dim.17), calls=%async_computation.3 | async-start | bytes 262144 | tf_op jit(solution)/shard_map/all_to_all | solution.py:557
  107.6 0.0 collective-permute-done.2.refs_4_
  107.6 0.0 copy-start.7
  107.6 0.6 copy-done.6
  108.2 0.0 copy-done.7
  108.2 12.4 %middle_next.1 = (f32[64,128]{1,0:T(8,128)}, f32[64,128]{1,0:T(8,128)}) custom-call(s32[272]{0:T(512)} %get-tuple-element.23.refs_0_, s32[16,32]{1,0:T(8,128)} %bitcast.21, f32[4,8192]{1,0:T(4,128)} %copy-done.4, f32[4,8192]{1,0:T(4,128)} %copy-done.5, f32[64,128]{1,0:T(8,128)} %copy-done.6, f32[64,128]{1,0:T(8,128)} %copy-done.7, ...), custom_call_target="tpu_custom_call" | custom-call | flops 20000000000 | bytes 1000000 | tf_op jit(solution)/shard_map/middle_next/pallas_call | solution.py:531
  120.7 0.0 all-to-all-done.3.refs_3_
  120.7 0.6 copy-done.3
  121.3 4.4 %finish_next.1 = (f32[64,128]{1,0:T(8,128)}, f32[256,1,128]{2,1,0:T(1,128)}) custom-call(s32[1,32]{1,0:T(1,128)} %refs_0_.3, f32[3,64]{1,0:T(4,128)} %refs_1_.7, f32[8,64,128]{2,1,0:T(8,128)} %copy-done.2, f32[8,32,128]{2,1,0:T(8,128)} %copy-done.3, f32[64,128]{1,0:T(8,128)} %get-tuple-element.38.refs_4_, f32[64,128]{1,0:T(8,128)} %get-tuple-element.39.refs_5_, ...), custom_call_target="tpu_custom_call" | custom-call | flops 4000000000 | bytes 1000000 | tf_op jit(solution)/shard_map/finish_next/pallas_call | solution.py:531
  125.7 35.6 %all_to_all.25.refs_4_ = f32[256,1,128]{2,1,0:T(1,128)} all-to-all(f32[256,1,128]{2,1,0:T(1,128)} %get-tuple-element.41), channel_id=1, replica_groups=mesh['grp'=8,'dev'=32] {'grp','dev'}, dimensions={0} | all-to-all | bytes 262144 | tf_op jit(solution)/shard_map/all_to_all | solution.py:557
  161.4 2.1 %last.1 = (f32[64,128]{1,0:T(8,128)}, f32[64,128]{1,0:T(8,128)}) custom-call(f32[64,128]{1,0:T(8,128)} %bitcast.19, f32[64,128]{1,0:T(8,128)} %get-tuple-element.32.refs_2_.refs_7_.refs_1_, f32[64,128]{1,0:T(8,128)} %get-tuple-element.40.refs_2_, f32[8,32,128]{2,1,0:T(8,128)} %copy-done.3, f32[256,1,128]{2,1,0:T(1,128)} %all_to_all.25.refs_4_), custom_call_target="tpu_custom_call" | custom-call | flops 1000000000 | bytes 1000000 | tf_op jit(solution)/shard_map/last/pallas_call | solution.py:531
  (14 shorter events, 0.0 us)
Async XLA Ops:
  4.4 27.9 %all-to-all-start = ((f32[32,72,128]{2,1,0:T(8,128)}), f32[32,72,128]{2,1,0:T(8,128)S(1)}, u32[]{:S(2)}, u32[]{:S(2)}) async-start(f32[32,72,128]{2,1,0:T(8,128)} %prepare.1), calls=%async_computation | async-start | bytes 2359296 | tf_op jit(solution)/shard_map/all_to_all | solution.py:557
  25.9 18.3 %collective-permute-start = (f32[4,8192]{1,0:T(4,128)}, f32[4,8192]{1,0:T(4,128)S(1)}, u32[]{:S(2)}, u32[]{:S(2)}) collective-permute-start(f32[4,8192]{1,0:T(4,128)} %get-tuple-element.24), channel_id=1, source_target_pairs={{0,1},{1,2},{2,3},{3,4},{4,5},{5,6},{6,7},{7,8},{8,9},{9,10},{10,1... | collective-permute-start | bytes 393224 | tf_op jit(solution)/shard_map/ppermute | solution.py:553
  30.4 13.8 %collective-permute-start.1 = (f32[4,8192]{1,0:T(4,128)}, f32[4,8192]{1,0:T(4,128)S(1)}, u32[]{:S(2)}, u32[]{:S(2)}) collective-permute-start(f32[4,8192]{1,0:T(4,128)} %get-tuple-element.24), channel_id=1, source_target_pairs={{1,0},{2,1},{3,2},{4,3},{5,4},{6,5},{7,6},{8,7},{9,8},{10,9},{11,1... | collective-permute-start | bytes 393224 | tf_op jit(solution)/shard_map/ppermute | solution.py:553
  32.3 11.9 %copy-start = (f32[32,72,128]{2,1,0:T(8,128)}, f32[32,72,128]{2,1,0:T(8,128)S(1)}, u32[]{:S(2)}) copy-start(f32[32,72,128]{2,1,0:T(8,128)S(1)} %all-to-all-done.refs_9_) | copy-start | bytes 3538948
  33.2 25.5 %all-to-all-start.1 = ((f32[8,64,128]{2,1,0:T(8,128)}), f32[8,64,128]{2,1,0:T(8,128)S(1)}, u32[]{:S(2)}, u32[]{:S(2)}) async-start(f32[8,64,128]{2,1,0:T(8,128)} %broadcast_in_dim.15), calls=%async_computation.1 | async-start | bytes 524288 | tf_op jit(solution)/shard_map/all_to_all | solution.py:557
  44.2 0.6 copy-start.4
  44.2 0.7 copy-start.5
  58.7 0.7 copy-start.2
  64.2 33.5 %all-to-all-start.2 = ((f32[32,24,128]{2,1,0:T(8,128)}), f32[32,24,128]{2,1,0:T(8,128)S(1)}, u32[]{:S(2)}, u32[]{:S(2)}) async-start(f32[32,24,128]{2,1,0:T(8,128)} %get-tuple-element.33), calls=%async_computation.2 | async-start | bytes 786432 | tf_op jit(solution)/shard_map/all_to_all | solution.py:557
  91.2 16.3 %collective-permute-start.2 = (f32[64,128]{1,0:T(8,128)}, f32[64,128]{1,0:T(8,128)S(1)}, u32[]{:S(2)}, u32[]{:S(2)}) collective-permute-start(f32[64,128]{1,0:T(8,128)} %get-tuple-element.35), channel_id=1, source_target_pairs={{0,1},{1,2},{2,3},{3,4},{4,5},{5,6},{6,7},{7,8},{8,9},{9,10},{10,1... | collective-permute-start | bytes 98312 | tf_op jit(solution)/shard_map/ppermute | solution.py:553
  95.7 11.9 %collective-permute-start.3 = (f32[64,128]{1,0:T(8,128)}, f32[64,128]{1,0:T(8,128)S(1)}, u32[]{:S(2)}, u32[]{:S(2)}) collective-permute-start(f32[64,128]{1,0:T(8,128)} %get-tuple-element.35), channel_id=1, source_target_pairs={{1,0},{2,1},{3,2},{4,3},{5,4},{6,5},{7,6},{8,7},{9,8},{10,9},{11,1... | collective-permute-start | bytes 98312 | tf_op jit(solution)/shard_map/ppermute | solution.py:553
  97.7 10.0 %copy-start.1 = (f32[32,24,128]{2,1,0:T(8,128)}, f32[32,24,128]{2,1,0:T(8,128)S(1)}, u32[]{:S(2)}) copy-start(f32[32,24,128]{2,1,0:T(8,128)S(1)} %all-to-all-done.2.refs_11_) | copy-start | bytes 1179652
  98.4 22.2 %all-to-all-start.3 = ((f32[8,32,128]{2,1,0:T(8,128)}), f32[8,32,128]{2,1,0:T(8,128)S(1)}, u32[]{:S(2)}, u32[]{:S(2)}) async-start(f32[8,32,128]{2,1,0:T(8,128)} %broadcast_in_dim.17), calls=%async_computation.3 | async-start | bytes 262144 | tf_op jit(solution)/shard_map/all_to_all | solution.py:557
  107.6 0.6 copy-start.6
  107.6 0.6 copy-start.7
  120.7 0.7 copy-start.3

commit v4 on v3

--- a/solution.py
+++ b/solution.py
@@ -26,7 +26,7 @@
 
 
 def params():
-    return pltpu.CompilerParams(vmem_limit_bytes=58 * 1024 * 1024)
+    return pltpu.CompilerParams(vmem_limit_bytes=64 * 1024 * 1024)
 
 
 def split(x):

time: 164 us -> 162 us (0.988)
    unnamed x16 -> x0, local copies, waits for them, and re-layouts: 2.64 us -> none
    all_to_all x4, starting transfers between devices: 45.8 us -> 43.2 us  [exchange(): return lax.all_to_all(copies, axes, 0, 0, tiled=True)]
    ppermute x4, starting transfers between devices: 12.8 us -> 14.8 us  [neighbours(): return (lax.ppermute(block, AXES, up), lax.ppermute(block, AXES, down))]
  transfers between devices with their start and end apart: 8 -> 8, of which waited for: 0 -> 0; matrix products, arithmetic and copies ran while one was open for 1% -> 2% of each run, Pallas kernels for 30% -> 30%
where the time goes in v4:
time: 162 us
  Pallas kernels  64.1 us (40%)
  starting transfers between devices  58 us (36%)
  blocking collectives  35.5 us (22%)
  local copies, waits for them, and re-layouts  3.2 us (2%)
    pallas_call x8, Pallas kernels, call(): pl.pallas_call(body, grid=(1,), out_shape=[jax.ShapeDtypeStruct(shape, dt...  64.1 us
    all_to_all x4, starting transfers between devices, exchange(): return lax.all_to_all(copies, axes, 0, 0, tiled=True)  43.2 us
    all_to_all x1, blocking collectives, exchange(): return lax.all_to_all(copies, axes, 0, 0, tiled=True)  35.5 us
    ppermute x4, starting transfers between devices, neighbours(): return (lax.ppermute(block, AXES, up), lax.ppermute(block, AXES, down))  14.8 us
  transfers between devices with their start and end apart: 8, of which 0 were waited for; matrix products, arithmetic and copies ran while one was open for 2% of the time, Pallas kernels for 30%

profile of v4, /device:TPU:1, one launch (start us, length us, event | category | flops | bytes accessed | tf_op | source)
XLA Modules:
  0.0 161.6 jit_solution(13455916217215745960)
XLA Ops:
  0.6 3.8 %prepare.1 = f32[32,72,128]{2,1,0:T(8,128)} custom-call(f32[64,128]{1,0:T(8,128)} %bitcast.15, f32[32,64,256]{2,1,0:T(8,128)} %bitcast.12, f32[32,64,64]{2,1,0:T(8,128)} %refs_9_.1, f32[3,2048]{1,0:T(4,128)} %refs_4_.3, f32[3,64]{1,0:T(4,128)} %refs_1_.7), custom_call_target="tpu_custom_call" | custom-call | flops 4000000000 | bytes 1000000 | tf_op jit(solution)/shard_map/prepare/pallas_call | solution.py:531
  4.4 8.6 %all-to-all-start = ((f32[32,72,128]{2,1,0:T(8,128)}), f32[32,72,128]{2,1,0:T(8,128)}, u32[]{:S(2)}, u32[]{:S(2)}) async-start(f32[32,72,128]{2,1,0:T(8,128)} %prepare.1), calls=%async_computation | async-start | bytes 2359296 | tf_op jit(solution)/shard_map/all_to_all | solution.py:557
  13.1 12.8 %own_first.1 = (bf16[32,256,128]{2,1,0:T(8,128)(2,1)}, f32[32,8,128]{2,1,0:T(8,128)}, bf16[32,64,128]{2,1,0:T(8,128)(2,1)}, f32[32,8,128]{2,1,0:T(8,128)}, s32[2...) custom-call(s32[8,32]{1,0:T(8,128)} %bitcast.22, s32[32]{0:T(128)} %refs_1_.4, f32[3,8192]{1,0:T(4,128)} %refs_1_.6, ...), custom_call_target="tpu_custom_call" | custom-call | flops 15000000512 | bytes 1000000 | tf_op jit(solution)/shard_map/own_first/pallas_call | solution.py:531
  26.0 3.5 %collective-permute-start = (f32[4,8192]{1,0:T(4,128)}, f32[4,8192]{1,0:T(4,128)}, u32[]{:S(2)}, u32[]{:S(2)}) collective-permute-start(f32[4,8192]{1,0:T(4,128)} %get-tuple-element.24), channel_id=1, source_target_pairs={{0,1},{1,2},{2,3},{3,4},{4,5},{5,6},{6,7},{7,8},{8,9},{9,10},{10,1... | collective-permute-start | bytes 393224 | tf_op jit(solution)/shard_map/ppermute | solution.py:553
  29.5 3.8 %collective-permute-start.1 = (f32[4,8192]{1,0:T(4,128)}, f32[4,8192]{1,0:T(4,128)}, u32[]{:S(2)}, u32[]{:S(2)}) collective-permute-start(f32[4,8192]{1,0:T(4,128)} %get-tuple-element.24), channel_id=1, source_target_pairs={{1,0},{2,1},{3,2},{4,3},{5,4},{6,5},{7,6},{8,7},{9,8},{10,9},{11,1... | collective-permute-start | bytes 393224 | tf_op jit(solution)/shard_map/ppermute | solution.py:553
  33.4 0.0 all-to-all-done.refs_9_
  33.4 0.9 slice_bitcast_fusion
  34.3 0.7 broadcast_in_dim.15
  35.0 9.3 %all-to-all-start.1 = ((f32[8,64,128]{2,1,0:T(8,128)}), f32[8,64,128]{2,1,0:T(8,128)}, u32[]{:S(2)}, u32[]{:S(2)}) async-start(f32[8,64,128]{2,1,0:T(8,128)} %broadcast_in_dim.15), calls=%async_computation.1 | async-start | bytes 524288 | tf_op jit(solution)/shard_map/all_to_all | solution.py:557
  44.3 0.0 collective-permute-done.refs_2_
  44.3 0.0 collective-permute-done.1.refs_3_
  44.3 13.8 %middle_first.1 = (f32[64,128]{1,0:T(8,128)}, f32[64,128]{1,0:T(8,128)}, bf16[32,48,1024]{2,1,0:T(8,128)(2,1)}) custom-call(s32[272]{0:T(512)} %get-tuple-element.23.refs_0_, s32[16,32]{1,0:T(8,128)} %bitcast.20, f32[4,8192]{1,0:T(4,128)} %collective-permute-done.refs_2_, f32[4,8192]{1,0:T(4,128)} %collective-permute-done.1.refs_3_, ...), custom_call_target="tpu_custom_call" | custom-call | flops 20000000000 | bytes 1000000 | tf_op jit(solution)/shard_map/middle_first/pallas_call | solution.py:531
  58.1 0.0 all-to-all-done.1.refs_2_
  58.1 4.7 %finish_first.1 = (f32[64,128]{1,0:T(8,128)}, f32[32,24,128]{2,1,0:T(8,128)}) custom-call(s32[1,32]{1,0:T(1,128)} %refs_0_.3, f32[3,64]{1,0:T(4,128)} %refs_1_.7, f32[8,64,128]{2,1,0:T(8,128)} %all-to-all-done.1.refs_2_, f32[64,128]{1,0:T(8,128)} %get-tuple-element.30.refs_3_, f32[64,128]{1,0:T(8,128)} %get-tuple-element.31.refs_4_, f32[64,128]{1,0:T(8,128)} %bitcast.17, ...), custom_call_target="tpu_custom_call" | custom-call | flops 4000000000 | bytes 1000000 | tf_op jit(solution)/shard_map/finish_first/pallas_call | solution.py:531
  62.9 15.7 %all-to-all-start.2 = ((f32[32,24,128]{2,1,0:T(8,128)}), f32[32,24,128]{2,1,0:T(8,128)}, u32[]{:S(2)}, u32[]{:S(2)}) async-start(f32[32,24,128]{2,1,0:T(8,128)} %get-tuple-element.33), calls=%async_computation.2 | async-start | bytes 786432 | tf_op jit(solution)/shard_map/all_to_all | solution.py:557
  78.6 10.0 %own_next.1 = (f32[64,128]{1,0:T(8,128)}, f32[64,128]{1,0:T(8,128)}) custom-call(s32[272]{0:T(512)} %get-tuple-element.34.refs_0_, f32[3,8192]{1,0:T(4,128)} %refs_1_.6, f32[64,128]{1,0:T(8,128)} %get-tuple-element.32.refs_2_.refs_7_.refs_1_, bf16[32,256,128]{2,1,0:T(8,128)(2,1)} %get-tuple-element.25.refs_4_.refs_3_.refs_6_, ...), custom_call_target="tpu_custom_call" | custom-call | flops 10000000000 | bytes 1000000 | tf_op jit(solution)/shard_map/own_next/pallas_call | solution.py:531
  88.6 3.5 %collective-permute-start.2 = (f32[64,128]{1,0:T(8,128)}, f32[64,128]{1,0:T(8,128)}, u32[]{:S(2)}, u32[]{:S(2)}) collective-permute-start(f32[64,128]{1,0:T(8,128)} %get-tuple-element.35), channel_id=1, source_target_pairs={{0,1},{1,2},{2,3},{3,4},{4,5},{5,6},{6,7},{7,8},{8,9},{9,10},{10,1... | collective-permute-start | bytes 98312 | tf_op jit(solution)/shard_map/ppermute | solution.py:553
  92.1 3.8 %collective-permute-start.3 = (f32[64,128]{1,0:T(8,128)}, f32[64,128]{1,0:T(8,128)}, u32[]{:S(2)}, u32[]{:S(2)}) collective-permute-start(f32[64,128]{1,0:T(8,128)} %get-tuple-element.35), channel_id=1, source_target_pairs={{1,0},{2,1},{3,2},{4,3},{5,4},{6,5},{7,6},{8,7},{9,8},{10,9},{11,1... | collective-permute-start | bytes 98312 | tf_op jit(solution)/shard_map/ppermute | solution.py:553
  95.9 0.0 all-to-all-done.2.refs_11_
  96.0 0.9 slice.9
  96.9 0.7 broadcast_in_dim.17
  97.5 9.6 %all-to-all-start.3 = ((f32[8,32,128]{2,1,0:T(8,128)}), f32[8,32,128]{2,1,0:T(8,128)}, u32[]{:S(2)}, u32[]{:S(2)}) async-start(f32[8,32,128]{2,1,0:T(8,128)} %broadcast_in_dim.17), calls=%async_computation.3 | async-start | bytes 262144 | tf_op jit(solution)/shard_map/all_to_all | solution.py:557
  107.1 0.0 collective-permute-done.2.refs_4_
  107.1 0.0 collective-permute-done.3.refs_5_
  107.1 12.4 %middle_next.1 = (f32[64,128]{1,0:T(8,128)}, f32[64,128]{1,0:T(8,128)}) custom-call(s32[272]{0:T(512)} %get-tuple-element.23.refs_0_, s32[16,32]{1,0:T(8,128)} %bitcast.21, f32[4,8192]{1,0:T(4,128)} %collective-permute-done.refs_2_, f32[4,8192]{1,0:T(4,128)} %collective-permute-done.1.refs_3_, f32[64,128]{1,0:T(8,128)} %collective-permute-done.2.refs_4_, ...), custom_call_target="tpu_custom_call" | custom-call | flops 20000000000 | bytes 1000000 | tf_op jit(solution)/shard_map/middle_next/pallas_call | solution.py:531
  119.6 0.0 all-to-all-done.3.refs_3_
  119.6 4.4 %finish_next.1 = (f32[64,128]{1,0:T(8,128)}, f32[256,1,128]{2,1,0:T(1,128)}) custom-call(s32[1,32]{1,0:T(1,128)} %refs_0_.3, f32[3,64]{1,0:T(4,128)} %refs_1_.7, f32[8,64,128]{2,1,0:T(8,128)} %all-to-all-done.1.refs_2_, f32[8,32,128]{2,1,0:T(8,128)} %all-to-all-done.3.refs_3_, f32[64,128]{1,0:T(8,128)} %get-tuple-element.38.refs_4_, ...), custom_call_target="tpu_custom_call" | custom-call | flops 4000000000 | bytes 1000000 | tf_op jit(solution)/shard_map/finish_next/pallas_call | solution.py:531
  124.0 35.5 %all_to_all.25.refs_4_ = f32[256,1,128]{2,1,0:T(1,128)} all-to-all(f32[256,1,128]{2,1,0:T(1,128)} %get-tuple-element.41), channel_id=1, replica_groups=mesh['grp'=8,'dev'=32] {'grp','dev'}, dimensions={0} | all-to-all | bytes 262144 | tf_op jit(solution)/shard_map/all_to_all | solution.py:557
  159.5 2.1 %last.1 = (f32[64,128]{1,0:T(8,128)}, f32[64,128]{1,0:T(8,128)}) custom-call(f32[64,128]{1,0:T(8,128)} %bitcast.19, f32[64,128]{1,0:T(8,128)} %get-tuple-element.32.refs_2_.refs_7_.refs_1_, f32[64,128]{1,0:T(8,128)} %get-tuple-element.40.refs_2_, f32[8,32,128]{2,1,0:T(8,128)} %all-to-all-done.3.refs_3_, f32[256,1,128]{2,1,0:T(1,128)} %all_to_all.25.refs_4_), custom_call_target="tpu_custom_call" | custom-call | flops 1000000000 | bytes 1000000 | tf_op jit(solution)/shard_map/last/pallas_call | solution.py:531
  (1 shorter events, 0.0 us)
Async XLA Ops:
  4.4 28.9 %all-to-all-start = ((f32[32,72,128]{2,1,0:T(8,128)}), f32[32,72,128]{2,1,0:T(8,128)}, u32[]{:S(2)}, u32[]{:S(2)}) async-start(f32[32,72,128]{2,1,0:T(8,128)} %prepare.1), calls=%async_computation | async-start | bytes 2359296 | tf_op jit(solution)/shard_map/all_to_all | solution.py:557
  26.0 18.3 %collective-permute-start = (f32[4,8192]{1,0:T(4,128)}, f32[4,8192]{1,0:T(4,128)}, u32[]{:S(2)}, u32[]{:S(2)}) collective-permute-start(f32[4,8192]{1,0:T(4,128)} %get-tuple-element.24), channel_id=1, source_target_pairs={{0,1},{1,2},{2,3},{3,4},{4,5},{5,6},{6,7},{7,8},{8,9},{9,10},{10,1... | collective-permute-start | bytes 393224 | tf_op jit(solution)/shard_map/ppermute | solution.py:553
  29.5 14.8 %collective-permute-start.1 = (f32[4,8192]{1,0:T(4,128)}, f32[4,8192]{1,0:T(4,128)}, u32[]{:S(2)}, u32[]{:S(2)}) collective-permute-start(f32[4,8192]{1,0:T(4,128)} %get-tuple-element.24), channel_id=1, source_target_pairs={{1,0},{2,1},{3,2},{4,3},{5,4},{6,5},{7,6},{8,7},{9,8},{10,9},{11,1... | collective-permute-start | bytes 393224 | tf_op jit(solution)/shard_map/ppermute | solution.py:553
  35.0 23.1 %all-to-all-start.1 = ((f32[8,64,128]{2,1,0:T(8,128)}), f32[8,64,128]{2,1,0:T(8,128)}, u32[]{:S(2)}, u32[]{:S(2)}) async-start(f32[8,64,128]{2,1,0:T(8,128)} %broadcast_in_dim.15), calls=%async_computation.1 | async-start | bytes 524288 | tf_op jit(solution)/shard_map/all_to_all | solution.py:557
  62.9 33.1 %all-to-all-start.2 = ((f32[32,24,128]{2,1,0:T(8,128)}), f32[32,24,128]{2,1,0:T(8,128)}, u32[]{:S(2)}, u32[]{:S(2)}) async-start(f32[32,24,128]{2,1,0:T(8,128)} %get-tuple-element.33), calls=%async_computation.2 | async-start | bytes 786432 | tf_op jit(solution)/shard_map/all_to_all | solution.py:557
  88.6 18.5 %collective-permute-start.2 = (f32[64,128]{1,0:T(8,128)}, f32[64,128]{1,0:T(8,128)}, u32[]{:S(2)}, u32[]{:S(2)}) collective-permute-start(f32[64,128]{1,0:T(8,128)} %get-tuple-element.35), channel_id=1, source_target_pairs={{0,1},{1,2},{2,3},{3,4},{4,5},{5,6},{6,7},{7,8},{8,9},{9,10},{10,1... | collective-permute-start | bytes 98312 | tf_op jit(solution)/shard_map/ppermute | solution.py:553
  92.1 15.0 %collective-permute-start.3 = (f32[64,128]{1,0:T(8,128)}, f32[64,128]{1,0:T(8,128)}, u32[]{:S(2)}, u32[]{:S(2)}) collective-permute-start(f32[64,128]{1,0:T(8,128)} %get-tuple-element.35), channel_id=1, source_target_pairs={{1,0},{2,1},{3,2},{4,3},{5,4},{6,5},{7,6},{8,7},{9,8},{10,9},{11,1... | collective-permute-start | bytes 98312 | tf_op jit(solution)/shard_map/ppermute | solution.py:553
  97.5 22.0 %all-to-all-start.3 = ((f32[8,32,128]{2,1,0:T(8,128)}), f32[8,32,128]{2,1,0:T(8,128)}, u32[]{:S(2)}, u32[]{:S(2)}) async-start(f32[8,32,128]{2,1,0:T(8,128)} %broadcast_in_dim.17), calls=%async_computation.3 | async-start | bytes 262144 | tf_op jit(solution)/shard_map/all_to_all | solution.py:557

commit v5 on v4

--- a/solution.py
+++ b/solution.py
@@ -23,6 +23,7 @@
 DUMMY = 96
 STEP = 4
 LIST = 272
+PARTS = 4
 
 
 def params():
@@ -103,6 +104,15 @@
     return jnp.zeros((RANK, 128), F32), jnp.zeros((RANK, RANK), F32)
 
 
+def leaves_in_parts(operands, body, carry):
+    count = LEAVES // PARTS
+    for part in range(PARTS):
+        for operand in operands:
+            operand.wait(part)
+        carry = lax.fori_loop(part * count, (part + 1) * count, body, carry, unroll=count)
+    return carry
+
+
 def project_end(carry):
     rows = carry[0].T
     return jnp.concatenate([rows[:16], rows[16:32]], axis=1), jnp.sum(carry[1], axis=0, keepdims=True)
@@ -110,8 +120,8 @@
 
 def prepare_kernel(rhs_ref, basis_ref, transfer_ref, leaf_skel_ref, node_skel_ref, pay_ref):
     weights, node = project_end(
-        lax.fori_loop(
-            0, LEAVES, lambda l, c: project(c, l, row_of(rhs_ref, l), basis_ref, transfer_ref), project_start(), unroll=8
+        leaves_in_parts(
+            (basis_ref, transfer_ref), lambda l, c: project(c, l, row_of(rhs_ref, l), basis_ref, transfer_ref), project_start()
         )
     )
     skel = leaf_skel_ref[...]
@@ -217,8 +227,8 @@
 
 
 def own_first_kernel(
-    ids_ref, count_ref, points_ref, rhs_ref, skel_ref, target_ref, centre_ref, far_target_ref, far_centre_ref, own_list_ref, other_list_ref, out_ref, near_ref,
-    source_ref, acc_ref, dist_ref,
+    ids_ref, count_ref, points_ref, rhs_ref, skel_ref, target_out_ref, centre_ref, far_target_out_ref, far_centre_ref, own_list_ref, other_list_ref, out_ref,
+    near_ref, source_ref, acc_ref, dist_ref, target_ref, far_target_ref, out_sems,
 ):
     here = lax.shift_right_logical(ids_ref[0, 0], 5)
     base = (here - 1) * LEAVES
@@ -237,6 +247,14 @@
         return carry
 
     lax.fori_loop(0, LEAVES, targets, 0, unroll=4)
+    for l in range(LEAVES):
+        far_centre_ref[l], far_target_ref[l] = skel_target(skel_ref[:, l * RANK : (l + 1) * RANK])
+    copies = [
+        pltpu.make_async_copy(target_ref, target_out_ref, out_sems.at[0]),
+        pltpu.make_async_copy(far_target_ref, far_target_out_ref, out_sems.at[1]),
+    ]
+    for copy in copies:
+        copy.start()
 
     def slots(l, counts):
         own, other = counts
@@ -260,8 +278,8 @@
     other_list_ref[0] = other - 1
     near_pairs(own_list_ref, target_ref, centre_ref, source_ref, acc_ref, dist_ref)
     near_rows(acc_ref, out_ref, None)
-    for l in range(LEAVES):
-        far_centre_ref[l], far_target_ref[l] = skel_target(skel_ref[:, l * RANK : (l + 1) * RANK])
+    for copy in copies:
+        copy.wait()
 
 
 def own_next_kernel(
@@ -433,7 +451,7 @@
     far_node_ref, node_skel_ref, nodes_ref, near_ref, far_ref, rhs_ref, basis_ref, transfer_ref, out_ref, pay_ref
 ):
     down = node_down(far_node_ref, node_skel_ref, nodes_ref, None)
-    for operand in (near_ref, far_ref, rhs_ref, basis_ref, transfer_ref):
+    for operand in (near_ref, far_ref, rhs_ref):
         operand.wait()
 
     def leaf(l, carry):
@@ -441,7 +459,7 @@
         out_ref[pl.ds(2 * l, 2), :] = pair_of(row)
         return project(carry, l, row, basis_ref, transfer_ref)
 
-    weights, node = project_end(lax.fori_loop(0, LEAVES, leaf, project_start(), unroll=8))
+    weights, node = project_end(leaves_in_parts((basis_ref, transfer_ref), leaf, project_start()))
     rhs, image = rhs_ref[...], out_ref[...]
     extra = scalars([dot(rhs, rhs), dot(rhs, image)])
     last = jnp.where(lanes_of((1, 128)) < 64, jnp.concatenate([node, node], axis=1), extra)
@@ -465,14 +483,14 @@
     far_node_ref, node_skel_ref, nodes_ref, node_in_ref, near_ref, far_ref, rhs_ref, field_ref, basis_ref, transfer_ref, out_ref, pay_ref
 ):
     down = node_down(far_node_ref, node_skel_ref, nodes_ref, node_in_ref)
-    for operand in (near_ref, far_ref, rhs_ref, field_ref, basis_ref, transfer_ref):
+    for operand in (near_ref, far_ref, rhs_ref, field_ref):
         operand.wait()
 
     def leaf(l, carry):
         out_ref[pl.ds(2 * l, 2), :] = pair_of(leaf_row(l, down, far_ref, near_ref, basis_ref, transfer_ref))
         return carry
 
-    lax.fori_loop(0, LEAVES, leaf, 0, unroll=8)
+    leaves_in_parts((basis_ref, transfer_ref), leaf, 0)
     _, inner, energy, alpha = first_scalars(node_in_ref)
     rhs, field, field2 = rhs_ref[...], field_ref[...], out_ref[...]
     keep = inner / energy
@@ -499,18 +517,22 @@
 
 
 class Operand:
-    def __init__(self, ref, copy):
-        self.ref, self.copy = ref, copy
-        self.shape = ref.shape
-
-    def wait(self):
-        self.copy.wait()
+    def __init__(self, source, ref, sems, parts):
+        self.ref, self.shape = ref, ref.shape
+        if parts == 1:
+            self.copies = [pltpu.make_async_copy(source, ref, sems.at[0])]
+        else:
+            spans = [pl.ds(part * (ref.shape[0] // parts), ref.shape[0] // parts) for part in range(parts)]
+            self.copies = [pltpu.make_async_copy(source.at[span], ref.at[span], sems.at[n]) for n, span in enumerate(spans)]
+
+    def wait(self, part=0):
+        self.copies[part].wait()
 
     def __getitem__(self, at):
         return self.ref[at]
 
 
-def call(kernel, name, outs, ins, scratch=(), work=0, late=(), apart=()):
+def call(kernel, name, outs, ins, scratch=(), work=0, late=(), apart=(), split_up=()):
     floats = [at for at, array in enumerate(ins) if array.dtype != jnp.int32]
 
     def whole(shape):
@@ -520,9 +542,12 @@
         operands = list(refs[: len(ins)])
         buffers, sems = refs[-1 - len(floats) : -1], refs[-1]
         for k, at in enumerate(floats):
-            operands[at] = Operand(buffers[k], pltpu.make_async_copy(operands[at], buffers[k], sems.at[k]))
-        for at in [at for at in floats if at not in late] + list(late):
-            operands[at].copy.start()
+            operands[at] = Operand(operands[at], buffers[k], sems.at[k], PARTS if at in split_up else 1)
+        for at in [at for at in floats if at not in late] + [at for at in late if at not in split_up]:
+            operands[at].copies[0].start()
+        for part in range(PARTS if split_up else 0):
+            for at in split_up:
+                operands[at].copies[part].start()
         for at in floats:
             if at not in late:
                 operands[at].wait()
@@ -539,7 +564,7 @@
         ],
         scratch_shapes=list(scratch)
         + [pltpu.VMEM(ins[at].shape, ins[at].dtype) for at in floats]
-        + [pltpu.SemaphoreType.DMA((len(floats),))],
+        + [pltpu.SemaphoreType.DMA((len(floats), PARTS))],
         compiler_params=params(),
         cost_estimate=pl.CostEstimate(flops=work * 1_000_000_000, bytes_accessed=1_000_000, transcendentals=0),
         name=name,
@@ -572,6 +597,8 @@
         [((32, 72, 128), F32)],
         [rhs, basis, transfer, leaf_skel, node_skel],
         work=4,
+        late=(1, 2),
+        split_up=(1, 2),
     )
     group = exchange(pay, "dev")
     targets, centres, far_targets, far_centres, own_list, other_list, own_part, near_pay = call(
@@ -588,8 +615,10 @@
             ((4, LEAVES * PTS), F32),
         ],
         [near_ids.T, near_count, points, rhs, leaf_skel],
-        near_scratch,
+        near_scratch
+        + [pltpu.VMEM((LEAVES, PTS, 128), BF16), pltpu.VMEM((LEAVES, RANK, 128), BF16), pltpu.SemaphoreType.DMA((2,))],
         work=15,
+        apart=(0, 2),
     )
     prev_pay, next_pay = neighbours(near_pay)
     rows = jnp.swapaxes(group[:, 64:66], 0, 1).reshape(1, 64, 128)
@@ -612,6 +641,7 @@
         [far_node, node_skel, nodes, near_part, far_part, rhs, basis, transfer],
         work=4,
         late=(3, 4, 5, 6, 7),
+        split_up=(6, 7),
     )
     leaf_in = exchange(pay, "dev")
     own_part, near_field = call(
@@ -638,6 +668,7 @@
         [far_node, node_skel, nodes, node_in, near_part, far_part, rhs, field, basis, transfer],
         work=4,
         late=(4, 5, 6, 7, 8, 9),
+        split_up=(8, 9),
     )
     last = exchange(pay, AXES)
     answer, residual = call(last_kernel, "last", [vector, vector], [rhs, field, field2, node_in, last], work=1)

time: 162 us -> 161 us (level); the launches traced: 162 us -> 158 us
    all_to_all x4, starting transfers between devices: 43.2 us -> 37.5 us  [exchange(): return lax.all_to_all(copies, axes, 0, 0, tiled=True)]
    ppermute x4, starting transfers between devices: 14.8 us -> 19.3 us  [neighbours(): return (lax.ppermute(block, AXES, up), lax.ppermute(block, AXES, down))]
  transfers between devices with their start and end apart: 8 -> 8, of which waited for: 0 -> 0; matrix products, arithmetic and copies ran while one was open for 2% -> 2% of each run, Pallas kernels for 30% -> 31%
where the time goes in v5:
time: 161 us; the launch traced here: 158 us
  Pallas kernels  62.8 us (39%)
  starting transfers between devices  56.8 us (35%)
  blocking collectives  34.7 us (22%)
  local copies, waits for them, and re-layouts  3.2 us (2%)
    pallas_call x8, Pallas kernels, call(): pl.pallas_call(body, grid=(1,), out_shape=[jax.ShapeDtypeStruct(shape, dt...  62.8 us
    all_to_all x4, starting transfers between devices, exchange(): return lax.all_to_all(copies, axes, 0, 0, tiled=True)  37.5 us
    all_to_all x1, blocking collectives, exchange(): return lax.all_to_all(copies, axes, 0, 0, tiled=True)  34.7 us
    ppermute x4, starting transfers between devices, neighbours(): return (lax.ppermute(block, AXES, up), lax.ppermute(block, AXES, down))  19.3 us
  transfers between devices with their start and end apart: 8, of which 0 were waited for; matrix products, arithmetic and copies ran while one was open for 2% of the time, Pallas kernels for 31%

profile of v5, /device:TPU:1, one launch (start us, length us, event | category | flops | bytes accessed | tf_op | source)
XLA Modules:
  0.0 158.3 jit_solution(6633645336105979604)
XLA Ops:
  0.6 3.5 %prepare.1 = f32[32,72,128]{2,1,0:T(8,128)} custom-call(f32[64,128]{1,0:T(8,128)} %bitcast.15, f32[32,64,256]{2,1,0:T(8,128)} %bitcast.12, f32[32,64,64]{2,1,0:T(8,128)} %refs_9_.1, f32[3,2048]{1,0:T(4,128)} %refs_4_.3, f32[3,64]{1,0:T(4,128)} %refs_1_.7), custom_call_target="tpu_custom_call" | custom-call | flops 4000000000 | bytes 1000000 | tf_op jit(solution)/shard_map/prepare/pallas_call | solution.py:556
  4.1 8.6 %all-to-all-start = ((f32[32,72,128]{2,1,0:T(8,128)}), f32[32,72,128]{2,1,0:T(8,128)}, u32[]{:S(2)}, u32[]{:S(2)}) async-start(f32[32,72,128]{2,1,0:T(8,128)} %prepare.1), calls=%async_computation | async-start | bytes 2359296 | tf_op jit(solution)/shard_map/all_to_all | solution.py:582
  12.7 12.8 %own_first.1 = (bf16[32,256,128]{2,1,0:T(8,128)(2,1)}, f32[32,8,128]{2,1,0:T(8,128)}, bf16[32,64,128]{2,1,0:T(8,128)(2,1)}, f32[32,8,128]{2,1,0:T(8,128)}, s32[2...) custom-call(s32[8,32]{1,0:T(8,128)} %bitcast.22, s32[32]{0:T(128)} %refs_1_.4, f32[3,8192]{1,0:T(4,128)} %refs_1_.6, ...), custom_call_target="tpu_custom_call" | custom-call | flops 15000000512 | bytes 1000000 | tf_op jit(solution)/shard_map/own_first/pallas_call | solution.py:556
  25.5 4.5 %collective-permute-start = (f32[4,8192]{1,0:T(4,128)}, f32[4,8192]{1,0:T(4,128)}, u32[]{:S(2)}, u32[]{:S(2)}) collective-permute-start(f32[4,8192]{1,0:T(4,128)} %get-tuple-element.24), channel_id=1, source_target_pairs={{0,1},{1,2},{2,3},{3,4},{4,5},{5,6},{6,7},{7,8},{8,9},{9,10},{10,1... | collective-permute-start | bytes 393224 | tf_op jit(solution)/shard_map/ppermute | solution.py:578
  30.0 5.2 %collective-permute-start.1 = (f32[4,8192]{1,0:T(4,128)}, f32[4,8192]{1,0:T(4,128)}, u32[]{:S(2)}, u32[]{:S(2)}) collective-permute-start(f32[4,8192]{1,0:T(4,128)} %get-tuple-element.24), channel_id=1, source_target_pairs={{1,0},{2,1},{3,2},{4,3},{5,4},{6,5},{7,6},{8,7},{9,8},{10,9},{11,1... | collective-permute-start | bytes 393224 | tf_op jit(solution)/shard_map/ppermute | solution.py:578
  35.2 0.0 all-to-all-done.refs_9_
  35.2 0.9 slice_bitcast_fusion
  36.2 0.7 broadcast_in_dim.15
  36.9 7.2 %all-to-all-start.1 = ((f32[8,64,128]{2,1,0:T(8,128)}), f32[8,64,128]{2,1,0:T(8,128)}, u32[]{:S(2)}, u32[]{:S(2)}) async-start(f32[8,64,128]{2,1,0:T(8,128)} %broadcast_in_dim.15), calls=%async_computation.1 | async-start | bytes 524288 | tf_op jit(solution)/shard_map/all_to_all | solution.py:582
  44.1 0.0 collective-permute-done.refs_2_
  44.1 0.0 collective-permute-done.1.refs_3_
  44.1 13.5 %middle_first.1 = (f32[64,128]{1,0:T(8,128)}, f32[64,128]{1,0:T(8,128)}, bf16[32,48,1024]{2,1,0:T(8,128)(2,1)}) custom-call(s32[272]{0:T(512)} %get-tuple-element.23.refs_0_, s32[16,32]{1,0:T(8,128)} %bitcast.20, f32[4,8192]{1,0:T(4,128)} %collective-permute-done.refs_2_, f32[4,8192]{1,0:T(4,128)} %collective-permute-done.1.refs_3_, ...), custom_call_target="tpu_custom_call" | custom-call | flops 20000000000 | bytes 1000000 | tf_op jit(solution)/shard_map/middle_first/pallas_call | solution.py:556
  57.6 0.0 all-to-all-done.1.refs_2_
  57.6 4.5 %finish_first.1 = (f32[64,128]{1,0:T(8,128)}, f32[32,24,128]{2,1,0:T(8,128)}) custom-call(s32[1,32]{1,0:T(1,128)} %refs_0_.3, f32[3,64]{1,0:T(4,128)} %refs_1_.7, f32[8,64,128]{2,1,0:T(8,128)} %all-to-all-done.1.refs_2_, f32[64,128]{1,0:T(8,128)} %get-tuple-element.30.refs_3_, f32[64,128]{1,0:T(8,128)} %get-tuple-element.31.refs_4_, f32[64,128]{1,0:T(8,128)} %bitcast.17, ...), custom_call_target="tpu_custom_call" | custom-call | flops 4000000000 | bytes 1000000 | tf_op jit(solution)/shard_map/finish_first/pallas_call | solution.py:556
  62.1 13.8 %all-to-all-start.2 = ((f32[32,24,128]{2,1,0:T(8,128)}), f32[32,24,128]{2,1,0:T(8,128)}, u32[]{:S(2)}, u32[]{:S(2)}) async-start(f32[32,24,128]{2,1,0:T(8,128)} %get-tuple-element.33), calls=%async_computation.2 | async-start | bytes 786432 | tf_op jit(solution)/shard_map/all_to_all | solution.py:582
  75.9 10.1 %own_next.1 = (f32[64,128]{1,0:T(8,128)}, f32[64,128]{1,0:T(8,128)}) custom-call(s32[272]{0:T(512)} %get-tuple-element.34.refs_0_, f32[3,8192]{1,0:T(4,128)} %refs_1_.6, f32[64,128]{1,0:T(8,128)} %get-tuple-element.32.refs_2_.refs_7_.refs_1_, bf16[32,256,128]{2,1,0:T(8,128)(2,1)} %get-tuple-element.25.refs_4_.refs_3_.refs_6_, ...), custom_call_target="tpu_custom_call" | custom-call | flops 10000000000 | bytes 1000000 | tf_op jit(solution)/shard_map/own_next/pallas_call | solution.py:556
  86.1 4.5 %collective-permute-start.2 = (f32[64,128]{1,0:T(8,128)}, f32[64,128]{1,0:T(8,128)}, u32[]{:S(2)}, u32[]{:S(2)}) collective-permute-start(f32[64,128]{1,0:T(8,128)} %get-tuple-element.35), channel_id=1, source_target_pairs={{0,1},{1,2},{2,3},{3,4},{4,5},{5,6},{6,7},{7,8},{8,9},{9,10},{10,1... | collective-permute-start | bytes 98312 | tf_op jit(solution)/shard_map/ppermute | solution.py:578
  90.6 5.1 %collective-permute-start.3 = (f32[64,128]{1,0:T(8,128)}, f32[64,128]{1,0:T(8,128)}, u32[]{:S(2)}, u32[]{:S(2)}) collective-permute-start(f32[64,128]{1,0:T(8,128)} %get-tuple-element.35), channel_id=1, source_target_pairs={{1,0},{2,1},{3,2},{4,3},{5,4},{6,5},{7,6},{8,7},{9,8},{10,9},{11,1... | collective-permute-start | bytes 98312 | tf_op jit(solution)/shard_map/ppermute | solution.py:578
  95.7 0.0 all-to-all-done.2.refs_11_
  95.7 0.9 slice.9
  96.7 0.7 broadcast_in_dim.17
  97.3 7.8 %all-to-all-start.3 = ((f32[8,32,128]{2,1,0:T(8,128)}), f32[8,32,128]{2,1,0:T(8,128)}, u32[]{:S(2)}, u32[]{:S(2)}) async-start(f32[8,32,128]{2,1,0:T(8,128)} %broadcast_in_dim.17), calls=%async_computation.3 | async-start | bytes 262144 | tf_op jit(solution)/shard_map/all_to_all | solution.py:582
  105.1 0.0 collective-permute-done.2.refs_4_
  105.1 0.0 collective-permute-done.3.refs_5_
  105.1 12.2 %middle_next.1 = (f32[64,128]{1,0:T(8,128)}, f32[64,128]{1,0:T(8,128)}) custom-call(s32[272]{0:T(512)} %get-tuple-element.23.refs_0_, s32[16,32]{1,0:T(8,128)} %bitcast.21, f32[4,8192]{1,0:T(4,128)} %collective-permute-done.refs_2_, f32[4,8192]{1,0:T(4,128)} %collective-permute-done.1.refs_3_, f32[64,128]{1,0:T(8,128)} %collective-permute-done.2.refs_4_, ...), custom_call_target="tpu_custom_call" | custom-call | flops 20000000000 | bytes 1000000 | tf_op jit(solution)/shard_map/middle_next/pallas_call | solution.py:556
  117.3 0.0 all-to-all-done.3.refs_3_
  117.4 4.1 %finish_next.1 = (f32[64,128]{1,0:T(8,128)}, f32[256,1,128]{2,1,0:T(1,128)}) custom-call(s32[1,32]{1,0:T(1,128)} %refs_0_.3, f32[3,64]{1,0:T(4,128)} %refs_1_.7, f32[8,64,128]{2,1,0:T(8,128)} %all-to-all-done.1.refs_2_, f32[8,32,128]{2,1,0:T(8,128)} %all-to-all-done.3.refs_3_, f32[64,128]{1,0:T(8,128)} %get-tuple-element.38.refs_4_, ...), custom_call_target="tpu_custom_call" | custom-call | flops 4000000000 | bytes 1000000 | tf_op jit(solution)/shard_map/finish_next/pallas_call | solution.py:556
  121.4 34.7 %all_to_all.25.refs_4_ = f32[256,1,128]{2,1,0:T(1,128)} all-to-all(f32[256,1,128]{2,1,0:T(1,128)} %get-tuple-element.41), channel_id=1, replica_groups=mesh['grp'=8,'dev'=32] {'grp','dev'}, dimensions={0} | all-to-all | bytes 262144 | tf_op jit(solution)/shard_map/all_to_all | solution.py:582
  156.1 2.2 %last.1 = (f32[64,128]{1,0:T(8,128)}, f32[64,128]{1,0:T(8,128)}) custom-call(f32[64,128]{1,0:T(8,128)} %bitcast.19, f32[64,128]{1,0:T(8,128)} %get-tuple-element.32.refs_2_.refs_7_.refs_1_, f32[64,128]{1,0:T(8,128)} %get-tuple-element.40.refs_2_, f32[8,32,128]{2,1,0:T(8,128)} %all-to-all-done.3.refs_3_, f32[256,1,128]{2,1,0:T(1,128)} %all_to_all.25.refs_4_), custom_call_target="tpu_custom_call" | custom-call | flops 1000000000 | bytes 1000000 | tf_op jit(solution)/shard_map/last/pallas_call | solution.py:556
  (1 shorter events, 0.0 us)
Async XLA Ops:
  4.1 31.1 %all-to-all-start = ((f32[32,72,128]{2,1,0:T(8,128)}), f32[32,72,128]{2,1,0:T(8,128)}, u32[]{:S(2)}, u32[]{:S(2)}) async-start(f32[32,72,128]{2,1,0:T(8,128)} %prepare.1), calls=%async_computation | async-start | bytes 2359296 | tf_op jit(solution)/shard_map/all_to_all | solution.py:582
  25.5 18.5 %collective-permute-start = (f32[4,8192]{1,0:T(4,128)}, f32[4,8192]{1,0:T(4,128)}, u32[]{:S(2)}, u32[]{:S(2)}) collective-permute-start(f32[4,8192]{1,0:T(4,128)} %get-tuple-element.24), channel_id=1, source_target_pairs={{0,1},{1,2},{2,3},{3,4},{4,5},{5,6},{6,7},{7,8},{8,9},{9,10},{10,1... | collective-permute-start | bytes 393224 | tf_op jit(solution)/shard_map/ppermute | solution.py:578
  30.0 14.1 %collective-permute-start.1 = (f32[4,8192]{1,0:T(4,128)}, f32[4,8192]{1,0:T(4,128)}, u32[]{:S(2)}, u32[]{:S(2)}) collective-permute-start(f32[4,8192]{1,0:T(4,128)} %get-tuple-element.24), channel_id=1, source_target_pairs={{1,0},{2,1},{3,2},{4,3},{5,4},{6,5},{7,6},{8,7},{9,8},{10,9},{11,1... | collective-permute-start | bytes 393224 | tf_op jit(solution)/shard_map/ppermute | solution.py:578
  36.9 20.8 %all-to-all-start.1 = ((f32[8,64,128]{2,1,0:T(8,128)}), f32[8,64,128]{2,1,0:T(8,128)}, u32[]{:S(2)}, u32[]{:S(2)}) async-start(f32[8,64,128]{2,1,0:T(8,128)} %broadcast_in_dim.15), calls=%async_computation.1 | async-start | bytes 524288 | tf_op jit(solution)/shard_map/all_to_all | solution.py:582
  62.1 33.6 %all-to-all-start.2 = ((f32[32,24,128]{2,1,0:T(8,128)}), f32[32,24,128]{2,1,0:T(8,128)}, u32[]{:S(2)}, u32[]{:S(2)}) async-start(f32[32,24,128]{2,1,0:T(8,128)} %get-tuple-element.33), calls=%async_computation.2 | async-start | bytes 786432 | tf_op jit(solution)/shard_map/all_to_all | solution.py:582
  86.1 19.1 %collective-permute-start.2 = (f32[64,128]{1,0:T(8,128)}, f32[64,128]{1,0:T(8,128)}, u32[]{:S(2)}, u32[]{:S(2)}) collective-permute-start(f32[64,128]{1,0:T(8,128)} %get-tuple-element.35), channel_id=1, source_target_pairs={{0,1},{1,2},{2,3},{3,4},{4,5},{5,6},{6,7},{7,8},{8,9},{9,10},{10,1... | collective-permute-start | bytes 98312 | tf_op jit(solution)/shard_map/ppermute | solution.py:578
  90.6 14.5 %collective-permute-start.3 = (f32[64,128]{1,0:T(8,128)}, f32[64,128]{1,0:T(8,128)}, u32[]{:S(2)}, u32[]{:S(2)}) collective-permute-start(f32[64,128]{1,0:T(8,128)} %get-tuple-element.35), channel_id=1, source_target_pairs={{1,0},{2,1},{3,2},{4,3},{5,4},{6,5},{7,6},{8,7},{9,8},{10,9},{11,1... | collective-permute-start | bytes 98312 | tf_op jit(solution)/shard_map/ppermute | solution.py:578
  97.3 20.0 %all-to-all-start.3 = ((f32[8,32,128]{2,1,0:T(8,128)}), f32[8,32,128]{2,1,0:T(8,128)}, u32[]{:S(2)}, u32[]{:S(2)}) async-start(f32[8,32,128]{2,1,0:T(8,128)} %broadcast_in_dim.17), calls=%async_computation.3 | async-start | bytes 262144 | tf_op jit(solution)/shard_map/all_to_all | solution.py:582

commit v6 on v5

--- a/solution.py
+++ b/solution.py
@@ -205,7 +205,7 @@
         out_ref[pl.ds(2 * l, 2), :] = value
         return carry
 
-    lax.fori_loop(0, LEAVES, leaf, 0, unroll=4)
+    lax.fori_loop(0, LEAVES, leaf, 0, unroll=16)
 
 
 def fill(source_ref, at, block_ref):

time: 161 us -> 157 us (0.975); the launches traced: 158 us -> 157 us
  Pallas kernels: 62.8 us -> 83.2 us
  starting transfers between devices: 56.8 us -> 42.3 us
  blocking collectives: 34.7 us -> 27.6 us
    pallas_call x8, Pallas kernels: 62.8 us -> 83.2 us  [call(): pl.pallas_call(body, grid=(1,), out_shape=[jax.ShapeDtypeStruct(shape, dt...]
    ppermute x4, starting transfers between devices: 19.3 us -> 11 us  [neighbours(): return (lax.ppermute(block, AXES, up), lax.ppermute(block, AXES, down))]
    all_to_all x1, blocking collectives: 34.7 us -> 27.6 us  [exchange(): return lax.all_to_all(copies, axes, 0, 0, tiled=True)]
    all_to_all x4, starting transfers between devices: 37.5 us -> 31.3 us  [exchange(): return lax.all_to_all(copies, axes, 0, 0, tiled=True)]
  transfers between devices with their start and end apart: 8 -> 8, of which waited for: 0 -> 0; matrix products, arithmetic and copies ran while one was open for 2% -> 2% of each run, Pallas kernels for 31% -> 44%
where the time goes in v6:
time: 157 us
  Pallas kernels  83.2 us (53%)
  starting transfers between devices  42.3 us (27%)
  blocking collectives  27.6 us (18%)
  local copies, waits for them, and re-layouts  3.2 us (2%)
    pallas_call x8, Pallas kernels, call(): pl.pallas_call(body, grid=(1,), out_shape=[jax.ShapeDtypeStruct(shape, dt...  83.2 us
    all_to_all x4, starting transfers between devices, exchange(): return lax.all_to_all(copies, axes, 0, 0, tiled=True)  31.3 us
    all_to_all x1, blocking collectives, exchange(): return lax.all_to_all(copies, axes, 0, 0, tiled=True)  27.6 us
    ppermute x4, starting transfers between devices, neighbours(): return (lax.ppermute(block, AXES, up), lax.ppermute(block, AXES, down))  11 us
  transfers between devices with their start and end apart: 8, of which 0 were waited for; matrix products, arithmetic and copies ran while one was open for 2% of the time, Pallas kernels for 44%

profile of v6, /device:TPU:1, one launch (start us, length us, event | category | flops | bytes accessed | tf_op | source)
XLA Modules:
  0.0 157.3 jit_solution(12509930890268018600)
XLA Ops:
  0.6 3.5 %prepare.1 = f32[32,72,128]{2,1,0:T(8,128)} custom-call(f32[64,128]{1,0:T(8,128)} %bitcast.15, f32[32,64,256]{2,1,0:T(8,128)} %bitcast.12, f32[32,64,64]{2,1,0:T(8,128)} %refs_9_.1, f32[3,2048]{1,0:T(4,128)} %refs_4_.3, f32[3,64]{1,0:T(4,128)} %refs_1_.7), custom_call_target="tpu_custom_call" | custom-call | flops 4000000000 | bytes 1000000 | tf_op jit(solution)/shard_map/prepare/pallas_call | solution.py:556
  4.1 8.6 %all-to-all-start = ((f32[32,72,128]{2,1,0:T(8,128)}), f32[32,72,128]{2,1,0:T(8,128)}, u32[]{:S(2)}, u32[]{:S(2)}) async-start(f32[32,72,128]{2,1,0:T(8,128)} %prepare.1), calls=%async_computation | async-start | bytes 2359296 | tf_op jit(solution)/shard_map/all_to_all | solution.py:582
  12.7 16.4 %own_first.1 = (bf16[32,256,128]{2,1,0:T(8,128)(2,1)}, f32[32,8,128]{2,1,0:T(8,128)}, bf16[32,64,128]{2,1,0:T(8,128)(2,1)}, f32[32,8,128]{2,1,0:T(8,128)}, s32[2...) custom-call(s32[8,32]{1,0:T(8,128)} %bitcast.22, s32[32]{0:T(128)} %refs_1_.4, f32[3,8192]{1,0:T(4,128)} %refs_1_.6, ...), custom_call_target="tpu_custom_call" | custom-call | flops 15000000512 | bytes 1000000 | tf_op jit(solution)/shard_map/own_first/pallas_call | solution.py:556
  29.2 1.9 %collective-permute-start = (f32[4,8192]{1,0:T(4,128)}, f32[4,8192]{1,0:T(4,128)}, u32[]{:S(2)}, u32[]{:S(2)}) collective-permute-start(f32[4,8192]{1,0:T(4,128)} %get-tuple-element.24), channel_id=1, source_target_pairs={{0,1},{1,2},{2,3},{3,4},{4,5},{5,6},{6,7},{7,8},{8,9},{9,10},{10,1... | collective-permute-start | bytes 393224 | tf_op jit(solution)/shard_map/ppermute | solution.py:578
  31.1 3.6 %collective-permute-start.1 = (f32[4,8192]{1,0:T(4,128)}, f32[4,8192]{1,0:T(4,128)}, u32[]{:S(2)}, u32[]{:S(2)}) collective-permute-start(f32[4,8192]{1,0:T(4,128)} %get-tuple-element.24), channel_id=1, source_target_pairs={{1,0},{2,1},{3,2},{4,3},{5,4},{6,5},{7,6},{8,7},{9,8},{10,9},{11,1... | collective-permute-start | bytes 393224 | tf_op jit(solution)/shard_map/ppermute | solution.py:578
  34.7 0.0 all-to-all-done.refs_9_
  34.8 0.9 slice_bitcast_fusion
  35.7 0.7 broadcast_in_dim.15
  36.4 6.3 %all-to-all-start.1 = ((f32[8,64,128]{2,1,0:T(8,128)}), f32[8,64,128]{2,1,0:T(8,128)}, u32[]{:S(2)}, u32[]{:S(2)}) async-start(f32[8,64,128]{2,1,0:T(8,128)} %broadcast_in_dim.15), calls=%async_computation.1 | async-start | bytes 524288 | tf_op jit(solution)/shard_map/all_to_all | solution.py:582
  42.7 0.0 collective-permute-done.refs_2_
  42.7 0.0 collective-permute-done.1.refs_3_
  42.7 20.0 %middle_first.1 = (f32[64,128]{1,0:T(8,128)}, f32[64,128]{1,0:T(8,128)}, bf16[32,48,1024]{2,1,0:T(8,128)(2,1)}) custom-call(s32[272]{0:T(512)} %get-tuple-element.23.refs_0_, s32[16,32]{1,0:T(8,128)} %bitcast.20, f32[4,8192]{1,0:T(4,128)} %collective-permute-done.refs_2_, f32[4,8192]{1,0:T(4,128)} %collective-permute-done.1.refs_3_, ...), custom_call_target="tpu_custom_call" | custom-call | flops 20000000000 | bytes 1000000 | tf_op jit(solution)/shard_map/middle_first/pallas_call | solution.py:556
  62.7 0.0 all-to-all-done.1.refs_2_
  62.7 4.5 %finish_first.1 = (f32[64,128]{1,0:T(8,128)}, f32[32,24,128]{2,1,0:T(8,128)}) custom-call(s32[1,32]{1,0:T(1,128)} %refs_0_.3, f32[3,64]{1,0:T(4,128)} %refs_1_.7, f32[8,64,128]{2,1,0:T(8,128)} %all-to-all-done.1.refs_2_, f32[64,128]{1,0:T(8,128)} %get-tuple-element.30.refs_3_, f32[64,128]{1,0:T(8,128)} %get-tuple-element.31.refs_4_, f32[64,128]{1,0:T(8,128)} %bitcast.17, ...), custom_call_target="tpu_custom_call" | custom-call | flops 4000000000 | bytes 1000000 | tf_op jit(solution)/shard_map/finish_first/pallas_call | solution.py:556
  67.2 7.7 %all-to-all-start.2 = ((f32[32,24,128]{2,1,0:T(8,128)}), f32[32,24,128]{2,1,0:T(8,128)}, u32[]{:S(2)}, u32[]{:S(2)}) async-start(f32[32,24,128]{2,1,0:T(8,128)} %get-tuple-element.33), calls=%async_computation.2 | async-start | bytes 786432 | tf_op jit(solution)/shard_map/all_to_all | solution.py:582
  74.9 13.8 %own_next.1 = (f32[64,128]{1,0:T(8,128)}, f32[64,128]{1,0:T(8,128)}) custom-call(s32[272]{0:T(512)} %get-tuple-element.34.refs_0_, f32[3,8192]{1,0:T(4,128)} %refs_1_.6, f32[64,128]{1,0:T(8,128)} %get-tuple-element.32.refs_2_.refs_7_.refs_1_, bf16[32,256,128]{2,1,0:T(8,128)(2,1)} %get-tuple-element.25.refs_4_.refs_3_.refs_6_, ...), custom_call_target="tpu_custom_call" | custom-call | flops 10000000000 | bytes 1000000 | tf_op jit(solution)/shard_map/own_next/pallas_call | solution.py:556
  88.7 1.9 %collective-permute-start.2 = (f32[64,128]{1,0:T(8,128)}, f32[64,128]{1,0:T(8,128)}, u32[]{:S(2)}, u32[]{:S(2)}) collective-permute-start(f32[64,128]{1,0:T(8,128)} %get-tuple-element.35), channel_id=1, source_target_pairs={{0,1},{1,2},{2,3},{3,4},{4,5},{5,6},{6,7},{7,8},{8,9},{9,10},{10,1... | collective-permute-start | bytes 98312 | tf_op jit(solution)/shard_map/ppermute | solution.py:578
  90.7 3.6 %collective-permute-start.3 = (f32[64,128]{1,0:T(8,128)}, f32[64,128]{1,0:T(8,128)}, u32[]{:S(2)}, u32[]{:S(2)}) collective-permute-start(f32[64,128]{1,0:T(8,128)} %get-tuple-element.35), channel_id=1, source_target_pairs={{1,0},{2,1},{3,2},{4,3},{5,4},{6,5},{7,6},{8,7},{9,8},{10,9},{11,1... | collective-permute-start | bytes 98312 | tf_op jit(solution)/shard_map/ppermute | solution.py:578
  94.2 0.0 all-to-all-done.2.refs_11_
  94.2 0.9 slice.9
  95.2 0.7 broadcast_in_dim.17
  95.8 8.6 %all-to-all-start.3 = ((f32[8,32,128]{2,1,0:T(8,128)}), f32[8,32,128]{2,1,0:T(8,128)}, u32[]{:S(2)}, u32[]{:S(2)}) async-start(f32[8,32,128]{2,1,0:T(8,128)} %broadcast_in_dim.17), calls=%async_computation.3 | async-start | bytes 262144 | tf_op jit(solution)/shard_map/all_to_all | solution.py:582
  104.4 0.0 collective-permute-done.2.refs_4_
  104.4 0.0 collective-permute-done.3.refs_5_
  104.4 18.8 %middle_next.1 = (f32[64,128]{1,0:T(8,128)}, f32[64,128]{1,0:T(8,128)}) custom-call(s32[272]{0:T(512)} %get-tuple-element.23.refs_0_, s32[16,32]{1,0:T(8,128)} %bitcast.21, f32[4,8192]{1,0:T(4,128)} %collective-permute-done.refs_2_, f32[4,8192]{1,0:T(4,128)} %collective-permute-done.1.refs_3_, f32[64,128]{1,0:T(8,128)} %collective-permute-done.2.refs_4_, ...), custom_call_target="tpu_custom_call" | custom-call | flops 20000000000 | bytes 1000000 | tf_op jit(solution)/shard_map/middle_next/pallas_call | solution.py:556
  123.2 0.0 all-to-all-done.3.refs_3_
  123.3 4.1 %finish_next.1 = (f32[64,128]{1,0:T(8,128)}, f32[256,1,128]{2,1,0:T(1,128)}) custom-call(s32[1,32]{1,0:T(1,128)} %refs_0_.3, f32[3,64]{1,0:T(4,128)} %refs_1_.7, f32[8,64,128]{2,1,0:T(8,128)} %all-to-all-done.1.refs_2_, f32[8,32,128]{2,1,0:T(8,128)} %all-to-all-done.3.refs_3_, f32[64,128]{1,0:T(8,128)} %get-tuple-element.38.refs_4_, ...), custom_call_target="tpu_custom_call" | custom-call | flops 4000000000 | bytes 1000000 | tf_op jit(solution)/shard_map/finish_next/pallas_call | solution.py:556
  127.3 27.6 %all_to_all.25.refs_4_ = f32[256,1,128]{2,1,0:T(1,128)} all-to-all(f32[256,1,128]{2,1,0:T(1,128)} %get-tuple-element.41), channel_id=1, replica_groups=mesh['grp'=8,'dev'=32] {'grp','dev'}, dimensions={0} | all-to-all | bytes 262144 | tf_op jit(solution)/shard_map/all_to_all | solution.py:582
  155.0 2.2 %last.1 = (f32[64,128]{1,0:T(8,128)}, f32[64,128]{1,0:T(8,128)}) custom-call(f32[64,128]{1,0:T(8,128)} %bitcast.19, f32[64,128]{1,0:T(8,128)} %get-tuple-element.32.refs_2_.refs_7_.refs_1_, f32[64,128]{1,0:T(8,128)} %get-tuple-element.40.refs_2_, f32[8,32,128]{2,1,0:T(8,128)} %all-to-all-done.3.refs_3_, f32[256,1,128]{2,1,0:T(1,128)} %all_to_all.25.refs_4_), custom_call_target="tpu_custom_call" | custom-call | flops 1000000000 | bytes 1000000 | tf_op jit(solution)/shard_map/last/pallas_call | solution.py:556
  (1 shorter events, 0.0 us)
Async XLA Ops:
  4.1 30.7 %all-to-all-start = ((f32[32,72,128]{2,1,0:T(8,128)}), f32[32,72,128]{2,1,0:T(8,128)}, u32[]{:S(2)}, u32[]{:S(2)}) async-start(f32[32,72,128]{2,1,0:T(8,128)} %prepare.1), calls=%async_computation | async-start | bytes 2359296 | tf_op jit(solution)/shard_map/all_to_all | solution.py:582
  29.2 13.5 %collective-permute-start = (f32[4,8192]{1,0:T(4,128)}, f32[4,8192]{1,0:T(4,128)}, u32[]{:S(2)}, u32[]{:S(2)}) collective-permute-start(f32[4,8192]{1,0:T(4,128)} %get-tuple-element.24), channel_id=1, source_target_pairs={{0,1},{1,2},{2,3},{3,4},{4,5},{5,6},{6,7},{7,8},{8,9},{9,10},{10,1... | collective-permute-start | bytes 393224 | tf_op jit(solution)/shard_map/ppermute | solution.py:578
  31.1 11.6 %collective-permute-start.1 = (f32[4,8192]{1,0:T(4,128)}, f32[4,8192]{1,0:T(4,128)}, u32[]{:S(2)}, u32[]{:S(2)}) collective-permute-start(f32[4,8192]{1,0:T(4,128)} %get-tuple-element.24), channel_id=1, source_target_pairs={{1,0},{2,1},{3,2},{4,3},{5,4},{6,5},{7,6},{8,7},{9,8},{10,9},{11,1... | collective-permute-start | bytes 393224 | tf_op jit(solution)/shard_map/ppermute | solution.py:578
  36.4 26.3 %all-to-all-start.1 = ((f32[8,64,128]{2,1,0:T(8,128)}), f32[8,64,128]{2,1,0:T(8,128)}, u32[]{:S(2)}, u32[]{:S(2)}) async-start(f32[8,64,128]{2,1,0:T(8,128)} %broadcast_in_dim.15), calls=%async_computation.1 | async-start | bytes 524288 | tf_op jit(solution)/shard_map/all_to_all | solution.py:582
  67.2 27.0 %all-to-all-start.2 = ((f32[32,24,128]{2,1,0:T(8,128)}), f32[32,24,128]{2,1,0:T(8,128)}, u32[]{:S(2)}, u32[]{:S(2)}) async-start(f32[32,24,128]{2,1,0:T(8,128)} %get-tuple-element.33), calls=%async_computation.2 | async-start | bytes 786432 | tf_op jit(solution)/shard_map/all_to_all | solution.py:582
  88.7 15.7 %collective-permute-start.2 = (f32[64,128]{1,0:T(8,128)}, f32[64,128]{1,0:T(8,128)}, u32[]{:S(2)}, u32[]{:S(2)}) collective-permute-start(f32[64,128]{1,0:T(8,128)} %get-tuple-element.35), channel_id=1, source_target_pairs={{0,1},{1,2},{2,3},{3,4},{4,5},{5,6},{6,7},{7,8},{8,9},{9,10},{10,1... | collective-permute-start | bytes 98312 | tf_op jit(solution)/shard_map/ppermute | solution.py:578
  90.7 13.8 %collective-permute-start.3 = (f32[64,128]{1,0:T(8,128)}, f32[64,128]{1,0:T(8,128)}, u32[]{:S(2)}, u32[]{:S(2)}) collective-permute-start(f32[64,128]{1,0:T(8,128)} %get-tuple-element.35), channel_id=1, source_target_pairs={{1,0},{2,1},{3,2},{4,3},{5,4},{6,5},{7,6},{8,7},{9,8},{10,9},{11,1... | collective-permute-start | bytes 98312 | tf_op jit(solution)/shard_map/ppermute | solution.py:578
  95.8 27.4 %all-to-all-start.3 = ((f32[8,32,128]{2,1,0:T(8,128)}), f32[8,32,128]{2,1,0:T(8,128)}, u32[]{:S(2)}, u32[]{:S(2)}) async-start(f32[8,32,128]{2,1,0:T(8,128)} %broadcast_in_dim.17), calls=%async_computation.3 | async-start | bytes 262144 | tf_op jit(solution)/shard_map/all_to_all | solution.py:582

commit v7 on v6

--- a/solution.py
+++ b/solution.py
@@ -81,6 +81,10 @@
     return jnp.where(rows_of(shape) < 3, (tile - centre) * SCALE, 0.0)
 
 
+def less(tile, centre):
+    return jnp.where(rows_of(tile.shape) < 3, tile - centre, 0.0)
+
+
 def eight(tile):
     return jnp.concatenate([tile, jnp.zeros((8 - tile.shape[0], tile.shape[1]), F32)], axis=0)
 
@@ -143,11 +147,11 @@
 def near_parts(target_ref, centre_ref, source_ref, acc_ref, dist_ref):
     def distances(l, at, slot):
         centre = centre_ref[l]
-        coords = centred(source_ref[at], jnp.concatenate([centre, centre], axis=1))
+        coords = less(source_ref[at], jnp.concatenate([centre, centre], axis=1))
         dist_ref[slot] = squares(target_ref[l], source_stack(coords))
 
     def products(l, at, slot, first):
-        weights = source_ref[at, 3:4, :] * FACTOR
+        weights = source_ref[at, 3:4, :]
         for row in range(0, PTS, 64):
             value = weighted(dist_ref[slot, row : row + 64, :], weights)
             if first:
@@ -210,14 +214,15 @@
 
 def fill(source_ref, at, block_ref):
     for l in range(LEAVES):
-        source_ref[at + l] = eight(block_ref[:, l * PTS : (l + 1) * PTS])
+        tile = eight(block_ref[:, l * PTS : (l + 1) * PTS])
+        source_ref[at + l] = tile * jnp.where(rows_of(tile.shape) < 3, SCALE, FACTOR)
     source_ref[DUMMY] = jnp.zeros((8, PTS), F32)
 
 
 def set_values(source_ref, at, block_ref):
     for l in range(LEAVES):
         pair = block_ref[2 * l : 2 * l + 2, :]
-        source_ref[at + l, 3:4, :] = jnp.concatenate([pair[:1], pair[1:]], axis=1)
+        source_ref[at + l, 3:4, :] = jnp.concatenate([pair[:1], pair[1:]], axis=1) * FACTOR
 
 
 def skel_target(tile):
@@ -243,7 +248,7 @@
         tile = source_ref[LEAVES + l]
         centre = jnp.broadcast_to(jnp.sum(tile, axis=1, keepdims=True) * (1.0 / PTS), (8, 128))
         centre_ref[l] = centre
-        target_ref[l] = target_stack(centred(tile, jnp.concatenate([centre, centre], axis=1)))
+        target_ref[l] = target_stack(less(tile, jnp.concatenate([centre, centre], axis=1)))
         return carry
 
     lax.fori_loop(0, LEAVES, targets, 0, unroll=4)

time: 157 us -> 157 us (level)
  Pallas kernels: 83.2 us -> 74.6 us
  starting transfers between devices: 42.3 us -> 47.7 us
  blocking collectives: 27.6 us -> 31.8 us
    pallas_call x8, Pallas kernels: 83.2 us -> 74.6 us  [call(): pl.pallas_call(body, grid=(1,), out_shape=[jax.ShapeDtypeStruct(shape, dt...]
    ppermute x4, starting transfers between devices: 11 us -> 18.1 us  [neighbours(): return (lax.ppermute(block, AXES, up), lax.ppermute(block, AXES, down))]
    all_to_all x1, blocking collectives: 27.6 us -> 31.8 us  [exchange(): return lax.all_to_all(copies, axes, 0, 0, tiled=True)]
    all_to_all x4, starting transfers between devices: 31.3 us -> 29.5 us  [exchange(): return lax.all_to_all(copies, axes, 0, 0, tiled=True)]
  transfers between devices with their start and end apart: 8 -> 8, of which waited for: 0 -> 0; matrix products, arithmetic and copies ran while one was open for 2% -> 2% of each run, Pallas kernels for 44% -> 38%
where the time goes in v7:
time: 157 us; the launch traced here: 158 us
  Pallas kernels  74.6 us (48%)
  starting transfers between devices  47.7 us (30%)
  blocking collectives  31.8 us (20%)
  local copies, waits for them, and re-layouts  3.2 us (2%)
    pallas_call x8, Pallas kernels, call(): pl.pallas_call(body, grid=(1,), out_shape=[jax.ShapeDtypeStruct(shape, dt...  74.6 us
    all_to_all x1, blocking collectives, exchange(): return lax.all_to_all(copies, axes, 0, 0, tiled=True)  31.8 us
    all_to_all x4, starting transfers between devices, exchange(): return lax.all_to_all(copies, axes, 0, 0, tiled=True)  29.5 us
    ppermute x4, starting transfers between devices, neighbours(): return (lax.ppermute(block, AXES, up), lax.ppermute(block, AXES, down))  18.1 us
  transfers between devices with their start and end apart: 8, of which 0 were waited for; matrix products, arithmetic and copies ran while one was open for 2% of the time, Pallas kernels for 38%

profile of v7, /device:TPU:1, one launch (start us, length us, event | category | flops | bytes accessed | tf_op | source)
XLA Modules:
  0.0 158.3 jit_solution(15052077926135638928)
XLA Ops:
  0.6 3.5 %prepare.1 = f32[32,72,128]{2,1,0:T(8,128)} custom-call(f32[64,128]{1,0:T(8,128)} %bitcast.15, f32[32,64,256]{2,1,0:T(8,128)} %bitcast.12, f32[32,64,64]{2,1,0:T(8,128)} %refs_9_.1, f32[3,2048]{1,0:T(4,128)} %refs_4_.3, f32[3,64]{1,0:T(4,128)} %refs_1_.7), custom_call_target="tpu_custom_call" | custom-call | flops 4000000000 | bytes 1000000 | tf_op jit(solution)/shard_map/prepare/pallas_call | solution.py:561
  4.1 8.6 %all-to-all-start = ((f32[32,72,128]{2,1,0:T(8,128)}), f32[32,72,128]{2,1,0:T(8,128)}, u32[]{:S(2)}, u32[]{:S(2)}) async-start(f32[32,72,128]{2,1,0:T(8,128)} %prepare.1), calls=%async_computation | async-start | bytes 2359296 | tf_op jit(solution)/shard_map/all_to_all | solution.py:587
  12.7 14.5 %own_first.1 = (bf16[32,256,128]{2,1,0:T(8,128)(2,1)}, f32[32,8,128]{2,1,0:T(8,128)}, bf16[32,64,128]{2,1,0:T(8,128)(2,1)}, f32[32,8,128]{2,1,0:T(8,128)}, s32[2...) custom-call(s32[8,32]{1,0:T(8,128)} %bitcast.22, s32[32]{0:T(128)} %refs_1_.4, f32[3,8192]{1,0:T(4,128)} %refs_1_.6, ...), custom_call_target="tpu_custom_call" | custom-call | flops 15000000512 | bytes 1000000 | tf_op jit(solution)/shard_map/own_first/pallas_call | solution.py:561
  27.2 2.6 %collective-permute-start = (f32[4,8192]{1,0:T(4,128)}, f32[4,8192]{1,0:T(4,128)}, u32[]{:S(2)}, u32[]{:S(2)}) collective-permute-start(f32[4,8192]{1,0:T(4,128)} %get-tuple-element.24), channel_id=1, source_target_pairs={{0,1},{1,2},{2,3},{3,4},{4,5},{5,6},{6,7},{7,8},{8,9},{9,10},{10,1... | collective-permute-start | bytes 393224 | tf_op jit(solution)/shard_map/ppermute | solution.py:583
  29.9 6.4 %collective-permute-start.1 = (f32[4,8192]{1,0:T(4,128)}, f32[4,8192]{1,0:T(4,128)}, u32[]{:S(2)}, u32[]{:S(2)}) collective-permute-start(f32[4,8192]{1,0:T(4,128)} %get-tuple-element.24), channel_id=1, source_target_pairs={{1,0},{2,1},{3,2},{4,3},{5,4},{6,5},{7,6},{8,7},{9,8},{10,9},{11,1... | collective-permute-start | bytes 393224 | tf_op jit(solution)/shard_map/ppermute | solution.py:583
  36.3 0.0 all-to-all-done.refs_9_
  36.3 0.9 slice_bitcast_fusion
  37.3 0.7 broadcast_in_dim.15
  38.0 5.5 %all-to-all-start.1 = ((f32[8,64,128]{2,1,0:T(8,128)}), f32[8,64,128]{2,1,0:T(8,128)}, u32[]{:S(2)}, u32[]{:S(2)}) async-start(f32[8,64,128]{2,1,0:T(8,128)} %broadcast_in_dim.15), calls=%async_computation.1 | async-start | bytes 524288 | tf_op jit(solution)/shard_map/all_to_all | solution.py:587
  43.4 0.0 collective-permute-done.refs_2_
  43.5 0.0 collective-permute-done.1.refs_3_
  43.5 17.5 %middle_first.1 = (f32[64,128]{1,0:T(8,128)}, f32[64,128]{1,0:T(8,128)}, bf16[32,48,1024]{2,1,0:T(8,128)(2,1)}) custom-call(s32[272]{0:T(512)} %get-tuple-element.23.refs_0_, s32[16,32]{1,0:T(8,128)} %bitcast.20, f32[4,8192]{1,0:T(4,128)} %collective-permute-done.refs_2_, f32[4,8192]{1,0:T(4,128)} %collective-permute-done.1.refs_3_, ...), custom_call_target="tpu_custom_call" | custom-call | flops 20000000000 | bytes 1000000 | tf_op jit(solution)/shard_map/middle_first/pallas_call | solution.py:561
  61.0 0.0 all-to-all-done.1.refs_2_
  61.0 4.5 %finish_first.1 = (f32[64,128]{1,0:T(8,128)}, f32[32,24,128]{2,1,0:T(8,128)}) custom-call(s32[1,32]{1,0:T(1,128)} %refs_0_.3, f32[3,64]{1,0:T(4,128)} %refs_1_.7, f32[8,64,128]{2,1,0:T(8,128)} %all-to-all-done.1.refs_2_, f32[64,128]{1,0:T(8,128)} %get-tuple-element.30.refs_3_, f32[64,128]{1,0:T(8,128)} %get-tuple-element.31.refs_4_, f32[64,128]{1,0:T(8,128)} %bitcast.17, ...), custom_call_target="tpu_custom_call" | custom-call | flops 4000000000 | bytes 1000000 | tf_op jit(solution)/shard_map/finish_first/pallas_call | solution.py:561
  65.5 9.3 %all-to-all-start.2 = ((f32[32,24,128]{2,1,0:T(8,128)}), f32[32,24,128]{2,1,0:T(8,128)}, u32[]{:S(2)}, u32[]{:S(2)}) async-start(f32[32,24,128]{2,1,0:T(8,128)} %get-tuple-element.33), calls=%async_computation.2 | async-start | bytes 786432 | tf_op jit(solution)/shard_map/all_to_all | solution.py:587
  74.8 11.8 %own_next.1 = (f32[64,128]{1,0:T(8,128)}, f32[64,128]{1,0:T(8,128)}) custom-call(s32[272]{0:T(512)} %get-tuple-element.34.refs_0_, f32[3,8192]{1,0:T(4,128)} %refs_1_.6, f32[64,128]{1,0:T(8,128)} %get-tuple-element.32.refs_2_.refs_7_.refs_1_, bf16[32,256,128]{2,1,0:T(8,128)(2,1)} %get-tuple-element.25.refs_4_.refs_3_.refs_6_, ...), custom_call_target="tpu_custom_call" | custom-call | flops 10000000000 | bytes 1000000 | tf_op jit(solution)/shard_map/own_next/pallas_call | solution.py:561
  86.6 2.6 %collective-permute-start.2 = (f32[64,128]{1,0:T(8,128)}, f32[64,128]{1,0:T(8,128)}, u32[]{:S(2)}, u32[]{:S(2)}) collective-permute-start(f32[64,128]{1,0:T(8,128)} %get-tuple-element.35), channel_id=1, source_target_pairs={{0,1},{1,2},{2,3},{3,4},{4,5},{5,6},{6,7},{7,8},{8,9},{9,10},{10,1... | collective-permute-start | bytes 98312 | tf_op jit(solution)/shard_map/ppermute | solution.py:583
  89.3 6.4 %collective-permute-start.3 = (f32[64,128]{1,0:T(8,128)}, f32[64,128]{1,0:T(8,128)}, u32[]{:S(2)}, u32[]{:S(2)}) collective-permute-start(f32[64,128]{1,0:T(8,128)} %get-tuple-element.35), channel_id=1, source_target_pairs={{1,0},{2,1},{3,2},{4,3},{5,4},{6,5},{7,6},{8,7},{9,8},{10,9},{11,1... | collective-permute-start | bytes 98312 | tf_op jit(solution)/shard_map/ppermute | solution.py:583
  95.7 0.0 all-to-all-done.2.refs_11_
  95.7 0.9 slice.9
  96.6 0.7 broadcast_in_dim.17
  97.3 6.1 %all-to-all-start.3 = ((f32[8,32,128]{2,1,0:T(8,128)}), f32[8,32,128]{2,1,0:T(8,128)}, u32[]{:S(2)}, u32[]{:S(2)}) async-start(f32[8,32,128]{2,1,0:T(8,128)} %broadcast_in_dim.17), calls=%async_computation.3 | async-start | bytes 262144 | tf_op jit(solution)/shard_map/all_to_all | solution.py:587
  103.4 0.0 collective-permute-done.2.refs_4_
  103.4 0.0 collective-permute-done.3.refs_5_
  103.4 16.6 %middle_next.1 = (f32[64,128]{1,0:T(8,128)}, f32[64,128]{1,0:T(8,128)}) custom-call(s32[272]{0:T(512)} %get-tuple-element.23.refs_0_, s32[16,32]{1,0:T(8,128)} %bitcast.21, f32[4,8192]{1,0:T(4,128)} %collective-permute-done.refs_2_, f32[4,8192]{1,0:T(4,128)} %collective-permute-done.1.refs_3_, f32[64,128]{1,0:T(8,128)} %collective-permute-done.2.refs_4_, ...), custom_call_target="tpu_custom_call" | custom-call | flops 20000000000 | bytes 1000000 | tf_op jit(solution)/shard_map/middle_next/pallas_call | solution.py:561
  120.0 0.0 all-to-all-done.3.refs_3_
  120.0 4.1 %finish_next.1 = (f32[64,128]{1,0:T(8,128)}, f32[256,1,128]{2,1,0:T(1,128)}) custom-call(s32[1,32]{1,0:T(1,128)} %refs_0_.3, f32[3,64]{1,0:T(4,128)} %refs_1_.7, f32[8,64,128]{2,1,0:T(8,128)} %all-to-all-done.1.refs_2_, f32[8,32,128]{2,1,0:T(8,128)} %all-to-all-done.3.refs_3_, f32[64,128]{1,0:T(8,128)} %get-tuple-element.38.refs_4_, ...), custom_call_target="tpu_custom_call" | custom-call | flops 4000000000 | bytes 1000000 | tf_op jit(solution)/shard_map/finish_next/pallas_call | solution.py:561
  124.1 31.8 %all_to_all.25.refs_4_ = f32[256,1,128]{2,1,0:T(1,128)} all-to-all(f32[256,1,128]{2,1,0:T(1,128)} %get-tuple-element.41), channel_id=1, replica_groups=mesh['grp'=8,'dev'=32] {'grp','dev'}, dimensions={0} | all-to-all | bytes 262144 | tf_op jit(solution)/shard_map/all_to_all | solution.py:587
  155.9 2.2 %last.1 = (f32[64,128]{1,0:T(8,128)}, f32[64,128]{1,0:T(8,128)}) custom-call(f32[64,128]{1,0:T(8,128)} %bitcast.19, f32[64,128]{1,0:T(8,128)} %get-tuple-element.32.refs_2_.refs_7_.refs_1_, f32[64,128]{1,0:T(8,128)} %get-tuple-element.40.refs_2_, f32[8,32,128]{2,1,0:T(8,128)} %all-to-all-done.3.refs_3_, f32[256,1,128]{2,1,0:T(1,128)} %all_to_all.25.refs_4_), custom_call_target="tpu_custom_call" | custom-call | flops 1000000000 | bytes 1000000 | tf_op jit(solution)/shard_map/last/pallas_call | solution.py:561
  (1 shorter events, 0.0 us)
Async XLA Ops:
  4.1 32.2 %all-to-all-start = ((f32[32,72,128]{2,1,0:T(8,128)}), f32[32,72,128]{2,1,0:T(8,128)}, u32[]{:S(2)}, u32[]{:S(2)}) async-start(f32[32,72,128]{2,1,0:T(8,128)} %prepare.1), calls=%async_computation | async-start | bytes 2359296 | tf_op jit(solution)/shard_map/all_to_all | solution.py:587
  27.2 16.2 %collective-permute-start = (f32[4,8192]{1,0:T(4,128)}, f32[4,8192]{1,0:T(4,128)}, u32[]{:S(2)}, u32[]{:S(2)}) collective-permute-start(f32[4,8192]{1,0:T(4,128)} %get-tuple-element.24), channel_id=1, source_target_pairs={{0,1},{1,2},{2,3},{3,4},{4,5},{5,6},{6,7},{7,8},{8,9},{9,10},{10,1... | collective-permute-start | bytes 393224 | tf_op jit(solution)/shard_map/ppermute | solution.py:583
  29.9 13.6 %collective-permute-start.1 = (f32[4,8192]{1,0:T(4,128)}, f32[4,8192]{1,0:T(4,128)}, u32[]{:S(2)}, u32[]{:S(2)}) collective-permute-start(f32[4,8192]{1,0:T(4,128)} %get-tuple-element.24), channel_id=1, source_target_pairs={{1,0},{2,1},{3,2},{4,3},{5,4},{6,5},{7,6},{8,7},{9,8},{10,9},{11,1... | collective-permute-start | bytes 393224 | tf_op jit(solution)/shard_map/ppermute | solution.py:583
  38.0 23.0 %all-to-all-start.1 = ((f32[8,64,128]{2,1,0:T(8,128)}), f32[8,64,128]{2,1,0:T(8,128)}, u32[]{:S(2)}, u32[]{:S(2)}) async-start(f32[8,64,128]{2,1,0:T(8,128)} %broadcast_in_dim.15), calls=%async_computation.1 | async-start | bytes 524288 | tf_op jit(solution)/shard_map/all_to_all | solution.py:587
  65.5 30.2 %all-to-all-start.2 = ((f32[32,24,128]{2,1,0:T(8,128)}), f32[32,24,128]{2,1,0:T(8,128)}, u32[]{:S(2)}, u32[]{:S(2)}) async-start(f32[32,24,128]{2,1,0:T(8,128)} %get-tuple-element.33), calls=%async_computation.2 | async-start | bytes 786432 | tf_op jit(solution)/shard_map/all_to_all | solution.py:587
  86.6 16.7 %collective-permute-start.2 = (f32[64,128]{1,0:T(8,128)}, f32[64,128]{1,0:T(8,128)}, u32[]{:S(2)}, u32[]{:S(2)}) collective-permute-start(f32[64,128]{1,0:T(8,128)} %get-tuple-element.35), channel_id=1, source_target_pairs={{0,1},{1,2},{2,3},{3,4},{4,5},{5,6},{6,7},{7,8},{8,9},{9,10},{10,1... | collective-permute-start | bytes 98312 | tf_op jit(solution)/shard_map/ppermute | solution.py:583
  89.3 14.1 %collective-permute-start.3 = (f32[64,128]{1,0:T(8,128)}, f32[64,128]{1,0:T(8,128)}, u32[]{:S(2)}, u32[]{:S(2)}) collective-permute-start(f32[64,128]{1,0:T(8,128)} %get-tuple-element.35), channel_id=1, source_target_pairs={{1,0},{2,1},{3,2},{4,3},{5,4},{6,5},{7,6},{8,7},{9,8},{10,9},{11,1... | collective-permute-start | bytes 98312 | tf_op jit(solution)/shard_map/ppermute | solution.py:583
  97.3 22.7 %all-to-all-start.3 = ((f32[8,32,128]{2,1,0:T(8,128)}), f32[8,32,128]{2,1,0:T(8,128)}, u32[]{:S(2)}, u32[]{:S(2)}) async-start(f32[8,32,128]{2,1,0:T(8,128)} %broadcast_in_dim.17), calls=%async_computation.3 | async-start | bytes 262144 | tf_op jit(solution)/shard_map/all_to_all | solution.py:587
